TPU v7x, 1024 devices: a whole 8x8x8 slice. The times are simulated.
1024 devices in a mesh: expert: 64 (over z_hi, x, core), tensor: 8 (over y), dp: 2 (over z_lo).
Axes of the slice: x: 8, y: 8, z: 8 (z_hi: 4, z_lo: 2; z = z_hi * 2 + z_lo), core: 2. Of those that a mesh axis runs over, the one named last changes fastest.
Arguments:
- grad_out: bfloat16 [16384, 3584], P('expert', ('tensor', 'dp')), may hold values from -16 to 16
- routes: int32 [16384, 2], P('expert'), may hold values from 0 to 63, all different within a row; in each aligned block of 256 rows (0 to 255, 256 to 511, ...) at most 12 rows name the same one
- probs: float32 [16384, 2], P('expert'), may hold values from 0.1 to 1
- expert_down: bfloat16 [64, 2432, 3584], P('expert', ('tensor', 'dp')), may hold values from -0.09375 to 0.09375
- expert_saved: bfloat16 [64, 2, 768, 2432], P('expert', None, None, ('tensor', 'dp')), may hold values from -4 to 4
- dense_down: bfloat16 [2432, 3584], P(('tensor', 'dp')), may hold values from -0.09375 to 0.09375
- dense_saved: bfloat16 [2, 16384, 2432], P(None, 'expert', ('tensor', 'dp')), may hold values from -4 to 4
Outputs:
- expert_pre_grad: bfloat16 [64, 2, 768, 2432], P('expert', None, None, ('tensor', 'dp'))
- expert_down_grad: bfloat16 [64, 2432, 3584], P('expert', ('tensor', 'dp'))
- dense_pre_grad: bfloat16 [2, 16384, 2432], P(None, 'expert', ('tensor', 'dp'))
- dense_down_grad: bfloat16 [2432, 3584], P(('tensor', 'dp'), 'expert')
Inputs may be any that keep to these rules, and one draw needn't show every extreme that they name: `routes`: within each aligned block of 256 tokens (one group) no expert is named by more than 12 tokens, and in some block one expert is named by exactly 12; the two experts of a token differ.
All inputs are finite; a program needn't handle non-finite values.
Results may differ from a plain program's by a relative error of at most 0.0057.
Values may be sent and summed in bfloat16 or wider, within the bound.
No kernel may reach another device: no remote copies, remote signals or barrier semaphores. Data moves between devices by JAX's collectives and lax.ppermute only.
A program may use at most 64 MiB of HBM per device.

v0:
```python
import jax
import jax.numpy as jnp
from jax import lax
from jax.sharding import PartitionSpec as P


def slot_numbers(routes_group, expert_count, capacity):
    flat_routes = routes_group.reshape(-1)
    experts_row = jnp.arange(expert_count, dtype=jnp.int32)
    onehot = (flat_routes[:, None] == experts_row[None, :]).astype(jnp.int32)
    before = jnp.cumsum(onehot, axis=0) - onehot
    position = jnp.sum(before * onehot, axis=1)
    return (flat_routes * capacity + position).reshape(routes_group.shape)


def dispatch_table(routes_group, probs_group, expert_count, capacity):
    slots_here = slot_numbers(routes_group, expert_count, capacity)
    targets = jnp.arange(expert_count * capacity, dtype=jnp.int32)
    match = slots_here[None, :, :] == targets[:, None, None]
    return jnp.sum(jnp.where(match, probs_group[None, :, :], jnp.float32(0.0)), axis=2)


def swiglu_parts(saved_pair):
    gate_pre = saved_pair[0].astype(jnp.float32)
    up_pre = saved_pair[1].astype(jnp.float32)
    sigmoid_gate = jax.nn.sigmoid(gate_pre)
    hidden = (gate_pre * sigmoid_gate * up_pre).astype(jnp.bfloat16)
    return (gate_pre, up_pre, sigmoid_gate, hidden)


def pre_cotangents(hidden_cot, gate_pre, up_pre, sigmoid_gate):
    gate_cot = hidden_cot * up_pre * sigmoid_gate * (1.0 + gate_pre * (1.0 - sigmoid_gate))
    up_cot = hidden_cot * gate_pre * sigmoid_gate
    return jnp.stack([gate_cot, up_cot]).astype(jnp.bfloat16)


def absorb(portion, hidden, down_rows):
    hidden_cot = jnp.einsum("rf,hf->rh", portion, down_rows, preferred_element_type=jnp.float32)
    grad_block = jnp.einsum("rh,rf->hf", hidden, portion, preferred_element_type=jnp.float32)
    return (hidden_cot, grad_block)


def expert_fold(received, expert_step, expert_start):
    return expert_step(
        expert_start, lax.all_gather(received, ("tensor", "dp"), axis=1, tiled=True), jnp.int32(0)
    )


def body(grad_out, routes, probs, expert_down, expert_saved, dense_down, dense_saved):
    expert_count = lax.axis_size("expert")
    capacity = expert_saved.shape[2] // expert_count
    feature_width = grad_out.shape[1]
    down_local = expert_down[0]
    model_width = down_local.shape[1]
    table = dispatch_table(routes, probs, expert_count, capacity)
    outgoing = jnp.dot(table, grad_out.astype(jnp.float32), precision=lax.Precision.HIGHEST).astype(
        jnp.bfloat16
    )
    outgoing = outgoing.reshape(expert_count, capacity, feature_width)
    gate_dense, up_dense, sigmoid_dense, dense_hidden = swiglu_parts(dense_saved)
    gate_expert, up_expert, sigmoid_expert, expert_hidden = swiglu_parts(expert_saved[0])
    expert_start = (
        jnp.zeros((expert_count * capacity, down_local.shape[0]), jnp.float32),
        jnp.zeros((down_local.shape[0], model_width), jnp.float32),
    )

    def expert_step(state_pair, portion, offset):
        return absorb(portion, expert_hidden, down_local)

    received = lax.all_to_all(outgoing, "expert", split_axis=0, concat_axis=0, tiled=True)
    received = received.reshape(expert_count * capacity, feature_width)
    dense_cot, dense_grad = absorb(
        lax.all_gather(grad_out, ("tensor", "dp"), axis=1, tiled=True), dense_hidden, dense_down
    )
    expert_cot, expert_grad = expert_fold(received, expert_step, expert_start)
    dense_share = lax.psum_scatter(dense_grad, "expert", scatter_dimension=1, tiled=True)
    expert_pre_grad = pre_cotangents(expert_cot, gate_expert, up_expert, sigmoid_expert)[None]
    expert_down_grad = expert_grad.astype(jnp.bfloat16)[None]
    dense_pre_grad = pre_cotangents(dense_cot, gate_dense, up_dense, sigmoid_dense)
    dense_down_grad = dense_share.astype(jnp.bfloat16)
    return (expert_pre_grad, expert_down_grad, dense_pre_grad, dense_down_grad)


def solution(mesh):
    return jax.shard_map(
        body,
        mesh=mesh,
        in_specs=(
            P("expert", ("tensor", "dp")),
            P("expert", None),
            P("expert", None),
            P("expert", ("tensor", "dp"), None),
            P("expert", None, None, ("tensor", "dp")),
            P(("tensor", "dp"), None),
            P(None, "expert", ("tensor", "dp")),
        ),
        out_specs=(
            P("expert", None, None, ("tensor", "dp")),
            P("expert", ("tensor", "dp"), None),
            P(None, "expert", ("tensor", "dp")),
            P(("tensor", "dp"), "expert"),
        ),
        check_vma=False,
    )
```

profile of v0, /device:TPU:1, one launch (start us, length us, event | category | flops | bytes accessed | tf_op | source)
XLA Modules:
  0.0 416.5 jit_solution(9677018746168350140)
XLA Ops:
  7.2 0.0 all-gather.5.cloned.1.call-start
  7.2 0.7 all-gather.5.cloned.1.call-update
  7.9 0.0 reduce-scatter.2.cloned.1.call-start
  8.0 82.5 %all-gather.5.cloned.1.call-done = bf16[256,3584]{0,1:T(8,128)(2,1)} async-done(((bf16[256,224]{0,1:T(8,128)(2,1)}), bf16[256,3584]{0,1:T(8,128)(2,1)}) %all-gather.5.cloned.1.call-update) | async-done | bytes 1835024 | tf_op jit(solution)/shard_map/all_gather | solution.py:73
  90.5 4.1 fusion.35
  94.6 0.0 reduce-scatter.2.cloned.1.call-update
  94.6 0.0 all-gather.3.cloned.1.call-start
  94.7 0.6 copy-done.3
  95.3 0.1 copy.36
  95.4 0.1 eq.42
  95.6 0.1 eq.38
  95.7 1.2 reduce-window.6
  96.9 0.2 slice_reduce_fusion
  97.2 0.1 fusion.33
  97.3 0.1 reduce_sum.21
  97.5 0.1 copy.39
  97.6 0.3 select_reduce_fusion
  97.9 0.6 convolution_convert_fusion.1
  98.5 0.2 copy.40
  98.7 0.1 reshape.85
  98.8 41.8 %all_to_all.5 = bf16[64,12,224]{2,1,0:T(8,128)(2,1)S(1)} all-to-all(bf16[64,12,224]{2,1,0:T(8,128)(2,1)S(1)} %reshape.85), channel_id=1, replica_groups=mesh['expert'=64,'tensor'=8,'dp'=2] {'expert'}, dimensions={0} | all-to-all | bytes 688128 | tf_op jit(solution)/shard_map/all_to_all | solution.py:70
  140.6 0.2 reshape.86
  140.8 0.9 copy.41
  141.7 0.0 all-gather.3.cloned.1.call-update
  141.8 2.0 fusion.41
  143.8 0.7 pad_maximum_fusion.1
  144.5 122.5 %reduce-scatter.2.cloned.1.call-done = f32[152,56]{0,1:T(8,128)} async-done(((f32[152,3584]{0,1:T(8,128)}), f32[152,56]{0,1:T(8,128)}) %reduce-scatter.2.cloned.1.call-update) | async-done | bytes 34064 | tf_op jit(solution)/shard_map/reduce_scatter | solution.py:76
  267.1 1.4 convert_element_type.70
  268.5 133.8 %all-gather.3.cloned.1.call-done = bf16[768,3584]{0,1:T(8,128)(2,1)} async-done(((bf16[768,224]{0,1:T(8,128)(2,1)}), bf16[768,3584]{0,1:T(8,128)(2,1)}) %all-gather.3.cloned.1.call-update) | async-done | bytes 5505040 | tf_op jit(solution)/shard_map/all_gather | solution.py:45
  402.3 3.8 fusion.18
  406.2 0.8 pad_maximum_fusion
  407.0 3.0 fusion
  (19 shorter events, 0.1 us)
Async XLA Ops:
  7.2 395.2 %copy-start = (bf16[1,152,3584]{2,1,0:T(8,128)(2,1)S(1)}, bf16[1,152,3584]{2,1,0:T(8,128)(2,1)}, u32[]{:S(2)}) copy-start(bf16[1,152,3584]{2,1,0:T(8,128)(2,1)} %param.10) | copy-start | bytes 3268612
  7.2 83.3 %all-gather.5.cloned.1.call-start = ((), (), s32[]{:S(2)}) async-start(), calls=%async_computation.3 | async-start | bytes 1949696 | tf_op jit(solution)/shard_map/all_gather | solution.py:73
  7.9 259.1 %reduce-scatter.2.cloned.1.call-start = ((), (), s32[]{:S(2)}) async-start(), calls=%async_computation.4 | async-start | bytes 3727360 | tf_op jit(solution)/shard_map/reduce_scatter | solution.py:76
  94.6 0.7 copy-start.3
  94.6 3.0 copy-start.4
  94.6 3.3 copy-start.1
  94.6 307.7 %all-gather.3.cloned.1.call-start = ((), (), s32[]{:S(2)}) async-start(), calls=%async_computation.2 | async-start | bytes 5849088 | tf_op jit(solution)/shard_map/all_gather | solution.py:45
  98.7 43.1 %copy-start.2 = (bf16[2,256,152]{1,2,0:T(8,128)(2,1)S(1)}, bf16[2,256,152]{1,2,0:T(8,128)(2,1)}, u32[]{:S(2)}) copy-start(bf16[2,256,152]{1,2,0:T(8,128)(2,1)} %param.13) | copy-start | bytes 466948
  98.7 43.1 %copy-start.6 = (bf16[152,3584]{1,0:T(8,128)(2,1)S(1)}, bf16[152,3584]{1,0:T(8,128)(2,1)}, u32[]{:S(2)}) copy-start(bf16[152,3584]{1,0:T(8,128)(2,1)} %param.12) | copy-start | bytes 3268612
  141.8 260.5 %copy-start.7 = (bf16[1,2,768,152]{2,3,1,0:T(8,128)(2,1)S(1)}, bf16[1,2,768,152]{2,3,1,0:T(8,128)(2,1)}, u32[]{:S(2)}) copy-start(bf16[1,2,768,152]{2,3,1,0:T(8,128)(2,1)} %param.11) | copy-start | bytes 1400836
  402.3 4.7 %copy-start.5 = (bf16[768,3584]{0,1:T(8,128)(2,1)S(1)}, bf16[768,3584]{0,1:T(8,128)(2,1)}, u32[]{:S(2)}) copy-start(bf16[768,3584]{0,1:T(8,128)(2,1)} %all-gather.3.cloned.1.call-done) | copy-start | bytes 16515076
Sparse Core Ops, SparseCore 0:
  10.7 79.7 all-gather.4
  96.4 170.6 reduce-scatter.1
  270.7 131.6 all-gather.2
where the time goes:
time: 418 us; the launch traced here: 416 us
  waiting for transfers between devices  340 us (81%)
  blocking collectives  41.8 us (10%)
  between operations  13.9 us (3%)
  matrix products  13.5 us (3%)
  other arithmetic  4.65 us (1%)
    all_gather x1, waiting for transfers between devices, expert_fold(): lax.all_gather(received, ('tensor', 'dp'), axis=1, tiled=True)  134 us
    reduce_scatter x1, waiting for transfers between devices, body(): lax.psum_scatter(dense_grad, 'expert', scatter_dimension=1, tiled=True)  123 us
    all_gather x1, waiting for transfers between devices, body(): lax.all_gather(grad_out, ('tensor', 'dp'), axis=1, tiled=True)  82.5 us
    all_to_all x1, blocking collectives, body(): lax.all_to_all(outgoing, 'expert', split_axis=0, concat_axis=0, tiled=True)  41.8 us
  transfers between devices with their start and end apart: 3, of which 3 were waited for; matrix products, arithmetic and copies ran while one was open for 2% of the time, Pallas kernels for 0%

commit v1 on v0

v1 whole, which is shorter than its diff:
```python
import jax
import jax.numpy as jnp
from jax import lax
from jax.sharding import Mesh, PartitionSpec as P

BF = jnp.bfloat16
F32 = jnp.float32
EXPERT = ("zh", "x", "core")
SHARE = ("y", "zl")


def slot_numbers(routes_group, expert_count, capacity):
    flat_routes = routes_group.reshape(-1)
    experts_row = jnp.arange(expert_count, dtype=jnp.int32)
    onehot = (flat_routes[:, None] == experts_row[None, :]).astype(jnp.int32)
    before = jnp.cumsum(onehot, axis=0) - onehot
    position = jnp.sum(before * onehot, axis=1)
    return (flat_routes * capacity + position).reshape(routes_group.shape)


def dispatch_table(routes_group, probs_group, expert_count, capacity):
    slots_here = slot_numbers(routes_group, expert_count, capacity)
    targets = jnp.arange(expert_count * capacity, dtype=jnp.int32)
    match = slots_here[None, :, :] == targets[:, None, None]
    return jnp.sum(jnp.where(match, probs_group[None, :, :], jnp.float32(0.0)), axis=2)


def swiglu_parts(saved_pair):
    gate_pre = saved_pair[0].astype(F32)
    up_pre = saved_pair[1].astype(F32)
    sigmoid_gate = jax.nn.sigmoid(gate_pre)
    hidden = (gate_pre * sigmoid_gate * up_pre).astype(BF)
    return (gate_pre, up_pre, sigmoid_gate, hidden)


def pre_cotangents(hidden_cot, gate_pre, up_pre, sigmoid_gate):
    gate_cot = hidden_cot * up_pre * sigmoid_gate * (1.0 + gate_pre * (1.0 - sigmoid_gate))
    up_cot = hidden_cot * gate_pre * sigmoid_gate
    return jnp.stack([gate_cot, up_cot]).astype(BF)


def gather_features(columns):
    other = lax.ppermute(columns, "zl", [(0, 1), (1, 0)])
    first = lax.axis_index("zl") == 0
    pair = jnp.stack([jnp.where(first, columns, other), jnp.where(first, other, columns)])
    whole = lax.all_gather(pair, "y", axis=0, tiled=False)
    return whole.reshape(-1, columns.shape[1])


def scatter_sum(terms):
    parts = lax.axis_size(EXPERT)
    width, hidden = terms.shape[0] // parts, terms.shape[1]
    blocks = terms.astype(BF).reshape(parts, width, hidden)
    whole = hidden // 128 * 128
    tail = blocks[:, :, whole:].reshape(parts, width * (hidden - whole))
    tail_rows = -(-tail.shape[1] // 128)
    tail = jnp.pad(tail, ((0, 0), (0, tail_rows * 128 - tail.shape[1]))).reshape(parts, tail_rows, 128)
    packed = jnp.concatenate([blocks[:, :, :whole].reshape(parts, -1, 128), tail], axis=1)
    came = lax.all_to_all(packed, EXPERT, split_axis=0, concat_axis=0, tiled=True)
    total = jnp.sum(came.astype(F32), axis=0)
    head_rows = width * whole // 128
    head = total[:head_rows].reshape(width, whole)
    tail = total[head_rows:].reshape(-1)[: width * (hidden - whole)].reshape(width, hidden - whole)
    return jnp.concatenate([head, tail], axis=1)


def body(grad_out, routes, probs, expert_down, expert_saved, dense_down, dense_saved):
    expert_count = lax.axis_size(EXPERT)
    capacity = expert_saved.shape[2] // expert_count
    feature_width = grad_out.shape[1]
    down_local = expert_down[0]

    grad_whole = gather_features(grad_out.T)

    table = dispatch_table(routes, probs, expert_count, capacity)
    outgoing = jnp.dot(table, grad_out.astype(F32), precision=lax.Precision.HIGHEST).astype(BF)
    outgoing = outgoing.reshape(expert_count, capacity * feature_width // 128, 128)
    received = lax.all_to_all(outgoing, EXPERT, split_axis=0, concat_axis=0, tiled=True)
    received = received.reshape(expert_count * capacity, feature_width)
    sent = gather_features(received.T)

    gate_dense, up_dense, sigmoid_dense, dense_hidden = swiglu_parts(dense_saved)
    dense_terms = jnp.einsum("fr,rh->fh", grad_whole, dense_hidden, preferred_element_type=F32)
    dense_share = scatter_sum(dense_terms)
    dense_cot = jnp.einsum("fr,hf->rh", grad_whole, dense_down, preferred_element_type=F32)

    gate_expert, up_expert, sigmoid_expert, expert_hidden = swiglu_parts(expert_saved[0])
    expert_cot = jnp.einsum("fr,hf->rh", sent, down_local, preferred_element_type=F32)
    expert_grad = jnp.einsum("rh,fr->hf", expert_hidden, sent, preferred_element_type=F32)

    expert_pre_grad = pre_cotangents(expert_cot, gate_expert, up_expert, sigmoid_expert)[None]
    expert_down_grad = expert_grad.astype(BF)[None]
    dense_pre_grad = pre_cotangents(dense_cot, gate_dense, up_dense, sigmoid_dense)
    dense_down_grad = dense_share.T.astype(BF)
    return (expert_pre_grad, expert_down_grad, dense_pre_grad, dense_down_grad)


def solution(mesh):
    experts, tensors, pairs = mesh.devices.shape
    chips = min(8, experts // 2)
    fine = Mesh(
        mesh.devices.reshape(experts // (2 * chips), chips, 2, tensors, pairs),
        EXPERT + SHARE,
    )
    return jax.shard_map(
        body,
        mesh=fine,
        in_specs=(
            P(EXPERT, SHARE),
            P(EXPERT, None),
            P(EXPERT, None),
            P(EXPERT, SHARE, None),
            P(EXPERT, None, None, SHARE),
            P(SHARE, None),
            P(None, EXPERT, SHARE),
        ),
        out_specs=(
            P(EXPERT, None, None, SHARE),
            P(EXPERT, SHARE, None),
            P(None, EXPERT, SHARE),
            P(SHARE, EXPERT),
        ),
        check_vma=False,
    )
```

time: 418 us -> 163 us (0.39)
  waiting for transfers between devices: 340 us -> 57.6 us
  starting transfers between devices: 0.12 us -> 22.7 us
  local copies, waits for them, and re-layouts: 2.88 us -> 10.3 us
    all_gather x2, waiting for transfers between devices: 216 us -> 17 us  [gather_features(): whole = lax.all_gather(pair, 'y', axis=0, tiled=False)]
    reduce_scatter x1 -> x0, waiting for transfers between devices: 123 us -> none  [body(): lax.psum_scatter(dense_grad, 'expert', scatter_dimension=1, tiled=True)]
    all_to_all x0 -> x1, waiting for transfers between devices: none -> 29.4 us  [scatter_sum(): lax.all_to_all(packed, EXPERT, split_axis=0, concat_axis=0, tiled=True)]
    all_to_all x0 -> x1, starting transfers between devices: none -> 13.9 us  [scatter_sum(): lax.all_to_all(packed, EXPERT, split_axis=0, concat_axis=0, tiled=True)]
    ppermute x0 -> x2, waiting for transfers between devices: none -> 11.2 us  [gather_features(): other = lax.ppermute(columns, 'zl', [(0, 1), (1, 0)])]
    ppermute x0 -> x2, starting transfers between devices: none -> 8.75 us  [gather_features(): other = lax.ppermute(columns, 'zl', [(0, 1), (1, 0)])]
  transfers between devices with their start and end apart: 3 -> 5, of which waited for: 3 -> 4; matrix products, arithmetic and copies ran while one was open for 2% -> 13% of each run, Pallas kernels for 0% -> 0%
where the time goes in v1:
time: 163 us
  waiting for transfers between devices  57.6 us (35%)
  blocking collectives  38.2 us (23%)
  starting transfers between devices  22.7 us (14%)
  between operations  14.3 us (9%)
  matrix products  12.6 us (8%)
  local copies, waits for them, and re-layouts  10.3 us (6%)
  other arithmetic  7.06 us (4%)
    all_to_all x1, blocking collectives, body(): lax.all_to_all(outgoing, EXPERT, split_axis=0, concat_axis=0, tiled=True)  38.2 us
    all_to_all x1, waiting for transfers between devices, scatter_sum(): lax.all_to_all(packed, EXPERT, split_axis=0, concat_axis=0, tiled=True)  29.4 us
    all_gather x2, waiting for transfers between devices, gather_features(): whole = lax.all_gather(pair, 'y', axis=0, tiled=False)  17 us
    all_to_all x1, starting transfers between devices, scatter_sum(): lax.all_to_all(packed, EXPERT, split_axis=0, concat_axis=0, tiled=True)  13.9 us
    ppermute x2, waiting for transfers between devices, gather_features(): other = lax.ppermute(columns, 'zl', [(0, 1), (1, 0)])  11.2 us
    ppermute x2, starting transfers between devices, gather_features(): other = lax.ppermute(columns, 'zl', [(0, 1), (1, 0)])  8.75 us
    dot_general x1, matrix products, body(): jnp.einsum('rh,fr->hf', expert_hidden, sent, preferred_element_type=F32)  5.63 us
  transfers between devices with their start and end apart: 5, of which 4 were waited for; matrix products, arithmetic and copies ran while one was open for 13% of the time, Pallas kernels for 0%

profile of v1, /device:TPU:1, one launch (start us, length us, event | category | flops | bytes accessed | tf_op | source)
XLA Modules:
  0.0 162.9 jit_solution(4548334652107290294)
XLA Ops:
  7.2 5.9 %collective-permute-start.1 = (bf16[224,256]{1,0:T(8,128)(2,1)}, bf16[224,256]{1,0:T(8,128)(2,1)S(1)}, u32[]{:S(2)}, u32[]{:S(2)}) collective-permute-start(bf16[224,256]{1,0:T(8,128)(2,1)} %bitcast.162), channel_id=1, source_target_pairs={{0,1},{1,0},{2,3},{3,2},{4,5},{5,4},{6,7},{7,6},{8,9},{9,8},{10,11... | collective-permute-start | bytes 344072 | tf_op jit(solution)/shard_map/ppermute | solution.py:43
  13.1 2.4 %collective-permute-done.1 = bf16[224,256]{1,0:T(8,128)(2,1)S(1)} collective-permute-done((bf16[224,256]{1,0:T(8,128)(2,1)}, bf16[224,256]{1,0:T(8,128)(2,1)S(1)}, u32[]{:S(2)}, u32[]{:S(2)}) %collective-permute-start.1) | collective-permute-done | bytes 114720 | tf_op jit(solution)/shard_map/ppermute | solution.py:43
  15.5 0.9 select_bitcast_fusion.3
  16.4 0.7 pad_maximum_fusion.3
  17.2 0.8 copy.56
  18.3 1.2 reduce-window.6
  19.5 0.2 slice_reduce_fusion
  20.2 0.3 select_reduce_fusion
  20.5 0.6 convolution_convert_fusion.2
  21.3 0.8 reshape.110
  22.1 38.2 %all_to_all.10 = bf16[64,21,128]{2,1,0:T(8,128)(2,1)S(1)} all-to-all(bf16[64,21,128]{2,1,0:T(8,128)(2,1)S(1)} %reshape.110), channel_id=1, replica_groups=mesh['zh'=4,'x'=8,'core'=2,'y'=8,'zl'=2] {'zh','x','core'}, dimensions={0} | all-to-all | bytes 688128 | tf_op jit(solution)/shard_map/all_to_all | solution.py:78
  60.4 0.6 reshape.111
  60.9 2.9 %collective-permute-start = (bf16[224,768]{0,1:T(8,128)(2,1)S(1)}, bf16[224,768]{0,1:T(8,128)(2,1)S(1)}, u32[]{:S(2)}, u32[]{:S(2)}) collective-permute-start(bf16[224,768]{0,1:T(8,128)(2,1)S(1)} %bitcast.159), channel_id=1, source_target_pairs={{0,1},{1,0},{2,3},{3,2},{4,5},{5,4},{6,7},{7,6},{8,9},{9,8},{10,11... | collective-permute-start | bytes 1032200 | tf_op jit(solution)/shard_map/ppermute | solution.py:43
  63.8 8.8 %collective-permute-done = bf16[224,768]{0,1:T(8,128)(2,1)S(1)} collective-permute-done((bf16[224,768]{0,1:T(8,128)(2,1)S(1)}, bf16[224,768]{0,1:T(8,128)(2,1)S(1)}, u32[]{:S(2)}, u32[]{:S(2)}) %collective-permute-start) | collective-permute-done | bytes 344096 | tf_op jit(solution)/shard_map/ppermute | solution.py:43
  72.9 1.2 copy.61
  74.1 3.2 %convolution_convert_fusion = bf16[3584,152]{0,1:T(8,128)(2,1)} fusion(bf16[3584,256]{1,0:T(8,128)(2,1)} %bitcast.157, bf16[2,256,152]{1,2,0:T(8,128)(2,1)S(1)} %copy-done.3), kind=kOutput, calls=%fused_computation | convolution fusion | flops 279777280 | bytes 3080192 | tf_op jit(solution)/shard_map/fr,rh->fh/dot_general | solution.py:83
  77.4 1.7 %copy.62 = bf16[3584,152]{1,0:T(8,128)(2,1)S(1)} copy(bf16[3584,152]{0,1:T(8,128)(2,1)} %convolution_convert_fusion) | data formatting | bytes 2179072 | tf_op jit(solution)/shard_map/convert_element_type | solution.py:53
  79.1 1.1 slice.51
  80.2 1.1 slice.50
  81.2 1.7 %copy.63 = bf16[64,56,24]{0,2,1:T(8,128)(2,1)S(1)} copy(bf16[64,56,24]{2,1,0:T(8,128)(2,1)} %slice.51) | data formatting | bytes 344064 | tf_op jit(solution)/shard_map/slice | solution.py:55
  83.0 0.3 copy.65
  83.3 1.2 pad_maximum_fusion
  84.5 13.9 %all-to-all-start.1 = ((bf16[64,67,128]{2,1,0:T(8,128)(2,1)}), bf16[64,67,128]{2,1,0:T(8,128)(2,1)S(1)}, u32[]{:S(2)}, u32[]{:S(2)}) async-start(bf16[64,67,128]{2,1,0:T(8,128)(2,1)} %pad_maximum_fusion), calls=%async_computation.1 | async-start | bytes 2359296 | tf_op jit(solution)/shard_map/all_to_all | solution.py:59
  98.4 2.0 %fusion.50 = (bf16[1,256,152]{1,2,0:T(8,128)(2,1)S(1)}, bf16[1,256,152]{1,2,0:T(8,128)(2,1)S(1)}) fusion(bf16[2,256,152]{1,2,0:T(8,128)(2,1)S(1)} %copy-done.3, bf16[3584,256]{1,0:T(8,128)(2,1)} %bitcast.158, bf16[152,3584]{1,0:T(8,128)(2,1)S(1)} %copy-done.7), kind=kOutput, calls=%fused_computation.77 | convolution fusion | flops 279504896 | bytes 3235840 | tf_op jit(solution)/shard_map/fr,hf->rh/dot_general | solution.py:85
  100.4 0.7 pad_maximum_fusion.4
  101.1 29.4 %all-to-all-done.1 = bf16[64,67,128]{2,1,0:T(8,128)(2,1)S(1)} async-done(((bf16[64,67,128]{2,1,0:T(8,128)(2,1)}), bf16[64,67,128]{2,1,0:T(8,128)(2,1)S(1)}, u32[]{:S(2)}, u32[]{:S(2)}) %all-to-all-start.1) | async-done | bytes 1097760 | tf_op jit(solution)/shard_map/all_to_all | solution.py:59
  130.5 0.2 reduce
  130.8 0.6 maximum_bitcast_fusion
  131.4 17.0 %all-gather.5.cloned.1.call-done = bf16[16,224,768]{2,1,0:T(8,128)(2,1)} async-done(((bf16[2,224,768]{2,1,0:T(8,128)(2,1)}), bf16[16,224,768]{2,1,0:T(8,128)(2,1)}) %all-gather.5.cloned.1.call-update) | async-done | bytes 5505040 | tf_op jit(solution)/shard_map/all_gather | solution.py:46
  148.4 5.6 %fusion = bf16[1,152,3584]{2,1,0:T(8,128)(2,1)} fusion(bf16[3584,768]{1,0:T(8,128)(2,1)} %bitcast.164, bf16[1,2,768,152]{2,3,1,0:T(8,128)(2,1)S(1)} %copy-done.8), kind=kOutput, calls=%fused_computation.2 | convolution fusion | flops 838242304 | bytes 7061504 | tf_op jit(solution)/shard_map/rh,fr->hf/dot_general | solution.py:89
  154.0 1.2 fusion.26
  155.2 0.8 pad_maximum_fusion.2
  (39 shorter events, 1.4 us)
Async XLA Ops:
  7.2 146.9 %copy-start = (bf16[1,152,3584]{2,1,0:T(8,128)(2,1)S(1)}, bf16[1,152,3584]{2,1,0:T(8,128)(2,1)}, u32[]{:S(2)}) copy-start(bf16[1,152,3584]{2,1,0:T(8,128)(2,1)} %param.10) | copy-start | bytes 3268612
  7.2 13.0 %copy-start.4 = (s32[256,2]{0,1:T(2,128)S(1)}, s32[256,2]{0,1:T(2,128)}, u32[]{:S(2)}) copy-start(s32[256,2]{0,1:T(2,128)} %param.8) | copy-start | bytes 6148
  7.2 13.0 %copy-start.5 = (f32[256,2]{0,1:T(2,128)S(1)}, f32[256,2]{0,1:T(2,128)}, u32[]{:S(2)}) copy-start(f32[256,2]{0,1:T(2,128)} %param.9) | copy-start | bytes 6148
  7.2 66.9 %all-gather.7.cloned.1.call-start = ((), (), s32[]{:S(2)}) async-start(), calls=%async_computation.3 | async-start | bytes 2064384 | tf_op jit(solution)/shard_map/all_gather | solution.py:46
  7.2 8.3 %collective-permute-start.1 = (bf16[224,256]{1,0:T(8,128)(2,1)}, bf16[224,256]{1,0:T(8,128)(2,1)S(1)}, u32[]{:S(2)}, u32[]{:S(2)}) collective-permute-start(bf16[224,256]{1,0:T(8,128)(2,1)} %bitcast.162), channel_id=1, source_target_pairs={{0,1},{1,0},{2,3},{3,2},{4,5},{5,4},{6,7},{7,6},{8,9},{9,8},{10,11... | collective-permute-start | bytes 344072 | tf_op jit(solution)/shard_map/ppermute | solution.py:43
  13.1 7.4 %copy-start.2 = (bf16[256,224]{0,1:T(8,128)(2,1)S(1)}, bf16[256,224]{0,1:T(8,128)(2,1)}, u32[]{:S(2)}) copy-start(bf16[256,224]{0,1:T(8,128)(2,1)} %param.7) | copy-start | bytes 344068
  17.2 131.2 %all-gather.5.cloned.1.call-start = ((), (), s32[]{:S(2)}) async-start(), calls=%async_computation.2 | async-start | bytes 6193152 | tf_op jit(solution)/shard_map/all_gather | solution.py:46
  60.9 11.7 %collective-permute-start = (bf16[224,768]{0,1:T(8,128)(2,1)S(1)}, bf16[224,768]{0,1:T(8,128)(2,1)S(1)}, u32[]{:S(2)}, u32[]{:S(2)}) collective-permute-start(bf16[224,768]{0,1:T(8,128)(2,1)S(1)} %bitcast.159), channel_id=1, source_target_pairs={{0,1},{1,0},{2,3},{3,2},{4,5},{5,4},{6,7},{7,6},{8,9},{9,8},{10,11... | collective-permute-start | bytes 1032200 | tf_op jit(solution)/shard_map/ppermute | solution.py:43
  72.7 1.4 copy-start.3
  81.2 2.1 %copy-start.1 = (bf16[64,56,128]{2,1,0:T(8,128)(2,1)S(1)}, bf16[64,56,128]{2,1,0:T(8,128)(2,1)}, u32[]{:S(2)}) copy-start(bf16[64,56,128]{2,1,0:T(8,128)(2,1)} %slice.50) | copy-start | bytes 2752516
  84.5 13.9 %copy-start.7 = (bf16[152,3584]{1,0:T(8,128)(2,1)S(1)}, bf16[152,3584]{1,0:T(8,128)(2,1)}, u32[]{:S(2)}) copy-start(bf16[152,3584]{1,0:T(8,128)(2,1)} %param.12) | copy-start | bytes 3268612
  84.5 46.0 %all-to-all-start.1 = ((bf16[64,67,128]{2,1,0:T(8,128)(2,1)}), bf16[64,67,128]{2,1,0:T(8,128)(2,1)S(1)}, u32[]{:S(2)}, u32[]{:S(2)}) async-start(bf16[64,67,128]{2,1,0:T(8,128)(2,1)} %pad_maximum_fusion), calls=%async_computation.1 | async-start | bytes 2359296 | tf_op jit(solution)/shard_map/all_to_all | solution.py:59
  100.4 48.0 %copy-start.8 = (bf16[1,2,768,152]{2,3,1,0:T(8,128)(2,1)S(1)}, bf16[1,2,768,152]{2,3,1,0:T(8,128)(2,1)}, u32[]{:S(2)}) copy-start(bf16[1,2,768,152]{2,3,1,0:T(8,128)(2,1)} %param.11) | copy-start | bytes 1400836
  148.4 5.6 %copy-start.6 = (bf16[16,224,768]{2,1,0:T(8,128)(2,1)S(1)}, bf16[16,224,768]{2,1,0:T(8,128)(2,1)}, u32[]{:S(2)}) copy-start(bf16[16,224,768]{2,1,0:T(8,128)(2,1)} %all-gather.5.cloned.1.call-done) | copy-start | bytes 16515076
Sparse Core Ops, SparseCore 0:
  17.3 52.6 all-gather.6
  74.2 74.1 all-gather.4

commit v2 on v1

v2 whole, which is shorter than its diff:
```python
import functools

import jax
import jax.numpy as jnp
from jax import lax
from jax.experimental import pallas as pl
from jax.experimental.pallas import tpu as pltpu
from jax.sharding import Mesh, PartitionSpec as P

BF = jnp.bfloat16
F32 = jnp.float32
EXPERT = ("zh", "x", "core")
SHARE = ("y", "zl")
LANES = 128
VMEM_LIMIT = 48 * 1024 * 1024


def local_kernel(kernel, outs, flops, moved, scalars=0, arrays=1):
    specs = [pl.BlockSpec(memory_space=pltpu.SMEM)] * scalars
    return pl.pallas_call(
        kernel,
        out_shape=outs,
        in_specs=specs + [pl.BlockSpec(memory_space=pltpu.VMEM)] * arrays,
        compiler_params=pltpu.CompilerParams(vmem_limit_bytes=VMEM_LIMIT),
        cost_estimate=pl.CostEstimate(flops=flops, bytes_accessed=moved, transcendentals=0),
    )


def dispatch_kernel(experts, capacity, routes_ref, probs_ref, grad_ref, out_ref):
    tokens, features = routes_ref.shape[1], grad_ref.shape[0]
    rows = out_ref.shape[0]
    first, second = routes_ref[0:1, :], routes_ref[1:2, :]
    names = lax.broadcasted_iota(jnp.int32, (experts, tokens), 0)
    on_first, on_second = names == first, names == second
    named = (on_first | on_second).astype(F32).astype(BF)
    earlier = lax.broadcasted_iota(jnp.int32, (tokens, tokens), 0) < lax.broadcasted_iota(
        jnp.int32, (tokens, tokens), 1
    )
    before = jnp.dot(named, earlier.astype(F32).astype(BF), preferred_element_type=F32)
    place_first = jnp.sum(jnp.where(on_first, before, 0.0), axis=0, keepdims=True)
    place_second = jnp.sum(jnp.where(on_second, before, 0.0), axis=0, keepdims=True)
    slot_first = first * capacity + place_first.astype(jnp.int32)
    slot_second = second * capacity + place_second.astype(jnp.int32)
    step = rows // 4
    for part in range(4):
        row = lax.broadcasted_iota(jnp.int32, (step, 1), 0) + part * step
        slot = row // (2 * capacity) * capacity + row % capacity
        is_first, is_second = slot == slot_first, slot == slot_second
        table = jnp.where(is_first, probs_ref[0:1, :], jnp.where(is_second, probs_ref[1:2, :], 0.0))
        weight = jnp.sum(table, axis=1, keepdims=True)
        onehot = (is_first | is_second).astype(F32).astype(BF)
        picked = lax.dot_general(
            onehot, grad_ref[...], (((1,), (1,)), ((), ())), preferred_element_type=F32
        )
        sent = picked * weight
        low = sent[:, :LANES]
        high = jnp.concatenate(
            [sent[:, LANES:], jnp.zeros((step, 2 * LANES - features), F32)], axis=1
        )
        out_ref[part * step : (part + 1) * step, :] = jnp.where(
            row % (2 * capacity) < capacity, low, high
        ).astype(BF)


def arrange_kernel(capacity, came_ref, out_ref):
    rows, features, slots = came_ref.shape[0], out_ref.shape[0], out_ref.shape[1]
    parts = 2
    row_step, slot_step = rows // parts, slots // parts
    row = lax.broadcasted_iota(jnp.int32, (row_step, 1), 0)
    slot = lax.broadcasted_iota(jnp.int32, (1, slot_step), 1)
    wanted = slot // capacity * (2 * capacity) + slot % capacity
    for half in range(2):
        pick = (row == wanted + half * capacity).astype(F32).astype(BF)
        for part in range(parts):
            block = came_ref[part * row_step : (part + 1) * row_step, :]
            value = lax.dot_general(
                block, pick, (((0,), (0,)), ((), ())), preferred_element_type=F32
            ).astype(BF)
            top = min(features - half * LANES, LANES)
            out_ref[half * LANES : half * LANES + top, part * slot_step : (part + 1) * slot_step] = value[
                :top, :
            ]


def split_kernel(runs, half_ref, dense_ref, expert_ref, mine_ref, theirs_ref):
    width = dense_ref.shape[1] // (2 * runs)

    def columns(ref, half):
        return jnp.concatenate(
            [ref[:, (2 * run + half) * width : (2 * run + half + 1) * width] for run in range(runs)], axis=1
        )

    for half in range(2):

        @pl.when(half_ref[0] == half)
        def _():
            for index, ref in enumerate((dense_ref, expert_ref)):
                mine_ref[index] = columns(ref, half)
                theirs_ref[index] = columns(ref, 1 - half)


def join_kernel(runs, half_ref, own_ref, other_ref, out_ref):
    width = own_ref.shape[1] // runs

    def joined(low_ref, high_ref):
        pieces = []
        for run in range(runs):
            for ref in (low_ref, high_ref):
                pieces.append(ref[:, run * width : (run + 1) * width])
        return jnp.concatenate(pieces, axis=1)

    @pl.when(half_ref[0] == 0)
    def _():
        out_ref[...] = joined(own_ref, other_ref)

    @pl.when(half_ref[0] == 1)
    def _():
        out_ref[...] = joined(other_ref, own_ref)


def swiglu_parts(gate_saved, up_saved):
    gate_pre = gate_saved.astype(F32)
    up_pre = up_saved.astype(F32)
    sigmoid_gate = jax.nn.sigmoid(gate_pre)
    hidden = (gate_pre * sigmoid_gate * up_pre).astype(BF)
    return (gate_pre, up_pre, sigmoid_gate, hidden)


def pre_cotangents(hidden_cot, gate_pre, up_pre, sigmoid_gate):
    gate_cot = hidden_cot * up_pre * sigmoid_gate * (1.0 + gate_pre * (1.0 - sigmoid_gate))
    up_cot = hidden_cot * gate_pre * sigmoid_gate
    return jnp.stack([gate_cot, up_cot]).astype(BF)


def after(values, earlier):
    return lax.optimization_barrier((values, earlier))[0]


def swap(values):
    return lax.ppermute(values, "zl", [(0, 1), (1, 0)])


def gather_columns(rows):
    whole = lax.all_gather(rows, "y", axis=0, tiled=False)
    return whole.reshape(-1, rows.shape[1])


def terms_kernel(runs, grad_ref, first_ref, second_ref, out_ref):
    parts, rows, _ = out_ref.shape
    hidden, width = first_ref.shape[0], grad_ref.shape[0] * 2 // parts
    span = parts // (2 * runs)
    stack, extra = rows - width, hidden - LANES
    for run in range(runs):
        grads = grad_ref[run * span * width : (run + 1) * span * width, :]
        for half, ref in enumerate((first_ref, second_ref)):
            value = lax.dot_general(
                grads, ref[...], (((1,), (1,)), ((), ())), preferred_element_type=F32
            )
            for index in range(span):
                block = value[index * width : (index + 1) * width, :]
                last = jnp.concatenate(
                    [block[:, LANES:], jnp.zeros((-width % stack, extra), F32)], axis=0
                )
                count = last.shape[0] // stack
                last = jnp.concatenate(
                    [last[piece * stack : (piece + 1) * stack, :] for piece in range(count)]
                    + [jnp.zeros((stack, LANES - count * extra), F32)],
                    axis=1,
                )
                out_ref[(run * 2 + half) * span + index] = jnp.concatenate(
                    [block[:, :LANES], last], axis=0
                ).astype(BF)


def total_kernel(came_ref, out_ref):
    parts, rows, _ = came_ref.shape
    width, hidden = out_ref.shape
    stack, extra = rows - width, hidden - LANES
    total = came_ref[0].astype(F32)
    for part in range(1, parts):
        total = total + came_ref[part].astype(F32)
    last = jnp.concatenate(
        [total[width:, piece * extra : (piece + 1) * extra] for piece in range(-(-width // stack))], axis=0
    )
    out_ref[...] = jnp.concatenate([total[:width, :], last[:width, :]], axis=1).astype(BF)


def scatter_terms(grad_half, units):
    parts, runs = lax.axis_size(EXPERT), lax.axis_size("y")
    width, hidden = grad_half.shape[0] * 2 // parts, units[0].shape[0]
    return local_kernel(
        functools.partial(terms_kernel, runs),
        jax.ShapeDtypeStruct((parts, width + 16, LANES), BF),
        4 * grad_half.shape[0] * hidden * grad_half.shape[1],
        4 * parts * width * LANES,
        0,
        3,
    )(grad_half, *units)


def scatter_total(came, width, hidden):
    mine = local_kernel(
        total_kernel, jax.ShapeDtypeStruct((width, hidden), BF), came.size, 2 * came.size
    )(came)
    chips = lax.axis_size("x")
    route = [(2 * x + z, 2 * (x ^ 2) + (1 - z)) for x in range(chips) for z in range(2)]
    other = lax.ppermute(mine, ("x", "zl"), route)
    here = lax.axis_index("x") // 2 % 2 == lax.axis_index("zl")
    return jnp.where(here, mine, other)


def body(grad_out, routes, probs, expert_down, expert_saved, dense_down, dense_saved):
    expert_count, runs = lax.axis_size(EXPERT), lax.axis_size("y")
    slots, hidden_count = expert_saved.shape[2:]
    capacity = slots // expert_count
    tokens, feature_width = grad_out.shape
    model_width = dense_down.shape[1]
    half = lax.axis_index("zl").astype(jnp.int32)
    half_index = half.reshape(1)
    grad_rows = grad_out.T

    grad_half = gather_columns(grad_rows)

    outgoing = local_kernel(
        functools.partial(dispatch_kernel, expert_count, capacity),
        jax.ShapeDtypeStruct((expert_count * 2 * capacity, LANES), BF),
        4 * slots * tokens * feature_width,
        4 * slots * LANES,
        arrays=3,
    )(routes.T, probs.T, grad_rows)
    outgoing = outgoing.reshape(expert_count, 2 * capacity, LANES)
    received = lax.all_to_all(outgoing, EXPERT, split_axis=0, concat_axis=0, tiled=True)
    received = local_kernel(
        functools.partial(arrange_kernel, capacity),
        jax.ShapeDtypeStruct((feature_width, slots), BF),
        4 * slots * slots * LANES,
        8 * slots * LANES,
    )(received.reshape(-1, LANES))
    sent_half = gather_columns(received)

    dense_saved, expert_saved, dense_down, expert_down = after(
        (dense_saved, expert_saved, dense_down, expert_down), received
    )
    gate_dense, up_dense, sigmoid_dense, dense_units = swiglu_parts(dense_saved[0].T, dense_saved[1].T)
    gate_expert, up_expert, sigmoid_expert, expert_units = swiglu_parts(
        expert_saved[0, 0].T, expert_saved[0, 1].T
    )
    units_other = swap(jnp.concatenate([dense_units, expert_units], axis=1))
    dense_units_other, expert_units_other = units_other[:, :tokens], units_other[:, tokens:]
    weights = jax.ShapeDtypeStruct((2, hidden_count, model_width // 2), BF)
    mine, theirs = local_kernel(
        functools.partial(split_kernel, runs), [weights, weights], 0, 8 * hidden_count * model_width, 1, 2
    )(half_index, dense_down, expert_down[0])
    theirs = swap(theirs)

    first = half == 0
    units = (jnp.where(first, dense_units, dense_units_other), jnp.where(first, dense_units_other, dense_units))
    terms = scatter_terms(grad_half, units)
    came = lax.all_to_all(terms, EXPERT, split_axis=0, concat_axis=0, tiled=True)
    dense_share = scatter_total(came, model_width // expert_count, hidden_count)
    grad_half = after(grad_half, terms)
    cot_other = jnp.einsum("hf,fr->hr", theirs[0], grad_half, preferred_element_type=F32)
    cot_own = jnp.einsum("hf,fr->hr", mine[0], grad_half, preferred_element_type=F32)
    dense_cot = cot_own + swap(cot_other.astype(BF)).astype(F32)

    sent_half = after(sent_half, came)
    grad_other = jnp.einsum("hr,fr->hf", expert_units_other, sent_half, preferred_element_type=F32)
    grad_other = grad_other.astype(BF)
    sent_half = after(sent_half, grad_other)
    grad_other = swap(grad_other)
    cot_other = jnp.einsum("hf,fr->hr", theirs[1], sent_half, preferred_element_type=F32)
    cot_other = cot_other.astype(BF)
    sent_half = after(sent_half, cot_other)
    cot_other = swap(cot_other)
    grad_own = jnp.einsum("hr,fr->hf", expert_units, sent_half, preferred_element_type=F32).astype(BF)
    cot_own = jnp.einsum("hf,fr->hr", mine[1], sent_half, preferred_element_type=F32)
    expert_cot = cot_own + cot_other.astype(F32)
    expert_down_grad = local_kernel(
        functools.partial(join_kernel, runs),
        jax.ShapeDtypeStruct((hidden_count, model_width), BF),
        0,
        4 * hidden_count * model_width,
        1,
        2,
    )(half_index, grad_own, grad_other)[None]

    expert_pre_grad = pre_cotangents(expert_cot, gate_expert, up_expert, sigmoid_expert)
    expert_pre_grad = expert_pre_grad.transpose(0, 2, 1)[None]
    dense_pre_grad = pre_cotangents(dense_cot, gate_dense, up_dense, sigmoid_dense).transpose(0, 2, 1)
    dense_down_grad = dense_share.T
    return (expert_pre_grad, expert_down_grad, dense_pre_grad, dense_down_grad)


def solution(mesh):
    experts, tensors, pairs = mesh.devices.shape
    chips = min(8, experts // 2)
    fine = Mesh(
        mesh.devices.reshape(experts // (2 * chips), chips, 2, tensors, pairs),
        EXPERT + SHARE,
    )
    return jax.shard_map(
        body,
        mesh=fine,
        in_specs=(
            P(EXPERT, SHARE),
            P(EXPERT, None),
            P(EXPERT, None),
            P(EXPERT, SHARE, None),
            P(EXPERT, None, None, SHARE),
            P(SHARE, None),
            P(None, EXPERT, SHARE),
        ),
        out_specs=(
            P(EXPERT, None, None, SHARE),
            P(EXPERT, SHARE, None),
            P(None, EXPERT, SHARE),
            P(SHARE, EXPERT),
        ),
        check_vma=False,
    )
```

time: 163 us -> 194 us (1.19)
  blocking collectives: 38.2 us -> 64.9 us
  Pallas kernels: 0 us -> 7.7 us
  starting transfers between devices: 22.7 us -> 30.1 us
  local copies, waits for them, and re-layouts: 10.3 us -> 5.22 us
  matrix products: 12.6 us -> 8.11 us
  other arithmetic: 7.06 us -> 2.81 us
  waiting for transfers between devices: 57.6 us -> 59.7 us
    ppermute x2 -> x6, waiting for transfers between devices: 11.2 us -> 59.7 us  [the longest x5 56.7 us: swap(): return lax.ppermute(values, 'zl', [(0, 1), (1, 0)])]
    all_to_all x1, waiting for transfers between devices: 29.4 us -> 0.01 us  [body(): lax.all_to_all(terms, EXPERT, split_axis=0, concat_axis=0, tiled=True)]
    all_gather x0 -> x1, blocking collectives: none -> 26 us  [gather_columns(): whole = lax.all_gather(rows, 'y', axis=0, tiled=False)]
    all_gather x2 -> x1, waiting for transfers between devices: 17 us -> 0.01 us  [gather_columns(): whole = lax.all_gather(rows, 'y', axis=0, tiled=False)]
    ppermute x2 -> x6, starting transfers between devices: 8.75 us -> 17.9 us  [the longest x5 14.9 us: swap(): return lax.ppermute(values, 'zl', [(0, 1), (1, 0)])]
    pallas_call x0 -> x6, Pallas kernels: none -> 7.7 us  [the longest x1 1.77 us: scatter_terms(): local_kernel(functools.partial(terms_kernel, runs), jax.ShapeDtypeStruct(...]
    dot_general x5 -> x6, matrix products: 12.6 us -> 8.11 us  [the longest x1 2.99 us: body(): jnp.einsum('hr,fr->hf', expert_units_other, sent_half, preferred_element_...]
    unnamed x19 -> x30, local copies, waits for them, and re-layouts: 0.86 us -> 5.22 us
  transfers between devices with their start and end apart: 5 -> 8, of which waited for: 4 -> 4; matrix products, arithmetic and copies ran while one was open for 13% -> 4% of each run, Pallas kernels for 0% -> 2%
where the time goes in v2:
time: 194 us; the launch traced here: 193 us
  blocking collectives  64.9 us (33%)
  waiting for transfers between devices  59.7 us (31%)
  starting transfers between devices  30.1 us (16%)
  between operations  14.3 us (7%)
  matrix products  8.11 us (4%)
  Pallas kernels  7.7 us (4%)
  local copies, waits for them, and re-layouts  5.22 us (3%)
  other arithmetic  2.81 us (1%)
    ppermute x5, waiting for transfers between devices, swap(): return lax.ppermute(values, 'zl', [(0, 1), (1, 0)])  56.7 us
    all_to_all x1, blocking collectives, body(): lax.all_to_all(outgoing, EXPERT, split_axis=0, concat_axis=0, tiled=True)  38.9 us
    all_gather x1, blocking collectives, gather_columns(): whole = lax.all_gather(rows, 'y', axis=0, tiled=False)  26 us
    ppermute x5, starting transfers between devices, swap(): return lax.ppermute(values, 'zl', [(0, 1), (1, 0)])  14.9 us
    all_to_all x1, starting transfers between devices, body(): lax.all_to_all(terms, EXPERT, split_axis=0, concat_axis=0, tiled=True)  12.1 us
    unnamed x30, local copies, waits for them, and re-layouts  5.22 us
  transfers between devices with their start and end apart: 8, of which 4 were waited for; matrix products, arithmetic and copies ran while one was open for 4% of the time, Pallas kernels for 2%

profile of v2, /device:TPU:1, one launch (start us, length us, event | category | flops | bytes accessed | tf_op | source)
XLA Modules:
  0.0 192.9 jit_solution(14720652518033008167)
XLA Ops:
  7.2 0.9 copy-done.4
  8.1 0.7 copy-done.6
  8.8 0.7 copy-done.7
  9.5 1.1 shard_map.102
  10.6 38.9 %all_to_all.10 = bf16[64,24,128]{2,1,0:T(8,128)(2,1)S(1)} all-to-all(bf16[64,24,128]{2,1,0:T(8,128)(2,1)S(1)} %bitcast.187), channel_id=1, replica_groups=mesh['zh'=4,'x'=8,'core'=2,'y'=8,'zl'=2] {'zh','x','core'}, dimensions={0} | all-to-all | bytes 786432 | tf_op jit(solution)/shard_map/all_to_all | solution.py:232
  49.6 1.4 shard_map.103
  51.3 3.4 %collective-permute-start = (bf16[152,1024]{1,0:T(8,128)(2,1)S(1)}, bf16[152,1024]{1,0:T(8,128)(2,1)S(1)}, u32[]{:S(2)}, u32[]{:S(2)}) collective-permute-start(bf16[152,1024]{1,0:T(8,128)(2,1)S(1)} %pad_maximum_fusion), channel_id=1, source_target_pairs={{0,1},{1,0},{2,3},{3,2},{4,5},{5,4},{6,7},{7,6},{8,9},{9,8},{10,11... | collective-permute-start | bytes 933896 | tf_op jit(solution)/shard_map/ppermute | solution.py:140
  54.7 26.0 %all-gather.1.grad_ref = bf16[1792,256]{1,0:T(8,128)(2,1)S(1)} all-gather(bf16[224,256]{1,0:T(8,128)(2,1)S(1)} %bitcast.189), channel_id=3, replica_groups=mesh['zh'=4,'x'=8,'core'=2,'y'=8,'zl'=2] {'y'}, dimensions={0}, use_global_device_ids=true | all-gather | bytes 1032192 | tf_op jit(solution)/shard_map/all_gather | solution.py:144
  80.8 0.6 copy-done.13
  81.5 1.8 shard_map.105
  83.3 12.1 %all-to-all-start.1 = ((bf16[64,72,128]{2,1,0:T(8,128)(2,1)}), bf16[64,72,128]{2,1,0:T(8,128)(2,1)S(1)}, u32[]{:S(2)}, u32[]{:S(2)}) async-start(bf16[64,72,128]{2,1,0:T(8,128)(2,1)} %shard_map.105), calls=%async_computation.1 | async-start | bytes 2359296 | tf_op jit(solution)/shard_map/all_to_all | solution.py:259
  95.4 1.2 copy-done.1
  96.6 1.7 shard_map.104
  98.3 1.0 copy-done.2
  99.4 2.0 %collective-permute-start.1 = (bf16[2,152,1792]{2,1,0:T(8,128)(2,1)}, bf16[2,152,1792]{2,1,0:T(8,128)(2,1)}, u32[]{:S(2)}, u32[]{:S(2)}) collective-permute-start(bf16[2,152,1792]{2,1,0:T(8,128)(2,1)} %get-tuple-element.21), channel_id=1, source_target_pairs={{0,1},{1,0},{2,3},{3,2},{4,5},{5,4},{6,7},{7,6},{8,9},{9,8},{10,11... | collective-permute-start | bytes 3268616 | tf_op jit(solution)/shard_map/ppermute | solution.py:140
  101.4 44.8 %collective-permute-done.1 = bf16[2,152,1792]{2,1,0:T(8,128)(2,1)} collective-permute-done((bf16[2,152,1792]{2,1,0:T(8,128)(2,1)}, bf16[2,152,1792]{2,1,0:T(8,128)(2,1)}, u32[]{:S(2)}, u32[]{:S(2)}) %collective-permute-start.1) | collective-permute-done | bytes 1089568 | tf_op jit(solution)/shard_map/ppermute | solution.py:140
  146.2 1.4 convolution_convert_fusion.3
  147.6 4.2 %collective-permute-start.4 = (bf16[152,256]{1,0:T(8,128)(2,1)S(1)}, bf16[152,256]{1,0:T(8,128)(2,1)S(1)}, u32[]{:S(2)}, u32[]{:S(2)}) collective-permute-start(bf16[152,256]{1,0:T(8,128)(2,1)S(1)} %convolution_convert_fusion.3), channel_id=1, source_target_pairs={{0,1},{1,0},{2,3},{3,2},{4,5},{5,4},{6,7},{7,6},{8,9},{9,8},{10,11... | collective-permute-start | bytes 233480 | tf_op jit(solution)/shard_map/ppermute | solution.py:140
  152.2 2.0 %collective-permute-done.4 = bf16[152,256]{1,0:T(8,128)(2,1)S(1)} collective-permute-done((bf16[152,256]{1,0:T(8,128)(2,1)S(1)}, bf16[152,256]{1,0:T(8,128)(2,1)S(1)}, u32[]{:S(2)}, u32[]{:S(2)}) %collective-permute-start.4) | collective-permute-done | bytes 77856 | tf_op jit(solution)/shard_map/ppermute | solution.py:140
  154.5 3.0 %collective-permute-start.5 = (bf16[56,152]{1,0:T(8,128)(2,1)S(1)}, bf16[56,152]{1,0:T(8,128)(2,1)S(1)}, u32[]{:S(2)}, u32[]{:S(2)}) collective-permute-start(bf16[56,152]{1,0:T(8,128)(2,1)S(1)} %shard_map.107), channel_id=1, source_target_pairs={{0,65},{1,64},{32,97},{33,96},{64,1},{65,0},{96,33},{97,32},{128,1... | collective-permute-start | bytes 51080 | tf_op jit(solution)/shard_map/ppermute | solution.py:207
  157.5 0.7 maximum_bitcast_fusion.1
  158.2 3.0 %collective-permute-done.5 = bf16[56,152]{1,0:T(8,128)(2,1)S(1)} collective-permute-done((bf16[56,152]{1,0:T(8,128)(2,1)S(1)}, bf16[56,152]{1,0:T(8,128)(2,1)S(1)}, u32[]{:S(2)}, u32[]{:S(2)}) %collective-permute-start.5) | collective-permute-done | bytes 17056 | tf_op jit(solution)/shard_map/ppermute | solution.py:207
  161.2 0.6 select_bitcast_fusion
  161.9 3.0 %convolution_convert_fusion.1 = bf16[152,1792]{1,0:T(8,128)(2,1)S(1)} fusion(bf16[1792,768]{1,0:T(8,128)(2,1)} %all-gather.4.cloned.1.call-done, bf16[152,1024]{1,0:T(8,128)(2,1)S(1)} %copy-done.14), kind=kOutput, calls=%fused_computation.1 | convolution fusion | flops 418654208 | bytes 3530752 | tf_op jit(solution)/shard_map/hr,fr->hf/dot_general | solution.py:267
  164.9 2.8 %collective-permute-start.3 = (bf16[152,1792]{1,0:T(8,128)(2,1)S(1)}, bf16[152,1792]{1,0:T(8,128)(2,1)S(1)}, u32[]{:S(2)}, u32[]{:S(2)}) collective-permute-start(bf16[152,1792]{1,0:T(8,128)(2,1)S(1)} %convolution_convert_fusion.1), channel_id=1, source_target_pairs={{0,1},{1,0},{2,3},{3,2},{4,5},{5,4},{6,7},{7,6},{8,9},{9,8},{10,11... | collective-permute-start | bytes 1634312 | tf_op jit(solution)/shard_map/ppermute | solution.py:140
  167.6 1.7 convolution_convert_fusion.2
  169.3 2.5 %collective-permute-start.2 = (bf16[152,768]{1,0:T(8,128)(2,1)S(1)}, bf16[152,768]{1,0:T(8,128)(2,1)S(1)}, u32[]{:S(2)}, u32[]{:S(2)}) collective-permute-start(bf16[152,768]{1,0:T(8,128)(2,1)S(1)} %convolution_convert_fusion.2), channel_id=1, source_target_pairs={{0,1},{1,0},{2,3},{3,2},{4,5},{5,4},{6,7},{7,6},{8,9},{9,8},{10,11... | collective-permute-start | bytes 700424 | tf_op jit(solution)/shard_map/ppermute | solution.py:140
  171.9 0.6 fusion.2
  172.5 1.1 convolution_convert_fusion.own_ref
  173.6 10.0 %collective-permute-done.2 = bf16[152,768]{1,0:T(8,128)(2,1)S(1)} collective-permute-done((bf16[152,768]{1,0:T(8,128)(2,1)S(1)}, bf16[152,768]{1,0:T(8,128)(2,1)S(1)}, u32[]{:S(2)}, u32[]{:S(2)}) %collective-permute-start.2) | collective-permute-done | bytes 233504 | tf_op jit(solution)/shard_map/ppermute | solution.py:140
  183.8 0.8 maximum_bitcast_fusion
  184.7 1.4 shard_map.106
  (38 shorter events, 1.4 us)
Async XLA Ops:
  7.2 154.7 %all-gather.4.cloned.1.call-start = ((), (), s32[]{:S(2)}) async-start(), calls=%async_computation.2 | async-start | bytes 3096576 | tf_op jit(solution)/shard_map/all_gather | solution.py:144
  7.2 0.9 copy-start.4
  8.1 0.7 copy-start.6
  8.8 0.7 copy-start.7
  10.6 40.4 %copy-start.11 = (bf16[2,256,152]{1,2,0:T(8,128)(2,1)S(1)}, bf16[2,256,152]{1,2,0:T(8,128)(2,1)}, u32[]{:S(2)}) copy-start(bf16[2,256,152]{1,2,0:T(8,128)(2,1)} %param.13) | copy-start | bytes 466948
  10.6 40.5 %copy-start.9 = (bf16[1,2,768,152]{2,3,1,0:T(8,128)(2,1)S(1)}, bf16[1,2,768,152]{2,3,1,0:T(8,128)(2,1)}, u32[]{:S(2)}) copy-start(bf16[1,2,768,152]{2,3,1,0:T(8,128)(2,1)} %param.11) | copy-start | bytes 1400836
  51.0 3.7 %copy-start.5 = (bf16[256,224]{0,1:T(8,128)(2,1)S(1)}, bf16[256,224]{0,1:T(8,128)(2,1)}, u32[]{:S(2)}) copy-start(bf16[256,224]{0,1:T(8,128)(2,1)} %param.7) | copy-start | bytes 344068
  51.3 29.4 %collective-permute-start = (bf16[152,1024]{1,0:T(8,128)(2,1)S(1)}, bf16[152,1024]{1,0:T(8,128)(2,1)S(1)}, u32[]{:S(2)}, u32[]{:S(2)}) collective-permute-start(bf16[152,1024]{1,0:T(8,128)(2,1)S(1)} %pad_maximum_fusion), channel_id=1, source_target_pairs={{0,1},{1,0},{2,3},{3,2},{4,5},{5,4},{6,7},{7,6},{8,9},{9,8},{10,11... | collective-permute-start | bytes 933896 | tf_op jit(solution)/shard_map/ppermute | solution.py:140
  80.7 0.7 copy-start.13
  83.2 12.1 %copy-start = (bf16[152,3584]{1,0:T(8,128)(2,1)S(1)}, bf16[152,3584]{1,0:T(8,128)(2,1)}, u32[]{:S(2)}) copy-start(bf16[152,3584]{1,0:T(8,128)(2,1)} %dense_ref) | copy-start | bytes 3268612
  83.3 71.1 %all-to-all-start.1 = ((bf16[64,72,128]{2,1,0:T(8,128)(2,1)}), bf16[64,72,128]{2,1,0:T(8,128)(2,1)S(1)}, u32[]{:S(2)}, u32[]{:S(2)}) async-start(bf16[64,72,128]{2,1,0:T(8,128)(2,1)} %shard_map.105), calls=%async_computation.1 | async-start | bytes 2359296 | tf_op jit(solution)/shard_map/all_to_all | solution.py:259
  95.3 1.2 copy-start.1
  98.3 1.0 copy-start.2
  99.4 52.5 %copy-start.3 = (bf16[2,152,1792]{2,1,0:T(8,128)(2,1)S(1)}, bf16[2,152,1792]{2,1,0:T(8,128)(2,1)}, u32[]{:S(2)}) copy-start(bf16[2,152,1792]{2,1,0:T(8,128)(2,1)} %copy-done.2) | copy-start | bytes 3268612
  99.4 46.9 %collective-permute-start.1 = (bf16[2,152,1792]{2,1,0:T(8,128)(2,1)}, bf16[2,152,1792]{2,1,0:T(8,128)(2,1)}, u32[]{:S(2)}, u32[]{:S(2)}) collective-permute-start(bf16[2,152,1792]{2,1,0:T(8,128)(2,1)} %get-tuple-element.21), channel_id=1, source_target_pairs={{0,1},{1,0},{2,3},{3,2},{4,5},{5,4},{6,7},{7,6},{8,9},{9,8},{10,11... | collective-permute-start | bytes 3268616 | tf_op jit(solution)/shard_map/ppermute | solution.py:140
  147.6 6.6 %copy-start.12 = (bf16[2,256,152]{1,2,0:T(8,128)(2,1)S(1)}, bf16[2,256,152]{1,2,0:T(8,128)(2,1)}, u32[]{:S(2)}) copy-start(bf16[2,256,152]{1,2,0:T(8,128)(2,1)} %param.13) | copy-start | bytes 466948
  147.6 6.6 %collective-permute-start.4 = (bf16[152,256]{1,0:T(8,128)(2,1)S(1)}, bf16[152,256]{1,0:T(8,128)(2,1)S(1)}, u32[]{:S(2)}, u32[]{:S(2)}) collective-permute-start(bf16[152,256]{1,0:T(8,128)(2,1)S(1)} %convolution_convert_fusion.3), channel_id=1, source_target_pairs={{0,1},{1,0},{2,3},{3,2},{4,5},{5,4},{6,7},{7,6},{8,9},{9,8},{10,11... | collective-permute-start | bytes 233480 | tf_op jit(solution)/shard_map/ppermute | solution.py:140
  152.2 9.6 %copy-start.14 = (bf16[152,1024]{1,0:T(8,128)(2,1)S(1)}, bf16[152,1024]{1,0:T(8,128)(2,1)}, u32[]{:S(2)}) copy-start(bf16[152,1024]{1,0:T(8,128)(2,1)} %copy-done.13) | copy-start | bytes 933892
  154.5 6.7 %collective-permute-start.5 = (bf16[56,152]{1,0:T(8,128)(2,1)S(1)}, bf16[56,152]{1,0:T(8,128)(2,1)S(1)}, u32[]{:S(2)}, u32[]{:S(2)}) collective-permute-start(bf16[56,152]{1,0:T(8,128)(2,1)S(1)} %shard_map.107), channel_id=1, source_target_pairs={{0,65},{1,64},{32,97},{33,96},{64,1},{65,0},{96,33},{97,32},{128,1... | collective-permute-start | bytes 51080 | tf_op jit(solution)/shard_map/ppermute | solution.py:207
  161.9 5.8 %copy-start.8 = (bf16[1792,768]{1,0:T(8,128)(2,1)S(1)}, bf16[1792,768]{1,0:T(8,128)(2,1)}, u32[]{:S(2)}) copy-start(bf16[1792,768]{1,0:T(8,128)(2,1)} %all-gather.4.cloned.1.call-done) | copy-start | bytes 8257540
  164.9 19.8 %collective-permute-start.3 = (bf16[152,1792]{1,0:T(8,128)(2,1)S(1)}, bf16[152,1792]{1,0:T(8,128)(2,1)S(1)}, u32[]{:S(2)}, u32[]{:S(2)}) collective-permute-start(bf16[152,1792]{1,0:T(8,128)(2,1)S(1)} %convolution_convert_fusion.1), channel_id=1, source_target_pairs={{0,1},{1,0},{2,3},{3,2},{4,5},{5,4},{6,7},{7,6},{8,9},{9,8},{10,11... | collective-permute-start | bytes 1634312 | tf_op jit(solution)/shard_map/ppermute | solution.py:140
  169.3 14.2 %collective-permute-start.2 = (bf16[152,768]{1,0:T(8,128)(2,1)S(1)}, bf16[152,768]{1,0:T(8,128)(2,1)S(1)}, u32[]{:S(2)}, u32[]{:S(2)}) collective-permute-start(bf16[152,768]{1,0:T(8,128)(2,1)S(1)} %convolution_convert_fusion.2), channel_id=1, source_target_pairs={{0,1},{1,0},{2,3},{3,2},{4,5},{5,4},{6,7},{7,6},{8,9},{9,8},{10,11... | collective-permute-start | bytes 700424 | tf_op jit(solution)/shard_map/ppermute | solution.py:140
  172.5 11.0 %copy-start.10 = (bf16[1,2,768,152]{2,3,1,0:T(8,128)(2,1)S(1)}, bf16[1,2,768,152]{2,3,1,0:T(8,128)(2,1)}, u32[]{:S(2)}) copy-start(bf16[1,2,768,152]{2,3,1,0:T(8,128)(2,1)} %param.11) | copy-start | bytes 1400836
Sparse Core Ops, SparseCore 0:
  51.2 47.9 all-gather.3

commit v3 on v2

--- a/solution.py
+++ b/solution.py
@@ -82,21 +82,21 @@
             ]
 
 
-def split_kernel(runs, half_ref, dense_ref, expert_ref, mine_ref, theirs_ref):
-    width = dense_ref.shape[1] // (2 * runs)
-
-    def columns(ref, half):
+def split_kernel(runs, half_ref, weights_ref, mine_ref, theirs_ref):
+    width = weights_ref.shape[1] // (2 * runs)
+
+    def columns(half):
         return jnp.concatenate(
-            [ref[:, (2 * run + half) * width : (2 * run + half + 1) * width] for run in range(runs)], axis=1
+            [weights_ref[:, (2 * run + half) * width : (2 * run + half + 1) * width] for run in range(runs)],
+            axis=1,
         )
 
     for half in range(2):
 
         @pl.when(half_ref[0] == half)
         def _():
-            for index, ref in enumerate((dense_ref, expert_ref)):
-                mine_ref[index] = columns(ref, half)
-                theirs_ref[index] = columns(ref, 1 - half)
+            mine_ref[...] = columns(half)
+            theirs_ref[...] = columns(1 - half)
 
 
 def join_kernel(runs, half_ref, own_ref, other_ref, out_ref):
@@ -229,51 +229,61 @@
         arrays=3,
     )(routes.T, probs.T, grad_rows)
     outgoing = outgoing.reshape(expert_count, 2 * capacity, LANES)
+    dense_saved, expert_saved, dense_down, expert_down = after(
+        (dense_saved, expert_saved, dense_down, expert_down), outgoing
+    )
     received = lax.all_to_all(outgoing, EXPERT, split_axis=0, concat_axis=0, tiled=True)
     received = local_kernel(
         functools.partial(arrange_kernel, capacity),
         jax.ShapeDtypeStruct((feature_width, slots), BF),
         4 * slots * slots * LANES,
         8 * slots * LANES,
-    )(received.reshape(-1, LANES))
+    )(after(received.reshape(-1, LANES), grad_half))
     sent_half = gather_columns(received)
 
-    dense_saved, expert_saved, dense_down, expert_down = after(
-        (dense_saved, expert_saved, dense_down, expert_down), received
-    )
     gate_dense, up_dense, sigmoid_dense, dense_units = swiglu_parts(dense_saved[0].T, dense_saved[1].T)
     gate_expert, up_expert, sigmoid_expert, expert_units = swiglu_parts(
         expert_saved[0, 0].T, expert_saved[0, 1].T
     )
     units_other = swap(jnp.concatenate([dense_units, expert_units], axis=1))
     dense_units_other, expert_units_other = units_other[:, :tokens], units_other[:, tokens:]
-    weights = jax.ShapeDtypeStruct((2, hidden_count, model_width // 2), BF)
-    mine, theirs = local_kernel(
-        functools.partial(split_kernel, runs), [weights, weights], 0, 8 * hidden_count * model_width, 1, 2
-    )(half_index, dense_down, expert_down[0])
-    theirs = swap(theirs)
+    split = local_kernel(
+        functools.partial(split_kernel, runs),
+        [jax.ShapeDtypeStruct((hidden_count, model_width // 2), BF)] * 2,
+        0,
+        4 * hidden_count * model_width,
+        1,
+        1,
+    )
+    dense_mine, dense_theirs = split(half_index, dense_down)
+    dense_theirs = swap(dense_theirs)
+    expert_mine, expert_theirs = split(half_index, after(expert_down[0], dense_mine))
 
     first = half == 0
     units = (jnp.where(first, dense_units, dense_units_other), jnp.where(first, dense_units_other, dense_units))
+    units = after(units, (dense_theirs, expert_theirs))
     terms = scatter_terms(grad_half, units)
+    expert_theirs = swap(after(expert_theirs, terms))
     came = lax.all_to_all(terms, EXPERT, split_axis=0, concat_axis=0, tiled=True)
-    dense_share = scatter_total(came, model_width // expert_count, hidden_count)
     grad_half = after(grad_half, terms)
-    cot_other = jnp.einsum("hf,fr->hr", theirs[0], grad_half, preferred_element_type=F32)
-    cot_own = jnp.einsum("hf,fr->hr", mine[0], grad_half, preferred_element_type=F32)
+    cot_other = jnp.einsum("hf,fr->hr", dense_theirs, grad_half, preferred_element_type=F32)
+    cot_own = jnp.einsum("hf,fr->hr", dense_mine, grad_half, preferred_element_type=F32)
     dense_cot = cot_own + swap(cot_other.astype(BF)).astype(F32)
 
-    sent_half = after(sent_half, came)
-    grad_other = jnp.einsum("hr,fr->hf", expert_units_other, sent_half, preferred_element_type=F32)
-    grad_other = grad_other.astype(BF)
-    sent_half = after(sent_half, grad_other)
-    grad_other = swap(grad_other)
-    cot_other = jnp.einsum("hf,fr->hr", theirs[1], sent_half, preferred_element_type=F32)
+    dense_pre_grad = pre_cotangents(dense_cot, gate_dense, up_dense, sigmoid_dense).transpose(0, 2, 1)
+    sent_half = after(sent_half, dense_pre_grad)
+
+    cot_other = jnp.einsum("hf,fr->hr", expert_theirs, sent_half, preferred_element_type=F32)
     cot_other = cot_other.astype(BF)
     sent_half = after(sent_half, cot_other)
     cot_other = swap(cot_other)
+    grad_other = jnp.einsum("hr,fr->hf", expert_units_other, sent_half, preferred_element_type=F32)
+    grad_other = grad_other.astype(BF)
+    sent_half, came = after((sent_half, came), grad_other)
+    grad_other = swap(grad_other)
+    dense_share = scatter_total(came, model_width // expert_count, hidden_count)
     grad_own = jnp.einsum("hr,fr->hf", expert_units, sent_half, preferred_element_type=F32).astype(BF)
-    cot_own = jnp.einsum("hf,fr->hr", mine[1], sent_half, preferred_element_type=F32)
+    cot_own = jnp.einsum("hf,fr->hr", expert_mine, sent_half, preferred_element_type=F32)
     expert_cot = cot_own + cot_other.astype(F32)
     expert_down_grad = local_kernel(
         functools.partial(join_kernel, runs),
@@ -286,7 +296,6 @@
 
     expert_pre_grad = pre_cotangents(expert_cot, gate_expert, up_expert, sigmoid_expert)
     expert_pre_grad = expert_pre_grad.transpose(0, 2, 1)[None]
-    dense_pre_grad = pre_cotangents(dense_cot, gate_dense, up_dense, sigmoid_dense).transpose(0, 2, 1)
     dense_down_grad = dense_share.T
     return (expert_pre_grad, expert_down_grad, dense_pre_grad, dense_down_grad)
 

time: 194 us -> 177 us (0.912)
  blocking collectives: 64.9 us -> 24.8 us
  starting transfers between devices: 30.1 us -> 61.8 us
  waiting for transfers between devices: 59.7 us -> 45.5 us
  other arithmetic: 2.81 us -> 7.4 us
    all_to_all x1 -> x0, blocking collectives: 38.9 us -> none  [body(): lax.all_to_all(outgoing, EXPERT, split_axis=0, concat_axis=0, tiled=True)]
    all_to_all x0 -> x1, starting transfers between devices: none -> 22.7 us  [body(): lax.all_to_all(outgoing, EXPERT, split_axis=0, concat_axis=0, tiled=True)]
    ppermute x5 -> x6, waiting for transfers between devices: 56.7 us -> 45.5 us  [swap(): return lax.ppermute(values, 'zl', [(0, 1), (1, 0)])]
    all_to_all x1, starting transfers between devices: 12.1 us -> 17.3 us  [body(): lax.all_to_all(terms, EXPERT, split_axis=0, concat_axis=0, tiled=True)]
    ppermute x1, waiting for transfers between devices: 3.02 us -> 0.01 us  [scatter_total(): other = lax.ppermute(mine, ('x', 'zl'), route)]
    ppermute x5 -> x6, starting transfers between devices: 14.9 us -> 17.5 us  [swap(): return lax.ppermute(values, 'zl', [(0, 1), (1, 0)])]
    convert_element_type x2, other arithmetic: 0.21 us -> 2.19 us  [swiglu_parts(): hidden = (gate_pre * sigmoid_gate * up_pre).astype(BF)]
  transfers between devices with their start and end apart: 8 -> 10, of which waited for: 4 -> 3; matrix products, arithmetic and copies ran while one was open for 4% -> 10% of each run, Pallas kernels for 2% -> 2%
where the time goes in v3:
time: 177 us; the launch traced here: 176 us
  starting transfers between devices  61.8 us (35%)
  waiting for transfers between devices  45.5 us (26%)
  blocking collectives  24.8 us (14%)
  between operations  14.4 us (8%)
  matrix products  9.86 us (6%)
  Pallas kernels  7.64 us (4%)
  other arithmetic  7.4 us (4%)
  local copies, waits for them, and re-layouts  4.73 us (3%)
    ppermute x6, waiting for transfers between devices, swap(): return lax.ppermute(values, 'zl', [(0, 1), (1, 0)])  45.5 us
    all_gather x1, blocking collectives, gather_columns(): whole = lax.all_gather(rows, 'y', axis=0, tiled=False)  24.8 us
    all_to_all x1, starting transfers between devices, body(): lax.all_to_all(outgoing, EXPERT, split_axis=0, concat_axis=0, tiled=True)  22.7 us
    ppermute x6, starting transfers between devices, swap(): return lax.ppermute(values, 'zl', [(0, 1), (1, 0)])  17.5 us
    all_to_all x1, starting transfers between devices, body(): lax.all_to_all(terms, EXPERT, split_axis=0, concat_axis=0, tiled=True)  17.3 us
    unnamed x30, local copies, waits for them, and re-layouts  4.73 us
    ppermute x1, starting transfers between devices, scatter_total(): other = lax.ppermute(mine, ('x', 'zl'), route)  4.22 us
  transfers between devices with their start and end apart: 10, of which 3 were waited for; matrix products, arithmetic and copies ran while one was open for 10% of the time, Pallas kernels for 2%

profile of v3, /device:TPU:1, one launch (start us, length us, event | category | flops | bytes accessed | tf_op | source)
XLA Modules:
  0.0 176.1 jit_solution(10238579333559954878)
XLA Ops:
  7.2 1.0 copy-done.7
  9.5 1.9 %shard_map.102 = bf16[1536,128]{1,0:T(8,128)(2,1)} custom-call(s32[2,256]{1,0:T(2,128)S(1)} %bitcast.181, f32[2,256]{1,0:T(2,128)S(1)} %bitcast.182, bf16[224,256]{1,0:T(8,128)(2,1)S(1)} %bitcast.180), custom_call_target="tpu_custom_call" | custom-call | flops 176160768 | bytes 393216 | tf_op jit(solution)/shard_map/pallas_call | solution.py:224
  11.4 22.7 %all-to-all-start = ((bf16[64,24,128]{2,1,0:T(8,128)(2,1)}), bf16[64,24,128]{2,1,0:T(8,128)(2,1)S(1)}, u32[]{:S(2)}, u32[]{:S(2)}) async-start(bf16[64,24,128]{2,1,0:T(8,128)(2,1)} %bitcast.4), calls=%async_computation | async-start | bytes 786432 | tf_op jit(solution)/shard_map/all_to_all | solution.py:235
  34.2 24.8 %all-gather.grad_ref = bf16[1792,256]{1,0:T(8,128)(2,1)S(1)} all-gather(bf16[224,256]{1,0:T(8,128)(2,1)} %bitcast.179), channel_id=2, replica_groups=mesh['zh'=4,'x'=8,'core'=2,'y'=8,'zl'=2] {'y'}, dimensions={0}, use_global_device_ids=true | all-gather | bytes 1032192 | tf_op jit(solution)/shard_map/all_gather | solution.py:144
  59.0 0.7 shard_map.105
  59.8 0.7 copy-done.6
  60.5 1.2 shard_map.103
  61.7 0.8 copy-done.2
  62.6 4.0 %collective-permute-start.1 = (bf16[152,1792]{1,0:T(8,128)(2,1)}, bf16[152,1792]{1,0:T(8,128)(2,1)}, u32[]{:S(2)}, u32[]{:S(2)}) collective-permute-start(bf16[152,1792]{1,0:T(8,128)(2,1)} %get-tuple-element.30), channel_id=1, source_target_pairs={{0,1},{1,0},{2,3},{3,2},{4,5},{5,4},{6,7},{7,6},{8,9},{9,8},{10,11... | collective-permute-start | bytes 1634312 | tf_op jit(solution)/shard_map/ppermute | solution.py:140
  66.6 1.0 fusion.21
  67.5 1.2 fusion.2
  68.8 0.7 pad_maximum_fusion
  69.5 1.9 %collective-permute-start = (bf16[152,1024]{1,0:T(8,128)(2,1)}, bf16[152,1024]{1,0:T(8,128)(2,1)}, u32[]{:S(2)}, u32[]{:S(2)}) collective-permute-start(bf16[152,1024]{1,0:T(8,128)(2,1)} %pad_maximum_fusion), channel_id=1, source_target_pairs={{0,1},{1,0},{2,3},{3,2},{4,5},{5,4},{6,7},{7,6},{8,9},{9,8},{10,11... | collective-permute-start | bytes 933896 | tf_op jit(solution)/shard_map/ppermute | solution.py:140
  71.9 0.8 copy-done.8
  72.7 8.8 %collective-permute-done = bf16[152,1024]{1,0:T(8,128)(2,1)} collective-permute-done((bf16[152,1024]{1,0:T(8,128)(2,1)}, bf16[152,1024]{1,0:T(8,128)(2,1)}, u32[]{:S(2)}, u32[]{:S(2)}) %collective-permute-start) | collective-permute-done | bytes 311328 | tf_op jit(solution)/shard_map/ppermute | solution.py:140
  81.5 1.0 broadcast_select_fusion
  82.5 1.8 %shard_map.106 = bf16[64,72,128]{2,1,0:T(8,128)(2,1)} custom-call(bf16[1792,256]{1,0:T(8,128)(2,1)S(1)} %all-gather.grad_ref, bf16[152,256]{1,0:T(8,128)(2,1)S(1)} %get-tuple-element.32.first_ref, bf16[152,256]{1,0:T(8,128)(2,1)S(1)} %get-tuple-element.33.second_ref), custom_call_target="tpu_custom_call" | custom-call | flops 278921216 | bytes 1835008 | tf_op jit(solution)/shard_map/pallas_call | solution.py:191
  84.3 17.3 %all-to-all-start.1 = ((bf16[64,72,128]{2,1,0:T(8,128)(2,1)}), bf16[64,72,128]{2,1,0:T(8,128)(2,1)S(1)}, u32[]{:S(2)}, u32[]{:S(2)}) async-start(bf16[64,72,128]{2,1,0:T(8,128)(2,1)} %shard_map.106), calls=%async_computation.1 | async-start | bytes 2359296 | tf_op jit(solution)/shard_map/all_to_all | solution.py:267
  101.7 3.5 %collective-permute-start.3 = (bf16[152,1792]{1,0:T(8,128)(2,1)}, bf16[152,1792]{1,0:T(8,128)(2,1)}, u32[]{:S(2)}, u32[]{:S(2)}) collective-permute-start(bf16[152,1792]{1,0:T(8,128)(2,1)} %copy-done.8), channel_id=1, source_target_pairs={{0,1},{1,0},{2,3},{3,2},{4,5},{5,4},{6,7},{7,6},{8,9},{9,8},{10,11... | collective-permute-start | bytes 1634312 | tf_op jit(solution)/shard_map/ppermute | solution.py:140
  105.2 1.4 convolution_convert_fusion.3
  106.6 1.9 %collective-permute-start.2 = (bf16[152,256]{1,0:T(8,128)(2,1)S(1)}, bf16[152,256]{1,0:T(8,128)(2,1)S(1)}, u32[]{:S(2)}, u32[]{:S(2)}) collective-permute-start(bf16[152,256]{1,0:T(8,128)(2,1)S(1)} %convolution_convert_fusion.3), channel_id=1, source_target_pairs={{0,1},{1,0},{2,3},{3,2},{4,5},{5,4},{6,7},{7,6},{8,9},{9,8},{10,11... | collective-permute-start | bytes 233480 | tf_op jit(solution)/shard_map/ppermute | solution.py:140
  108.8 33.7 %collective-permute-done.2 = bf16[152,256]{1,0:T(8,128)(2,1)S(1)} collective-permute-done((bf16[152,256]{1,0:T(8,128)(2,1)S(1)}, bf16[152,256]{1,0:T(8,128)(2,1)S(1)}, u32[]{:S(2)}, u32[]{:S(2)}) %collective-permute-start.2) | collective-permute-done | bytes 77856 | tf_op jit(solution)/shard_map/ppermute | solution.py:140
  143.4 2.7 %convolution_convert_fusion.2 = bf16[152,768]{1,0:T(8,128)(2,1)S(1)} fusion(bf16[152,1792]{1,0:T(8,128)(2,1)} %collective-permute-done.3, bf16[1792,768]{1,0:T(8,128)(2,1)} %all-gather.4.cloned.1.call-done), kind=kOutput, calls=%fused_computation.2 | convolution fusion | flops 418498560 | bytes 3530752 | tf_op jit(solution)/shard_map/hf,fr->hr/dot_general | solution.py:276
  146.1 4.1 %collective-permute-start.4 = (bf16[152,768]{1,0:T(8,128)(2,1)S(1)}, bf16[152,768]{1,0:T(8,128)(2,1)}, u32[]{:S(2)}, u32[]{:S(2)}) collective-permute-start(bf16[152,768]{1,0:T(8,128)(2,1)S(1)} %convolution_convert_fusion.2), channel_id=1, source_target_pairs={{0,1},{1,0},{2,3},{3,2},{4,5},{5,4},{6,7},{7,6},{8,9},{9,8},{10,11... | collective-permute-start | bytes 700424 | tf_op jit(solution)/shard_map/ppermute | solution.py:140
  150.2 2.0 %convolution_convert_fusion.1 = bf16[152,1792]{1,0:T(8,128)(2,1)S(1)} fusion(bf16[1792,768]{1,0:T(8,128)(2,1)S(1)} %copy-done.11, bf16[152,1024]{1,0:T(8,128)(2,1)} %collective-permute-done), kind=kOutput, calls=%fused_computation.1 | convolution fusion | flops 418654208 | bytes 3530752 | tf_op jit(solution)/shard_map/hr,fr->hf/dot_general | solution.py:280
  152.2 2.1 %collective-permute-start.5 = (bf16[152,1792]{1,0:T(8,128)(2,1)S(1)}, bf16[152,1792]{1,0:T(8,128)(2,1)S(1)}, u32[]{:S(2)}, u32[]{:S(2)}) collective-permute-start(bf16[152,1792]{1,0:T(8,128)(2,1)S(1)} %convolution_convert_fusion.1), channel_id=1, source_target_pairs={{0,1},{1,0},{2,3},{3,2},{4,5},{5,4},{6,7},{7,6},{8,9},{9,8},{10,11... | collective-permute-start | bytes 1634312 | tf_op jit(solution)/shard_map/ppermute | solution.py:140
  154.5 4.2 %collective-permute-start.6 = (bf16[56,152]{1,0:T(8,128)(2,1)S(1)}, bf16[56,152]{1,0:T(8,128)(2,1)S(1)}, u32[]{:S(2)}, u32[]{:S(2)}) collective-permute-start(bf16[56,152]{1,0:T(8,128)(2,1)S(1)} %shard_map.108), channel_id=1, source_target_pairs={{0,65},{1,64},{32,97},{33,96},{64,1},{65,0},{96,33},{97,32},{128,1... | collective-permute-start | bytes 51080 | tf_op jit(solution)/shard_map/ppermute | solution.py:207
  158.7 2.8 %convolution_convert_fusion.own_ref = bf16[152,1792]{1,0:T(8,128)(2,1)S(1)} fusion(bf16[152,768]{1,0:T(8,128)(2,1)S(1)} %fusion.2, bf16[1792,768]{1,0:T(8,128)(2,1)} %all-gather.4.cloned.1.call-done), kind=kOutput, calls=%fused_computation | convolution fusion | flops 418654208 | bytes 3530752 | tf_op jit(solution)/shard_map/hr,fr->hf/dot_general | solution.py:285
  162.9 1.2 fusion.18
  164.1 0.8 maximum_bitcast_fusion
  164.9 3.0 %collective-permute-done.5.other_ref = bf16[152,1792]{1,0:T(8,128)(2,1)S(1)} collective-permute-done((bf16[152,1792]{1,0:T(8,128)(2,1)S(1)}, bf16[152,1792]{1,0:T(8,128)(2,1)S(1)}, u32[]{:S(2)}, u32[]{:S(2)}) %collective-permute-start.5) | collective-permute-done | bytes 544800 | tf_op jit(solution)/shard_map/ppermute | solution.py:140
  167.9 1.4 shard_map.107
  (42 shorter events, 4.5 us)
Async XLA Ops:
  7.2 53.3 %copy-start = (bf16[152,3584]{1,0:T(8,128)(2,1)S(1)}, bf16[152,3584]{1,0:T(8,128)(2,1)}, u32[]{:S(2)}) copy-start(bf16[152,3584]{1,0:T(8,128)(2,1)} %weights_ref) | copy-start | bytes 3268612
  7.2 1.0 copy-start.7
  8.2 0.7 copy-start.9
  8.8 0.7 copy-start.10
  11.4 47.6 %all-to-all-start = ((bf16[64,24,128]{2,1,0:T(8,128)(2,1)}), bf16[64,24,128]{2,1,0:T(8,128)(2,1)S(1)}, u32[]{:S(2)}, u32[]{:S(2)}) async-start(bf16[64,24,128]{2,1,0:T(8,128)(2,1)} %bitcast.4), calls=%async_computation | async-start | bytes 786432 | tf_op jit(solution)/shard_map/all_to_all | solution.py:235
  34.2 37.3 %copy-start.1 = (bf16[1,152,3584]{2,1,0:T(8,128)(2,1)S(1)}, bf16[1,152,3584]{2,1,0:T(8,128)(2,1)}, u32[]{:S(2)}) copy-start(bf16[1,152,3584]{2,1,0:T(8,128)(2,1)} %param.10) | copy-start | bytes 3268612
  34.2 109.2 %all-gather.4.cloned.1.call-start = ((), (), s32[]{:S(2)}) async-start(), calls=%async_computation.2 | async-start | bytes 3096576 | tf_op jit(solution)/shard_map/all_gather | solution.py:144
  59.7 0.7 copy-start.6
  61.7 0.8 copy-start.2
  62.6 20.0 %collective-permute-start.1 = (bf16[152,1792]{1,0:T(8,128)(2,1)}, bf16[152,1792]{1,0:T(8,128)(2,1)}, u32[]{:S(2)}, u32[]{:S(2)}) collective-permute-start(bf16[152,1792]{1,0:T(8,128)(2,1)} %get-tuple-element.30), channel_id=1, source_target_pairs={{0,1},{1,0},{2,3},{3,2},{4,5},{5,4},{6,7},{7,6},{8,9},{9,8},{10,11... | collective-permute-start | bytes 1634312 | tf_op jit(solution)/shard_map/ppermute | solution.py:140
  69.5 12.0 %collective-permute-start = (bf16[152,1024]{1,0:T(8,128)(2,1)}, bf16[152,1024]{1,0:T(8,128)(2,1)}, u32[]{:S(2)}, u32[]{:S(2)}) collective-permute-start(bf16[152,1024]{1,0:T(8,128)(2,1)} %pad_maximum_fusion), channel_id=1, source_target_pairs={{0,1},{1,0},{2,3},{3,2},{4,5},{5,4},{6,7},{7,6},{8,9},{9,8},{10,11... | collective-permute-start | bytes 933896 | tf_op jit(solution)/shard_map/ppermute | solution.py:140
  71.9 0.8 copy-start.8
  72.7 11.6 %copy-start.4 = (bf16[152,1792]{1,0:T(8,128)(2,1)}, bf16[152,1792]{1,0:T(8,128)(2,1)S(1)}, u32[]{:S(2)}) copy-start(bf16[152,1792]{1,0:T(8,128)(2,1)S(1)} %get-tuple-element.26) | copy-start | bytes 1634308
  82.5 26.0 %copy-start.3 = (bf16[152,1792]{1,0:T(8,128)(2,1)S(1)}, bf16[152,1792]{1,0:T(8,128)(2,1)}, u32[]{:S(2)}) copy-start(bf16[152,1792]{1,0:T(8,128)(2,1)} %copy-done.2) | copy-start | bytes 1634308
  84.3 70.0 %all-to-all-start.1 = ((bf16[64,72,128]{2,1,0:T(8,128)(2,1)}), bf16[64,72,128]{2,1,0:T(8,128)(2,1)S(1)}, u32[]{:S(2)}, u32[]{:S(2)}) async-start(bf16[64,72,128]{2,1,0:T(8,128)(2,1)} %shard_map.106), calls=%async_computation.1 | async-start | bytes 2359296 | tf_op jit(solution)/shard_map/all_to_all | solution.py:267
  101.6 40.9 %copy-start.14 = (bf16[2,256,152]{1,2,0:T(8,128)(2,1)S(1)}, bf16[2,256,152]{1,2,0:T(8,128)(2,1)}, u32[]{:S(2)}) copy-start(bf16[2,256,152]{1,2,0:T(8,128)(2,1)} %param.13) | copy-start | bytes 466948
  101.7 41.7 %collective-permute-start.3 = (bf16[152,1792]{1,0:T(8,128)(2,1)}, bf16[152,1792]{1,0:T(8,128)(2,1)}, u32[]{:S(2)}, u32[]{:S(2)}) collective-permute-start(bf16[152,1792]{1,0:T(8,128)(2,1)} %copy-done.8), channel_id=1, source_target_pairs={{0,1},{1,0},{2,3},{3,2},{4,5},{5,4},{6,7},{7,6},{8,9},{9,8},{10,11... | collective-permute-start | bytes 1634312 | tf_op jit(solution)/shard_map/ppermute | solution.py:140
  106.6 36.0 %collective-permute-start.2 = (bf16[152,256]{1,0:T(8,128)(2,1)S(1)}, bf16[152,256]{1,0:T(8,128)(2,1)S(1)}, u32[]{:S(2)}, u32[]{:S(2)}) collective-permute-start(bf16[152,256]{1,0:T(8,128)(2,1)S(1)} %convolution_convert_fusion.3), channel_id=1, source_target_pairs={{0,1},{1,0},{2,3},{3,2},{4,5},{5,4},{6,7},{7,6},{8,9},{9,8},{10,11... | collective-permute-start | bytes 233480 | tf_op jit(solution)/shard_map/ppermute | solution.py:140
  143.3 6.8 %copy-start.11 = (bf16[1792,768]{1,0:T(8,128)(2,1)S(1)}, bf16[1792,768]{1,0:T(8,128)(2,1)}, u32[]{:S(2)}) copy-start(bf16[1792,768]{1,0:T(8,128)(2,1)} %all-gather.4.cloned.1.call-done) | copy-start | bytes 8257540
  146.1 16.8 %collective-permute-start.4 = (bf16[152,768]{1,0:T(8,128)(2,1)S(1)}, bf16[152,768]{1,0:T(8,128)(2,1)}, u32[]{:S(2)}, u32[]{:S(2)}) collective-permute-start(bf16[152,768]{1,0:T(8,128)(2,1)S(1)} %convolution_convert_fusion.2), channel_id=1, source_target_pairs={{0,1},{1,0},{2,3},{3,2},{4,5},{5,4},{6,7},{7,6},{8,9},{9,8},{10,11... | collective-permute-start | bytes 700424 | tf_op jit(solution)/shard_map/ppermute | solution.py:140
  152.2 9.4 %copy-start.5 = (bf16[152,1792]{1,0:T(8,128)(2,1)S(1)}, bf16[152,1792]{1,0:T(8,128)(2,1)}, u32[]{:S(2)}) copy-start(bf16[152,1792]{1,0:T(8,128)(2,1)} %copy-done.4) | copy-start | bytes 1634308
  152.2 15.7 %collective-permute-start.5 = (bf16[152,1792]{1,0:T(8,128)(2,1)S(1)}, bf16[152,1792]{1,0:T(8,128)(2,1)S(1)}, u32[]{:S(2)}, u32[]{:S(2)}) collective-permute-start(bf16[152,1792]{1,0:T(8,128)(2,1)S(1)} %convolution_convert_fusion.1), channel_id=1, source_target_pairs={{0,1},{1,0},{2,3},{3,2},{4,5},{5,4},{6,7},{7,6},{8,9},{9,8},{10,11... | collective-permute-start | bytes 1634312 | tf_op jit(solution)/shard_map/ppermute | solution.py:140
  154.3 7.3 %copy-start.12 = (bf16[1792,768]{1,0:T(8,128)(2,1)S(1)}, bf16[1792,768]{1,0:T(8,128)(2,1)}, u32[]{:S(2)}) copy-start(bf16[1792,768]{1,0:T(8,128)(2,1)} %all-gather.4.cloned.1.call-done) | copy-start | bytes 8257540
  154.5 7.7 %collective-permute-start.6 = (bf16[56,152]{1,0:T(8,128)(2,1)S(1)}, bf16[56,152]{1,0:T(8,128)(2,1)S(1)}, u32[]{:S(2)}, u32[]{:S(2)}) collective-permute-start(bf16[56,152]{1,0:T(8,128)(2,1)S(1)} %shard_map.108), channel_id=1, source_target_pairs={{0,65},{1,64},{32,97},{33,96},{64,1},{65,0},{96,33},{97,32},{128,1... | collective-permute-start | bytes 51080 | tf_op jit(solution)/shard_map/ppermute | solution.py:207
  161.6 1.3 copy-start.13
Sparse Core Ops, SparseCore 0:
  60.6 50.0 all-gather.3

commit v4 on v3

--- a/solution.py
+++ b/solution.py
@@ -12,6 +12,7 @@
 EXPERT = ("zh", "x", "core")
 SHARE = ("y", "zl")
 LANES = 128
+STACK = 16
 VMEM_LIMIT = 48 * 1024 * 1024
 
 
@@ -147,11 +148,11 @@
 
 def terms_kernel(runs, grad_ref, first_ref, second_ref, out_ref):
     parts, rows, _ = out_ref.shape
-    hidden, width = first_ref.shape[0], grad_ref.shape[0] * 2 // parts
-    span = parts // (2 * runs)
+    hidden, width = first_ref.shape[0], rows - STACK
+    span, step = parts // (2 * runs), grad_ref.shape[0] // runs
     stack, extra = rows - width, hidden - LANES
     for run in range(runs):
-        grads = grad_ref[run * span * width : (run + 1) * span * width, :]
+        grads = grad_ref[run * step : run * step + span * width, :]
         for half, ref in enumerate((first_ref, second_ref)):
             value = lax.dot_general(
                 grads, ref[...], (((1,), (1,)), ((), ())), preferred_element_type=F32
@@ -185,17 +186,16 @@
     out_ref[...] = jnp.concatenate([total[:width, :], last[:width, :]], axis=1).astype(BF)
 
 
-def scatter_terms(grad_half, units):
+def scatter_terms(grad_runs, units, width):
     parts, runs = lax.axis_size(EXPERT), lax.axis_size("y")
-    width, hidden = grad_half.shape[0] * 2 // parts, units[0].shape[0]
     return local_kernel(
         functools.partial(terms_kernel, runs),
-        jax.ShapeDtypeStruct((parts, width + 16, LANES), BF),
-        4 * grad_half.shape[0] * hidden * grad_half.shape[1],
+        jax.ShapeDtypeStruct((parts, width + STACK, LANES), BF),
+        2 * parts * width * units[0].size,
         4 * parts * width * LANES,
         0,
         3,
-    )(grad_half, *units)
+    )(grad_runs, *units)
 
 
 def scatter_total(came, width, hidden):
@@ -219,7 +219,8 @@
     half_index = half.reshape(1)
     grad_rows = grad_out.T
 
-    grad_half = gather_columns(grad_rows)
+    padded = -feature_width % LANES
+    grad_runs = gather_columns(jnp.pad(grad_rows, ((0, padded), (0, 0))))
 
     outgoing = local_kernel(
         functools.partial(dispatch_kernel, expert_count, capacity),
@@ -233,20 +234,20 @@
         (dense_saved, expert_saved, dense_down, expert_down), outgoing
     )
     received = lax.all_to_all(outgoing, EXPERT, split_axis=0, concat_axis=0, tiled=True)
+    gate_dense, up_dense, sigmoid_dense, dense_units = swiglu_parts(dense_saved[0].T, dense_saved[1].T)
+    gate_expert, up_expert, sigmoid_expert, expert_units = swiglu_parts(
+        expert_saved[0, 0].T, expert_saved[0, 1].T
+    )
+    units_other = swap(jnp.concatenate([dense_units, expert_units], axis=1))
+    dense_units_other, expert_units_other = units_other[:, :tokens], units_other[:, tokens:]
     received = local_kernel(
         functools.partial(arrange_kernel, capacity),
         jax.ShapeDtypeStruct((feature_width, slots), BF),
         4 * slots * slots * LANES,
         8 * slots * LANES,
-    )(after(received.reshape(-1, LANES), grad_half))
+    )(received.reshape(-1, LANES))
     sent_half = gather_columns(received)
 
-    gate_dense, up_dense, sigmoid_dense, dense_units = swiglu_parts(dense_saved[0].T, dense_saved[1].T)
-    gate_expert, up_expert, sigmoid_expert, expert_units = swiglu_parts(
-        expert_saved[0, 0].T, expert_saved[0, 1].T
-    )
-    units_other = swap(jnp.concatenate([dense_units, expert_units], axis=1))
-    dense_units_other, expert_units_other = units_other[:, :tokens], units_other[:, tokens:]
     split = local_kernel(
         functools.partial(split_kernel, runs),
         [jax.ShapeDtypeStruct((hidden_count, model_width // 2), BF)] * 2,
@@ -256,35 +257,37 @@
         1,
     )
     dense_mine, dense_theirs = split(half_index, dense_down)
-    dense_theirs = swap(dense_theirs)
+    dense_swapped = swap(dense_theirs)
     expert_mine, expert_theirs = split(half_index, after(expert_down[0], dense_mine))
 
     first = half == 0
     units = (jnp.where(first, dense_units, dense_units_other), jnp.where(first, dense_units_other, dense_units))
-    units = after(units, (dense_theirs, expert_theirs))
-    terms = scatter_terms(grad_half, units)
+    units = after(units, (received, dense_theirs, expert_theirs))
+    terms = scatter_terms(grad_runs, units, model_width // expert_count)
     expert_theirs = swap(after(expert_theirs, terms))
+    dense_theirs = dense_swapped
     came = lax.all_to_all(terms, EXPERT, split_axis=0, concat_axis=0, tiled=True)
-    grad_half = after(grad_half, terms)
-    cot_other = jnp.einsum("hf,fr->hr", dense_theirs, grad_half, preferred_element_type=F32)
-    cot_own = jnp.einsum("hf,fr->hr", dense_mine, grad_half, preferred_element_type=F32)
-    dense_cot = cot_own + swap(cot_other.astype(BF)).astype(F32)
-
-    dense_pre_grad = pre_cotangents(dense_cot, gate_dense, up_dense, sigmoid_dense).transpose(0, 2, 1)
-    sent_half = after(sent_half, dense_pre_grad)
-
-    cot_other = jnp.einsum("hf,fr->hr", expert_theirs, sent_half, preferred_element_type=F32)
-    cot_other = cot_other.astype(BF)
-    sent_half = after(sent_half, cot_other)
-    cot_other = swap(cot_other)
+    grad_runs = after(grad_runs, terms).reshape(runs, -1, tokens)
+    grad_half = grad_runs[:, :feature_width].reshape(-1, tokens)
+    dense_other = jnp.einsum("hf,fr->hr", dense_theirs, grad_half, preferred_element_type=F32).astype(BF)
+    dense_cot = jnp.einsum("hf,fr->hr", dense_mine, grad_half, preferred_element_type=F32)
+    sent_half = after(sent_half, (dense_other, dense_cot))
+
     grad_other = jnp.einsum("hr,fr->hf", expert_units_other, sent_half, preferred_element_type=F32)
     grad_other = grad_other.astype(BF)
-    sent_half, came = after((sent_half, came), grad_other)
+    sent_half = after(sent_half, grad_other)
     grad_other = swap(grad_other)
+    cot_other = jnp.einsum("hf,fr->hr", expert_theirs, sent_half, preferred_element_type=F32)
+    cot_other = jnp.concatenate([dense_other, cot_other.astype(BF)], axis=1)
+    sent_half, came = after((sent_half, came), cot_other)
+    cot_other = swap(cot_other)
     dense_share = scatter_total(came, model_width // expert_count, hidden_count)
     grad_own = jnp.einsum("hr,fr->hf", expert_units, sent_half, preferred_element_type=F32).astype(BF)
     cot_own = jnp.einsum("hf,fr->hr", expert_mine, sent_half, preferred_element_type=F32)
-    expert_cot = cot_own + cot_other.astype(F32)
+    cot_other = cot_other.astype(F32)
+    expert_cot = cot_own + cot_other[:, tokens:]
+    dense_cot = dense_cot + cot_other[:, :tokens]
+    dense_pre_grad = pre_cotangents(dense_cot, gate_dense, up_dense, sigmoid_dense).transpose(0, 2, 1)
     expert_down_grad = local_kernel(
         functools.partial(join_kernel, runs),
         jax.ShapeDtypeStruct((hidden_count, model_width), BF),

time: 177 us -> 166 us (0.938)
  starting transfers between devices: 61.8 us -> 35.1 us
  blocking collectives: 24.8 us -> 38.8 us
  local copies, waits for them, and re-layouts: 4.73 us -> 6.84 us
    all_to_all x0 -> x1, blocking collectives: none -> 38.8 us  [body(): lax.all_to_all(outgoing, EXPERT, split_axis=0, concat_axis=0, tiled=True)]
    all_gather x1 -> x0, blocking collectives: 24.8 us -> none  [gather_columns(): whole = lax.all_gather(rows, 'y', axis=0, tiled=False)]
    all_to_all x1 -> x0, starting transfers between devices: 22.7 us -> none  [body(): lax.all_to_all(outgoing, EXPERT, split_axis=0, concat_axis=0, tiled=True)]
    ppermute x6 -> x5, starting transfers between devices: 17.5 us -> 15.5 us  [swap(): return lax.ppermute(values, 'zl', [(0, 1), (1, 0)])]
    all_to_all x1, starting transfers between devices: 17.3 us -> 15.4 us  [body(): lax.all_to_all(terms, EXPERT, split_axis=0, concat_axis=0, tiled=True)]
    ppermute x6 -> x5, waiting for transfers between devices: 45.5 us -> 46.5 us  [swap(): return lax.ppermute(values, 'zl', [(0, 1), (1, 0)])]
    unnamed x30 -> x28, local copies, waits for them, and re-layouts: 4.73 us -> 5.13 us
  transfers between devices with their start and end apart: 10 -> 9, of which waited for: 3 -> 4; matrix products, arithmetic and copies ran while one was open for 10% -> 10% of each run, Pallas kernels for 2% -> 3%
where the time goes in v4:
time: 166 us
  waiting for transfers between devices  46.6 us (28%)
  blocking collectives  38.8 us (23%)
  starting transfers between devices  35.1 us (21%)
  between operations  14.4 us (9%)
  matrix products  10 us (6%)
  other arithmetic  7.05 us (4%)
  local copies, waits for them, and re-layouts  6.84 us (4%)
  Pallas kernels  6.81 us (4%)
    ppermute x5, waiting for transfers between devices, swap(): return lax.ppermute(values, 'zl', [(0, 1), (1, 0)])  46.5 us
    all_to_all x1, blocking collectives, body(): lax.all_to_all(outgoing, EXPERT, split_axis=0, concat_axis=0, tiled=True)  38.8 us
    ppermute x5, starting transfers between devices, swap(): return lax.ppermute(values, 'zl', [(0, 1), (1, 0)])  15.5 us
    all_to_all x1, starting transfers between devices, body(): lax.all_to_all(terms, EXPERT, split_axis=0, concat_axis=0, tiled=True)  15.4 us
    unnamed x28, local copies, waits for them, and re-layouts  5.13 us
    ppermute x1, starting transfers between devices, scatter_total(): other = lax.ppermute(mine, ('x', 'zl'), route)  4.02 us
  transfers between devices with their start and end apart: 9, of which 4 were waited for; matrix products, arithmetic and copies ran while one was open for 10% of the time, Pallas kernels for 3%

profile of v4, /device:TPU:1, one launch (start us, length us, event | category | flops | bytes accessed | tf_op | source)
XLA Modules:
  0.0 165.5 jit_solution(11735254908195733821)
XLA Ops:
  7.2 1.6 pad.4
  9.0 0.9 copy-done.4
  11.2 1.1 shard_map.102
  12.3 38.8 %all_to_all.10 = bf16[64,24,128]{2,1,0:T(8,128)(2,1)S(1)} all-to-all(bf16[64,24,128]{2,1,0:T(8,128)(2,1)S(1)} %bitcast.182), channel_id=1, replica_groups=mesh['zh'=4,'x'=8,'core'=2,'y'=8,'zl'=2] {'zh','x','core'}, dimensions={0} | all-to-all | bytes 786432 | tf_op jit(solution)/shard_map/all_to_all | solution.py:236
  51.1 1.4 shard_map.105
  52.7 1.2 fusion.2
  53.9 0.8 pad_maximum_fusion
  54.7 3.4 %collective-permute-start.1 = (bf16[152,1024]{1,0:T(8,128)(2,1)}, bf16[152,1024]{1,0:T(8,128)(2,1)}, u32[]{:S(2)}, u32[]{:S(2)}) collective-permute-start(bf16[152,1024]{1,0:T(8,128)(2,1)} %pad_maximum_fusion), channel_id=1, source_target_pairs={{0,1},{1,0},{2,3},{3,2},{4,5},{5,4},{6,7},{7,6},{8,9},{9,8},{10,11... | collective-permute-start | bytes 933896 | tf_op jit(solution)/shard_map/ppermute | solution.py:141
  58.5 0.8 copy-done.6
  59.7 0.8 copy-done.5
  60.5 4.3 %collective-permute-done.1 = bf16[152,1024]{1,0:T(8,128)(2,1)} collective-permute-done((bf16[152,1024]{1,0:T(8,128)(2,1)}, bf16[152,1024]{1,0:T(8,128)(2,1)}, u32[]{:S(2)}, u32[]{:S(2)}) %collective-permute-start.1) | collective-permute-done | bytes 311328 | tf_op jit(solution)/shard_map/ppermute | solution.py:141
  64.8 1.0 broadcast_select_fusion
  65.9 1.2 copy-done
  67.1 1.8 %shard_map.106 = bf16[64,72,128]{2,1,0:T(8,128)(2,1)} custom-call(bf16[2048,256]{1,0:T(8,128)(2,1)S(1)} %copy-done, bf16[152,256]{1,0:T(8,128)(2,1)S(1)} %get-tuple-element.30.first_ref, bf16[152,256]{1,0:T(8,128)(2,1)S(1)} %get-tuple-element.31.second_ref), custom_call_target="tpu_custom_call" | custom-call | flops 278921216 | bytes 1835008 | tf_op jit(solution)/shard_map/pallas_call | solution.py:191
  68.9 15.4 %all-to-all-start.1 = ((bf16[64,72,128]{2,1,0:T(8,128)(2,1)}), bf16[64,72,128]{2,1,0:T(8,128)(2,1)S(1)}, u32[]{:S(2)}, u32[]{:S(2)}) async-start(bf16[64,72,128]{2,1,0:T(8,128)(2,1)} %shard_map.106), calls=%async_computation.1 | async-start | bytes 2359296 | tf_op jit(solution)/shard_map/all_to_all | solution.py:269
  84.3 2.4 %collective-permute-start = (bf16[152,1792]{1,0:T(8,128)(2,1)}, bf16[152,1792]{1,0:T(8,128)(2,1)}, u32[]{:S(2)}, u32[]{:S(2)}) collective-permute-start(bf16[152,1792]{1,0:T(8,128)(2,1)} %copy-done.6), channel_id=1, source_target_pairs={{0,1},{1,0},{2,3},{3,2},{4,5},{5,4},{6,7},{7,6},{8,9},{9,8},{10,11... | collective-permute-start | bytes 1634312 | tf_op jit(solution)/shard_map/ppermute | solution.py:141
  86.8 2.9 %collective-permute-start.2 = (bf16[152,1792]{1,0:T(8,128)(2,1)}, bf16[152,1792]{1,0:T(8,128)(2,1)}, u32[]{:S(2)}, u32[]{:S(2)}) collective-permute-start(bf16[152,1792]{1,0:T(8,128)(2,1)} %copy-done.5), channel_id=1, source_target_pairs={{0,1},{1,0},{2,3},{3,2},{4,5},{5,4},{6,7},{7,6},{8,9},{9,8},{10,11... | collective-permute-start | bytes 1634312 | tf_op jit(solution)/shard_map/ppermute | solution.py:141
  90.1 33.2 %collective-permute-done = bf16[152,1792]{1,0:T(8,128)(2,1)} collective-permute-done((bf16[152,1792]{1,0:T(8,128)(2,1)}, bf16[152,1792]{1,0:T(8,128)(2,1)}, u32[]{:S(2)}, u32[]{:S(2)}) %collective-permute-start) | collective-permute-done | bytes 544800 | tf_op jit(solution)/shard_map/ppermute | solution.py:141
  123.3 1.4 convolution_convert_fusion.3
  124.7 3.1 %convolution_convert_fusion.1 = bf16[152,1792]{1,0:T(8,128)(2,1)S(1)} fusion(bf16[1792,768]{1,0:T(8,128)(2,1)} %all-gather.5.cloned.1.call-done, bf16[152,1024]{1,0:T(8,128)(2,1)} %collective-permute-done.1), kind=kOutput, calls=%fused_computation.1 | convolution fusion | flops 418654208 | bytes 3530752 | tf_op jit(solution)/shard_map/hr,fr->hf/dot_general | solution.py:276
  127.8 3.4 %collective-permute-start.4 = (bf16[152,1792]{1,0:T(8,128)(2,1)S(1)}, bf16[152,1792]{1,0:T(8,128)(2,1)S(1)}, u32[]{:S(2)}, u32[]{:S(2)}) collective-permute-start(bf16[152,1792]{1,0:T(8,128)(2,1)S(1)} %convolution_convert_fusion.1), channel_id=1, source_target_pairs={{0,1},{1,0},{2,3},{3,2},{4,5},{5,4},{6,7},{7,6},{8,9},{9,8},{10,11... | collective-permute-start | bytes 1634312 | tf_op jit(solution)/shard_map/ppermute | solution.py:141
  131.2 3.8 %collective-permute-done.2 = bf16[152,1792]{1,0:T(8,128)(2,1)} collective-permute-done((bf16[152,1792]{1,0:T(8,128)(2,1)}, bf16[152,1792]{1,0:T(8,128)(2,1)}, u32[]{:S(2)}, u32[]{:S(2)}) %collective-permute-start.2) | collective-permute-done | bytes 544800 | tf_op jit(solution)/shard_map/ppermute | solution.py:141
  135.0 1.7 %convolution_convert_fusion.2 = bf16[152,768]{1,0:T(8,128)(2,1)S(1)} fusion(bf16[152,1792]{1,0:T(8,128)(2,1)} %collective-permute-done.2, bf16[1792,768]{1,0:T(8,128)(2,1)S(1)} %copy-done.9), kind=kOutput, calls=%fused_computation.2 | convolution fusion | flops 418498560 | bytes 3530752 | tf_op jit(solution)/shard_map/hf,fr->hr/dot_general | solution.py:280
  136.6 0.8 pad_maximum_fusion.1
  137.4 3.5 %collective-permute-start.3 = (bf16[152,1024]{1,0:T(8,128)(2,1)}, bf16[152,1024]{1,0:T(8,128)(2,1)}, u32[]{:S(2)}, u32[]{:S(2)}) collective-permute-start(bf16[152,1024]{1,0:T(8,128)(2,1)} %pad_maximum_fusion.1), channel_id=1, source_target_pairs={{0,1},{1,0},{2,3},{3,2},{4,5},{5,4},{6,7},{7,6},{8,9},{9,8},{10,11... | collective-permute-start | bytes 933896 | tf_op jit(solution)/shard_map/ppermute | solution.py:141
  141.1 4.0 %collective-permute-start.5 = (bf16[56,152]{1,0:T(8,128)(2,1)S(1)}, bf16[56,152]{1,0:T(8,128)(2,1)S(1)}, u32[]{:S(2)}, u32[]{:S(2)}) collective-permute-start(bf16[56,152]{1,0:T(8,128)(2,1)S(1)} %shard_map.108), channel_id=1, source_target_pairs={{0,65},{1,64},{32,97},{33,96},{64,1},{65,0},{96,33},{97,32},{128,1... | collective-permute-start | bytes 51080 | tf_op jit(solution)/shard_map/ppermute | solution.py:207
  145.2 2.8 %convolution_convert_fusion.own_ref = bf16[152,1792]{1,0:T(8,128)(2,1)S(1)} fusion(bf16[152,768]{1,0:T(8,128)(2,1)S(1)} %fusion.2, bf16[1792,768]{1,0:T(8,128)(2,1)} %all-gather.5.cloned.1.call-done), kind=kOutput, calls=%fused_computation | convolution fusion | flops 418654208 | bytes 3530752 | tf_op jit(solution)/shard_map/hr,fr->hf/dot_general | solution.py:285
  148.6 5.3 %collective-permute-done.3 = bf16[152,1024]{1,0:T(8,128)(2,1)} collective-permute-done((bf16[152,1024]{1,0:T(8,128)(2,1)}, bf16[152,1024]{1,0:T(8,128)(2,1)}, u32[]{:S(2)}, u32[]{:S(2)}) %collective-permute-start.3) | collective-permute-done | bytes 311328 | tf_op jit(solution)/shard_map/ppermute | solution.py:141
  153.9 1.0 convert_element_type.78
  155.8 0.7 fusion.18
  156.5 0.8 maximum_bitcast_fusion
  157.3 1.4 shard_map.107
  (42 shorter events, 4.5 us)
Async XLA Ops:
  7.2 50.9 %copy-start.2 = (bf16[152,3584]{1,0:T(8,128)(2,1)S(1)}, bf16[152,3584]{1,0:T(8,128)(2,1)}, u32[]{:S(2)}) copy-start(bf16[152,3584]{1,0:T(8,128)(2,1)} %weights_ref) | copy-start | bytes 3268612
  7.2 58.7 %all-gather.7.cloned.1.call-start = ((), (), s32[]{:S(2)}) async-start(), calls=%async_computation.3 | async-start | bytes 1179648 | tf_op jit(solution)/shard_map/all_gather | solution.py:145
  8.9 115.8 %all-gather.5.cloned.1.call-start = ((), (), s32[]{:S(2)}) async-start(), calls=%async_computation.2 | async-start | bytes 3096576 | tf_op jit(solution)/shard_map/all_gather | solution.py:145
  8.9 0.9 copy-start.4
  9.8 0.7 copy-start.7
  10.5 0.7 copy-start.8
  11.2 41.4 %copy-start.11 = (bf16[2,256,152]{1,2,0:T(8,128)(2,1)S(1)}, bf16[2,256,152]{1,2,0:T(8,128)(2,1)}, u32[]{:S(2)}) copy-start(bf16[2,256,152]{1,2,0:T(8,128)(2,1)} %param.13) | copy-start | bytes 466948
  11.2 48.1 %copy-start.3 = (bf16[1,152,3584]{2,1,0:T(8,128)(2,1)S(1)}, bf16[1,152,3584]{2,1,0:T(8,128)(2,1)}, u32[]{:S(2)}) copy-start(bf16[1,152,3584]{2,1,0:T(8,128)(2,1)} %param.10) | copy-start | bytes 3268612
  54.7 10.1 %collective-permute-start.1 = (bf16[152,1024]{1,0:T(8,128)(2,1)}, bf16[152,1024]{1,0:T(8,128)(2,1)}, u32[]{:S(2)}, u32[]{:S(2)}) collective-permute-start(bf16[152,1024]{1,0:T(8,128)(2,1)} %pad_maximum_fusion), channel_id=1, source_target_pairs={{0,1},{1,0},{2,3},{3,2},{4,5},{5,4},{6,7},{7,6},{8,9},{9,8},{10,11... | collective-permute-start | bytes 933896 | tf_op jit(solution)/shard_map/ppermute | solution.py:141
  58.5 0.8 copy-start.6
  59.7 0.8 copy-start.5
  65.9 1.2 copy-start
  67.1 19.7 %copy-start.1 = (bf16[2048,256]{1,0:T(8,128)(2,1)S(1)}, bf16[2048,256]{1,0:T(8,128)(2,1)}, u32[]{:S(2)}) copy-start(bf16[2048,256]{1,0:T(8,128)(2,1)} %all-gather.7.cloned.1.call-done.grad_ref) | copy-start | bytes 3145732
  68.9 72.0 %all-to-all-start.1 = ((bf16[64,72,128]{2,1,0:T(8,128)(2,1)}), bf16[64,72,128]{2,1,0:T(8,128)(2,1)S(1)}, u32[]{:S(2)}, u32[]{:S(2)}) async-start(bf16[64,72,128]{2,1,0:T(8,128)(2,1)} %shard_map.106), calls=%async_computation.1 | async-start | bytes 2359296 | tf_op jit(solution)/shard_map/all_to_all | solution.py:269
  84.3 39.0 %collective-permute-start = (bf16[152,1792]{1,0:T(8,128)(2,1)}, bf16[152,1792]{1,0:T(8,128)(2,1)}, u32[]{:S(2)}, u32[]{:S(2)}) collective-permute-start(bf16[152,1792]{1,0:T(8,128)(2,1)} %copy-done.6), channel_id=1, source_target_pairs={{0,1},{1,0},{2,3},{3,2},{4,5},{5,4},{6,7},{7,6},{8,9},{9,8},{10,11... | collective-permute-start | bytes 1634312 | tf_op jit(solution)/shard_map/ppermute | solution.py:141
  86.8 48.1 %collective-permute-start.2 = (bf16[152,1792]{1,0:T(8,128)(2,1)}, bf16[152,1792]{1,0:T(8,128)(2,1)}, u32[]{:S(2)}, u32[]{:S(2)}) collective-permute-start(bf16[152,1792]{1,0:T(8,128)(2,1)} %copy-done.5), channel_id=1, source_target_pairs={{0,1},{1,0},{2,3},{3,2},{4,5},{5,4},{6,7},{7,6},{8,9},{9,8},{10,11... | collective-permute-start | bytes 1634312 | tf_op jit(solution)/shard_map/ppermute | solution.py:141
  124.7 10.3 %copy-start.9 = (bf16[1792,768]{1,0:T(8,128)(2,1)S(1)}, bf16[1792,768]{1,0:T(8,128)(2,1)}, u32[]{:S(2)}) copy-start(bf16[1792,768]{1,0:T(8,128)(2,1)} %all-gather.5.cloned.1.call-done) | copy-start | bytes 8257540
  127.8 29.5 %collective-permute-start.4 = (bf16[152,1792]{1,0:T(8,128)(2,1)S(1)}, bf16[152,1792]{1,0:T(8,128)(2,1)S(1)}, u32[]{:S(2)}, u32[]{:S(2)}) collective-permute-start(bf16[152,1792]{1,0:T(8,128)(2,1)S(1)} %convolution_convert_fusion.1), channel_id=1, source_target_pairs={{0,1},{1,0},{2,3},{3,2},{4,5},{5,4},{6,7},{7,6},{8,9},{9,8},{10,11... | collective-permute-start | bytes 1634312 | tf_op jit(solution)/shard_map/ppermute | solution.py:141
  137.4 17.6 %copy-start.12 = (bf16[2,256,152]{1,2,0:T(8,128)(2,1)S(1)}, bf16[2,256,152]{1,2,0:T(8,128)(2,1)}, u32[]{:S(2)}) copy-start(bf16[2,256,152]{1,2,0:T(8,128)(2,1)} %param.13) | copy-start | bytes 466948
  137.4 16.5 %collective-permute-start.3 = (bf16[152,1024]{1,0:T(8,128)(2,1)}, bf16[152,1024]{1,0:T(8,128)(2,1)}, u32[]{:S(2)}, u32[]{:S(2)}) collective-permute-start(bf16[152,1024]{1,0:T(8,128)(2,1)} %pad_maximum_fusion.1), channel_id=1, source_target_pairs={{0,1},{1,0},{2,3},{3,2},{4,5},{5,4},{6,7},{7,6},{8,9},{9,8},{10,11... | collective-permute-start | bytes 933896 | tf_op jit(solution)/shard_map/ppermute | solution.py:141
  141.1 14.6 %copy-start.10 = (bf16[1792,768]{1,0:T(8,128)(2,1)S(1)}, bf16[1792,768]{1,0:T(8,128)(2,1)}, u32[]{:S(2)}) copy-start(bf16[1792,768]{1,0:T(8,128)(2,1)} %all-gather.5.cloned.1.call-done) | copy-start | bytes 8257540
  141.1 14.6 %copy-start.13 = (bf16[1,2,768,152]{2,3,1,0:T(8,128)(2,1)S(1)}, bf16[1,2,768,152]{2,3,1,0:T(8,128)(2,1)}, u32[]{:S(2)}) copy-start(bf16[1,2,768,152]{2,3,1,0:T(8,128)(2,1)} %param.11) | copy-start | bytes 1400836
  141.1 6.9 %collective-permute-start.5 = (bf16[56,152]{1,0:T(8,128)(2,1)S(1)}, bf16[56,152]{1,0:T(8,128)(2,1)S(1)}, u32[]{:S(2)}, u32[]{:S(2)}) collective-permute-start(bf16[56,152]{1,0:T(8,128)(2,1)S(1)} %shard_map.108), channel_id=1, source_target_pairs={{0,65},{1,64},{32,97},{33,96},{64,1},{65,0},{96,33},{97,32},{128,1... | collective-permute-start | bytes 51080 | tf_op jit(solution)/shard_map/ppermute | solution.py:207
Sparse Core Ops, SparseCore 0:
  11.2 51.6 all-gather.6
  66.2 49.4 all-gather.4

commit v5 on v3

--- a/solution.py
+++ b/solution.py
@@ -12,6 +12,7 @@
 EXPERT = ("zh", "x", "core")
 SHARE = ("y", "zl")
 LANES = 128
+STACK = 16
 VMEM_LIMIT = 48 * 1024 * 1024
 
 
@@ -145,31 +146,40 @@
     return whole.reshape(-1, rows.shape[1])
 
 
-def terms_kernel(runs, grad_ref, first_ref, second_ref, out_ref):
-    parts, rows, _ = out_ref.shape
-    hidden, width = first_ref.shape[0], grad_ref.shape[0] * 2 // parts
-    span = parts // (2 * runs)
-    stack, extra = rows - width, hidden - LANES
-    for run in range(runs):
-        grads = grad_ref[run * span * width : (run + 1) * span * width, :]
-        for half, ref in enumerate((first_ref, second_ref)):
-            value = lax.dot_general(
-                grads, ref[...], (((1,), (1,)), ((), ())), preferred_element_type=F32
-            )
-            for index in range(span):
-                block = value[index * width : (index + 1) * width, :]
-                last = jnp.concatenate(
-                    [block[:, LANES:], jnp.zeros((-width % stack, extra), F32)], axis=0
-                )
-                count = last.shape[0] // stack
-                last = jnp.concatenate(
-                    [last[piece * stack : (piece + 1) * stack, :] for piece in range(count)]
-                    + [jnp.zeros((stack, LANES - count * extra), F32)],
-                    axis=1,
-                )
-                out_ref[(run * 2 + half) * span + index] = jnp.concatenate(
-                    [block[:, :LANES], last], axis=0
-                ).astype(BF)
+def terms_kernel(runs, core_ref, grad_ref, first_ref, second_ref, mine_ref, theirs_ref):
+    pairs, rows, _ = mine_ref.shape
+    hidden, width = first_ref.shape[0], rows - STACK
+    span = pairs // runs
+    extra, missing = hidden - LANES, -width % STACK
+    for core in range(2):
+
+        @pl.when(core_ref[0] == core)
+        def _():
+            for run in range(runs):
+                grads = grad_ref[run * span * width : (run + 1) * span * width, :]
+                for half, ref in enumerate((first_ref, second_ref)):
+                    value = lax.dot_general(
+                        grads, ref[...], (((1,), (1,)), ((), ())), preferred_element_type=F32
+                    )
+                    for index in range(span):
+                        block = value[index * width : (index + 1) * width, :]
+                        last = jnp.concatenate([block[:, LANES:], jnp.zeros((missing, extra), F32)], axis=0)
+                        count = last.shape[0] // STACK
+                        last = jnp.concatenate(
+                            [last[piece * STACK : (piece + 1) * STACK, :] for piece in range(count)]
+                            + [jnp.zeros((STACK, LANES - count * extra), F32)],
+                            axis=1,
+                        )
+                        block = jnp.concatenate([block[:, :LANES], last], axis=0)
+                        place = (run * 2 + half) * span + index
+                        if place % 2 == core:
+                            mine_ref[place // 2] = block
+                        else:
+                            theirs_ref[place // 2] = block.astype(BF)
+
+
+def pair_kernel(mine_ref, other_ref, out_ref):
+    out_ref[...] = (mine_ref[...] + other_ref[...].astype(F32)).astype(BF)
 
 
 def total_kernel(came_ref, out_ref):
@@ -185,19 +195,6 @@
     out_ref[...] = jnp.concatenate([total[:width, :], last[:width, :]], axis=1).astype(BF)
 
 
-def scatter_terms(grad_half, units):
-    parts, runs = lax.axis_size(EXPERT), lax.axis_size("y")
-    width, hidden = grad_half.shape[0] * 2 // parts, units[0].shape[0]
-    return local_kernel(
-        functools.partial(terms_kernel, runs),
-        jax.ShapeDtypeStruct((parts, width + 16, LANES), BF),
-        4 * grad_half.shape[0] * hidden * grad_half.shape[1],
-        4 * parts * width * LANES,
-        0,
-        3,
-    )(grad_half, *units)
-
-
 def scatter_total(came, width, hidden):
     mine = local_kernel(
         total_kernel, jax.ShapeDtypeStruct((width, hidden), BF), came.size, 2 * came.size
@@ -215,38 +212,53 @@
     capacity = slots // expert_count
     tokens, feature_width = grad_out.shape
     model_width = dense_down.shape[1]
+    width = model_width // expert_count
     half = lax.axis_index("zl").astype(jnp.int32)
     half_index = half.reshape(1)
+    core_index = lax.axis_index("core").astype(jnp.int32).reshape(1)
+    first = half == 0
     grad_rows = grad_out.T
-
-    grad_half = gather_columns(grad_rows)
 
     outgoing = local_kernel(
         functools.partial(dispatch_kernel, expert_count, capacity),
         jax.ShapeDtypeStruct((expert_count * 2 * capacity, LANES), BF),
         4 * slots * tokens * feature_width,
         4 * slots * LANES,
-        arrays=3,
+        0,
+        3,
     )(routes.T, probs.T, grad_rows)
     outgoing = outgoing.reshape(expert_count, 2 * capacity, LANES)
-    dense_saved, expert_saved, dense_down, expert_down = after(
-        (dense_saved, expert_saved, dense_down, expert_down), outgoing
-    )
     received = lax.all_to_all(outgoing, EXPERT, split_axis=0, concat_axis=0, tiled=True)
+
+    dense_saved = after(dense_saved, outgoing)
+    gate_dense, up_dense, sigmoid_dense, dense_units = swiglu_parts(dense_saved[0].T, dense_saved[1].T)
+    dense_units_other = swap(dense_units)
+    grad_half = gather_columns(after(grad_rows, (outgoing, dense_units)))
+
     received = local_kernel(
         functools.partial(arrange_kernel, capacity),
         jax.ShapeDtypeStruct((feature_width, slots), BF),
         4 * slots * slots * LANES,
         8 * slots * LANES,
-    )(after(received.reshape(-1, LANES), grad_half))
+    )(after(received.reshape(-1, LANES), (grad_half, dense_units_other)))
     sent_half = gather_columns(received)
 
-    gate_dense, up_dense, sigmoid_dense, dense_units = swiglu_parts(dense_saved[0].T, dense_saved[1].T)
+    units = (jnp.where(first, dense_units, dense_units_other), jnp.where(first, dense_units_other, dense_units))
+    block = (expert_count // 2, width + STACK, LANES)
+    mine, theirs = local_kernel(
+        functools.partial(terms_kernel, runs),
+        [jax.ShapeDtypeStruct(block, F32), jax.ShapeDtypeStruct(block, BF)],
+        2 * model_width * hidden_count * tokens,
+        8 * model_width * LANES,
+        1,
+        3,
+    )(core_index, grad_half, *after(units, received))
+    expert_saved, dense_down, expert_down = after((expert_saved, dense_down, expert_down), theirs)
+    other = lax.ppermute(theirs, "core", [(0, 1), (1, 0)])
+
     gate_expert, up_expert, sigmoid_expert, expert_units = swiglu_parts(
         expert_saved[0, 0].T, expert_saved[0, 1].T
     )
-    units_other = swap(jnp.concatenate([dense_units, expert_units], axis=1))
-    dense_units_other, expert_units_other = units_other[:, :tokens], units_other[:, tokens:]
     split = local_kernel(
         functools.partial(split_kernel, runs),
         [jax.ShapeDtypeStruct((hidden_count, model_width // 2), BF)] * 2,
@@ -259,19 +271,21 @@
     dense_theirs = swap(dense_theirs)
     expert_mine, expert_theirs = split(half_index, after(expert_down[0], dense_mine))
 
-    first = half == 0
-    units = (jnp.where(first, dense_units, dense_units_other), jnp.where(first, dense_units_other, dense_units))
-    units = after(units, (dense_theirs, expert_theirs))
-    terms = scatter_terms(grad_half, units)
-    expert_theirs = swap(after(expert_theirs, terms))
-    came = lax.all_to_all(terms, EXPERT, split_axis=0, concat_axis=0, tiled=True)
-    grad_half = after(grad_half, terms)
-    cot_other = jnp.einsum("hf,fr->hr", dense_theirs, grad_half, preferred_element_type=F32)
-    cot_own = jnp.einsum("hf,fr->hr", dense_mine, grad_half, preferred_element_type=F32)
-    dense_cot = cot_own + swap(cot_other.astype(BF)).astype(F32)
-
+    pairs = local_kernel(
+        pair_kernel, jax.ShapeDtypeStruct(block, BF), mine.size, 8 * mine.size, 0, 2
+    )(mine, after(other, (dense_theirs, expert_units, expert_theirs)))
+    came = lax.all_to_all(pairs, ("zh", "x"), split_axis=0, concat_axis=0, tiled=True)
+    expert_theirs, expert_units_other = after((expert_theirs, expert_units), theirs)
+    expert_units_other = swap(expert_units_other)
+    expert_theirs = swap(expert_theirs)
+
+    grad_half = after(grad_half, pairs)
+    dense_other = jnp.einsum("hf,fr->hr", dense_theirs, grad_half, preferred_element_type=F32)
+    dense_cot = jnp.einsum("hf,fr->hr", dense_mine, grad_half, preferred_element_type=F32)
+    dense_cot = dense_cot + swap(dense_other.astype(BF)).astype(F32)
     dense_pre_grad = pre_cotangents(dense_cot, gate_dense, up_dense, sigmoid_dense).transpose(0, 2, 1)
-    sent_half = after(sent_half, dense_pre_grad)
+    dense_share = scatter_total(came, width, hidden_count)
+    sent_half = after(sent_half, (dense_pre_grad, dense_share))
 
     cot_other = jnp.einsum("hf,fr->hr", expert_theirs, sent_half, preferred_element_type=F32)
     cot_other = cot_other.astype(BF)
@@ -279,12 +293,12 @@
     cot_other = swap(cot_other)
     grad_other = jnp.einsum("hr,fr->hf", expert_units_other, sent_half, preferred_element_type=F32)
     grad_other = grad_other.astype(BF)
-    sent_half, came = after((sent_half, came), grad_other)
+    sent_half = after(sent_half, grad_other)
     grad_other = swap(grad_other)
-    dense_share = scatter_total(came, model_width // expert_count, hidden_count)
     grad_own = jnp.einsum("hr,fr->hf", expert_units, sent_half, preferred_element_type=F32).astype(BF)
     cot_own = jnp.einsum("hf,fr->hr", expert_mine, sent_half, preferred_element_type=F32)
     expert_cot = cot_own + cot_other.astype(F32)
+    expert_pre_grad = pre_cotangents(expert_cot, gate_expert, up_expert, sigmoid_expert)
     expert_down_grad = local_kernel(
         functools.partial(join_kernel, runs),
         jax.ShapeDtypeStruct((hidden_count, model_width), BF),
@@ -293,11 +307,8 @@
         1,
         2,
     )(half_index, grad_own, grad_other)[None]
-
-    expert_pre_grad = pre_cotangents(expert_cot, gate_expert, up_expert, sigmoid_expert)
     expert_pre_grad = expert_pre_grad.transpose(0, 2, 1)[None]
-    dense_down_grad = dense_share.T
-    return (expert_pre_grad, expert_down_grad, dense_pre_grad, dense_down_grad)
+    return (expert_pre_grad, expert_down_grad, dense_pre_grad, dense_share.T)
 
 
 def solution(mesh):

time: 177 us -> 180 us (1.017)
  waiting for transfers between devices: 45.5 us -> 50 us
  starting transfers between devices: 61.8 us -> 65.6 us
  other arithmetic: 7.4 us -> 4.8 us
  matrix products: 9.86 us -> 7.96 us
    ppermute x0 -> x1, starting transfers between devices: none -> 7.6 us  [body(): other = lax.ppermute(theirs, 'core', [(0, 1), (1, 0)])]
    all_to_all x1, starting transfers between devices: 17.3 us -> 12 us  [body(): lax.all_to_all(pairs, ('zh', 'x'), split_axis=0, concat_axis=0, tiled=True)]
    ppermute x6 -> x7, waiting for transfers between devices: 45.5 us -> 48.9 us  [swap(): return lax.ppermute(values, 'zl', [(0, 1), (1, 0)])]
    ppermute x6 -> x7, starting transfers between devices: 17.5 us -> 18.6 us  [swap(): return lax.ppermute(values, 'zl', [(0, 1), (1, 0)])]
    unnamed x30 -> x34, local copies, waits for them, and re-layouts: 4.73 us -> 4.71 us
  transfers between devices with their start and end apart: 10 -> 12, of which waited for: 3 -> 4; matrix products, arithmetic and copies ran while one was open for 10% -> 6% of each run, Pallas kernels for 2% -> 1%
where the time goes in v5:
time: 180 us; the launch traced here: 178 us
  starting transfers between devices  65.6 us (36%)
  waiting for transfers between devices  50 us (28%)
  blocking collectives  23.9 us (13%)
  between operations  14.4 us (8%)
  matrix products  7.96 us (4%)
  Pallas kernels  6.62 us (4%)
  other arithmetic  4.8 us (3%)
  local copies, waits for them, and re-layouts  4.71 us (3%)
    ppermute x7, waiting for transfers between devices, swap(): return lax.ppermute(values, 'zl', [(0, 1), (1, 0)])  48.9 us
    all_gather x1, blocking collectives, gather_columns(): whole = lax.all_gather(rows, 'y', axis=0, tiled=False)  23.9 us
    all_to_all x1, starting transfers between devices, body(): lax.all_to_all(outgoing, EXPERT, split_axis=0, concat_axis=0, tiled=True)  22.7 us
    ppermute x7, starting transfers between devices, swap(): return lax.ppermute(values, 'zl', [(0, 1), (1, 0)])  18.6 us
    all_to_all x1, starting transfers between devices, body(): lax.all_to_all(pairs, ('zh', 'x'), split_axis=0, concat_axis=0, tiled=True)  12 us
    ppermute x1, starting transfers between devices, body(): other = lax.ppermute(theirs, 'core', [(0, 1), (1, 0)])  7.6 us
    unnamed x34, local copies, waits for them, and re-layouts  4.71 us
    ppermute x1, starting transfers between devices, scatter_total(): other = lax.ppermute(mine, ('x', 'zl'), route)  4.6 us
  transfers between devices with their start and end apart: 12, of which 4 were waited for; matrix products, arithmetic and copies ran while one was open for 6% of the time, Pallas kernels for 1%

profile of v5, /device:TPU:1, one launch (start us, length us, event | category | flops | bytes accessed | tf_op | source)
XLA Modules:
  0.0 178.1 jit_solution(13664025238731914292)
XLA Ops:
  7.2 0.9 copy-done.7
  9.4 1.9 %shard_map.102 = bf16[1536,128]{1,0:T(8,128)(2,1)} custom-call(s32[2,256]{1,0:T(2,128)S(1)} %bitcast.182, f32[2,256]{1,0:T(2,128)S(1)} %bitcast.183, bf16[224,256]{1,0:T(8,128)(2,1)S(1)} %bitcast.181), custom_call_target="tpu_custom_call" | custom-call | flops 176160768 | bytes 393216 | tf_op jit(solution)/shard_map/pallas_call | solution.py:222
  11.3 22.7 %all-to-all-start = ((bf16[64,24,128]{2,1,0:T(8,128)(2,1)}), bf16[64,24,128]{2,1,0:T(8,128)(2,1)S(1)}, u32[]{:S(2)}, u32[]{:S(2)}) async-start(bf16[64,24,128]{2,1,0:T(8,128)(2,1)} %bitcast.5), calls=%async_computation | async-start | bytes 786432 | tf_op jit(solution)/shard_map/all_to_all | solution.py:231
  34.1 1.1 fusion.20
  35.2 4.0 %collective-permute-start = (bf16[152,256]{1,0:T(8,128)(2,1)S(1)}, bf16[152,256]{1,0:T(8,128)(2,1)}, u32[]{:S(2)}, u32[]{:S(2)}) collective-permute-start(bf16[152,256]{1,0:T(8,128)(2,1)S(1)} %fusion.20), channel_id=1, source_target_pairs={{0,1},{1,0},{2,3},{3,2},{4,5},{5,4},{6,7},{7,6},{8,9},{9,8},{10,11... | collective-permute-start | bytes 233480 | tf_op jit(solution)/shard_map/ppermute | solution.py:141
  39.2 23.9 %all-gather.grad_ref = bf16[1792,256]{1,0:T(8,128)(2,1)S(1)} all-gather(bf16[224,256]{1,0:T(8,128)(2,1)} %bitcast.180), channel_id=2, replica_groups=mesh['zh'=4,'x'=8,'core'=2,'y'=8,'zl'=2] {'y'}, dimensions={0}, use_global_device_ids=true | all-gather | bytes 1032192 | tf_op jit(solution)/shard_map/all_gather | solution.py:145
  63.1 0.7 shard_map.103
  63.9 0.7 copy-done.6
  64.7 1.1 broadcast_select_fusion
  65.8 0.7 shard_map.104
  66.5 7.6 %collective-permute-start.1 = (bf16[32,72,128]{2,1,0:T(8,128)(2,1)S(1)}, bf16[32,72,128]{2,1,0:T(8,128)(2,1)S(1)}, u32[]{:S(2)}, u32[]{:S(2)}) collective-permute-start(bf16[32,72,128]{2,1,0:T(8,128)(2,1)S(1)} %get-tuple-element.31), channel_id=1, source_target_pairs={{0,16},{16,0},{1,17},{17,1},{2,18},{18,2},{3,19},{19,3},{4,20},{20... | collective-permute-start | bytes 1769480 | tf_op jit(solution)/shard_map/ppermute | solution.py:257
  74.6 1.9 %collective-permute-start.2 = (bf16[152,1792]{1,0:T(8,128)(2,1)S(1)}, bf16[152,1792]{1,0:T(8,128)(2,1)S(1)}, u32[]{:S(2)}, u32[]{:S(2)}) collective-permute-start(bf16[152,1792]{1,0:T(8,128)(2,1)S(1)} %get-tuple-element.38), channel_id=1, source_target_pairs={{0,1},{1,0},{2,3},{3,2},{4,5},{5,4},{6,7},{7,6},{8,9},{9,8},{10,11... | collective-permute-start | bytes 1634312 | tf_op jit(solution)/shard_map/ppermute | solution.py:141
  76.9 0.8 copy-done.8
  77.9 12.6 %collective-permute-done.2 = bf16[152,1792]{1,0:T(8,128)(2,1)S(1)} collective-permute-done((bf16[152,1792]{1,0:T(8,128)(2,1)S(1)}, bf16[152,1792]{1,0:T(8,128)(2,1)S(1)}, u32[]{:S(2)}, u32[]{:S(2)}) %collective-permute-start.2) | collective-permute-done | bytes 544800 | tf_op jit(solution)/shard_map/ppermute | solution.py:141
  90.6 0.8 copy-done.16
  91.3 0.9 shard_map.107
  92.3 12.0 %all-to-all-start.1 = ((bf16[32,72,128]{2,1,0:T(8,128)(2,1)}), bf16[32,72,128]{2,1,0:T(8,128)(2,1)S(1)}, u32[]{:S(2)}, u32[]{:S(2)}) async-start(bf16[32,72,128]{2,1,0:T(8,128)(2,1)} %shard_map.107), calls=%async_computation.1 | async-start | bytes 1179648 | tf_op jit(solution)/shard_map/all_to_all | solution.py:277
  104.4 2.1 %collective-permute-start.5 = (bf16[152,1792]{1,0:T(8,128)(2,1)S(1)}, bf16[152,1792]{1,0:T(8,128)(2,1)S(1)}, u32[]{:S(2)}, u32[]{:S(2)}) collective-permute-start(bf16[152,1792]{1,0:T(8,128)(2,1)S(1)} %copy-done.9), channel_id=1, source_target_pairs={{0,1},{1,0},{2,3},{3,2},{4,5},{5,4},{6,7},{7,6},{8,9},{9,8},{10,11... | collective-permute-start | bytes 1634312 | tf_op jit(solution)/shard_map/ppermute | solution.py:141
  106.5 3.2 %collective-permute-start.6 = (bf16[152,768]{1,0:T(8,128)(2,1)S(1)}, bf16[152,768]{1,0:T(8,128)(2,1)}, u32[]{:S(2)}, u32[]{:S(2)}) collective-permute-start(bf16[152,768]{1,0:T(8,128)(2,1)S(1)} %fusion.2), channel_id=1, source_target_pairs={{0,1},{1,0},{2,3},{3,2},{4,5},{5,4},{6,7},{7,6},{8,9},{9,8},{10,11... | collective-permute-start | bytes 700424 | tf_op jit(solution)/shard_map/ppermute | solution.py:141
  109.7 1.4 convolution_convert_fusion.3
  111.1 2.1 %collective-permute-start.3 = (bf16[152,256]{1,0:T(8,128)(2,1)S(1)}, bf16[152,256]{1,0:T(8,128)(2,1)S(1)}, u32[]{:S(2)}, u32[]{:S(2)}) collective-permute-start(bf16[152,256]{1,0:T(8,128)(2,1)S(1)} %convolution_convert_fusion.3), channel_id=1, source_target_pairs={{0,1},{1,0},{2,3},{3,2},{4,5},{5,4},{6,7},{7,6},{8,9},{9,8},{10,11... | collective-permute-start | bytes 233480 | tf_op jit(solution)/shard_map/ppermute | solution.py:141
  113.5 24.4 %collective-permute-done.3 = bf16[152,256]{1,0:T(8,128)(2,1)S(1)} collective-permute-done((bf16[152,256]{1,0:T(8,128)(2,1)S(1)}, bf16[152,256]{1,0:T(8,128)(2,1)S(1)}, u32[]{:S(2)}, u32[]{:S(2)}) %collective-permute-start.3) | collective-permute-done | bytes 77856 | tf_op jit(solution)/shard_map/ppermute | solution.py:141
  138.1 4.6 %collective-permute-start.4 = (bf16[56,152]{1,0:T(8,128)(2,1)S(1)}, bf16[56,152]{1,0:T(8,128)(2,1)S(1)}, u32[]{:S(2)}, u32[]{:S(2)}) collective-permute-start(bf16[56,152]{1,0:T(8,128)(2,1)S(1)} %shard_map.108), channel_id=1, source_target_pairs={{0,65},{1,64},{32,97},{33,96},{64,1},{65,0},{96,33},{97,32},{128,1... | collective-permute-start | bytes 51080 | tf_op jit(solution)/shard_map/ppermute | solution.py:204
  143.4 1.1 collective-permute-done.4
  145.2 2.5 %convolution_convert_fusion.2 = bf16[152,768]{1,0:T(8,128)(2,1)S(1)} fusion(bf16[152,1792]{1,0:T(8,128)(2,1)S(1)} %collective-permute-done.5, bf16[1792,768]{1,0:T(8,128)(2,1)} %all-gather.4.cloned.1.call-done), kind=kOutput, calls=%fused_computation.2 | convolution fusion | flops 418498560 | bytes 3530752 | tf_op jit(solution)/shard_map/hf,fr->hr/dot_general | solution.py:290
  147.8 2.0 %convolution_convert_fusion.1 = bf16[152,1792]{1,0:T(8,128)(2,1)S(1)} fusion(bf16[152,768]{1,0:T(8,128)(2,1)} %collective-permute-done.6, bf16[1792,768]{1,0:T(8,128)(2,1)S(1)} %copy-done.12), kind=kOutput, calls=%fused_computation.1 | convolution fusion | flops 418654208 | bytes 3530752 | tf_op jit(solution)/shard_map/hr,fr->hf/dot_general | solution.py:294
  149.9 3.1 %collective-permute-start.8 = (bf16[152,1792]{1,0:T(8,128)(2,1)S(1)}, bf16[152,1792]{1,0:T(8,128)(2,1)S(1)}, u32[]{:S(2)}, u32[]{:S(2)}) collective-permute-start(bf16[152,1792]{1,0:T(8,128)(2,1)S(1)} %convolution_convert_fusion.1), channel_id=1, source_target_pairs={{0,1},{1,0},{2,3},{3,2},{4,5},{5,4},{6,7},{7,6},{8,9},{9,8},{10,11... | collective-permute-start | bytes 1634312 | tf_op jit(solution)/shard_map/ppermute | solution.py:141
  153.0 2.1 %collective-permute-start.7 = (bf16[152,768]{1,0:T(8,128)(2,1)S(1)}, bf16[152,768]{1,0:T(8,128)(2,1)S(1)}, u32[]{:S(2)}, u32[]{:S(2)}) collective-permute-start(bf16[152,768]{1,0:T(8,128)(2,1)S(1)} %convolution_convert_fusion.2), channel_id=1, source_target_pairs={{0,1},{1,0},{2,3},{3,2},{4,5},{5,4},{6,7},{7,6},{8,9},{9,8},{10,11... | collective-permute-start | bytes 700424 | tf_op jit(solution)/shard_map/ppermute | solution.py:141
  155.8 1.1 convolution_convert_fusion.own_ref
  156.9 11.8 %collective-permute-done.7 = bf16[152,768]{1,0:T(8,128)(2,1)S(1)} collective-permute-done((bf16[152,768]{1,0:T(8,128)(2,1)S(1)}, bf16[152,768]{1,0:T(8,128)(2,1)S(1)}, u32[]{:S(2)}, u32[]{:S(2)}) %collective-permute-start.7) | collective-permute-done | bytes 233504 | tf_op jit(solution)/shard_map/ppermute | solution.py:141
  169.0 0.8 maximum_bitcast_fusion
  169.8 1.4 shard_map.109
  (50 shorter events, 5.3 us)
Async XLA Ops:
  7.2 0.9 copy-start.7
  8.1 0.7 copy-start.10
  8.7 0.7 copy-start.11
  9.4 64.7 %copy-start = (bf16[152,3584]{1,0:T(8,128)(2,1)S(1)}, bf16[152,3584]{1,0:T(8,128)(2,1)}, u32[]{:S(2)}) copy-start(bf16[152,3584]{1,0:T(8,128)(2,1)} %weights_ref) | copy-start | bytes 3268612
  11.3 51.8 %all-to-all-start = ((bf16[64,24,128]{2,1,0:T(8,128)(2,1)}), bf16[64,24,128]{2,1,0:T(8,128)(2,1)S(1)}, u32[]{:S(2)}, u32[]{:S(2)}) async-start(bf16[64,24,128]{2,1,0:T(8,128)(2,1)} %bitcast.5), calls=%async_computation | async-start | bytes 786432 | tf_op jit(solution)/shard_map/all_to_all | solution.py:231
  34.1 42.4 %copy-start.1 = (bf16[1,152,3584]{2,1,0:T(8,128)(2,1)S(1)}, bf16[1,152,3584]{2,1,0:T(8,128)(2,1)}, u32[]{:S(2)}) copy-start(bf16[1,152,3584]{2,1,0:T(8,128)(2,1)} %param.10) | copy-start | bytes 3268612
  34.1 111.1 %all-gather.4.cloned.1.call-start = ((), (), s32[]{:S(2)}) async-start(), calls=%async_computation.2 | async-start | bytes 3096576 | tf_op jit(solution)/shard_map/all_gather | solution.py:145
  35.2 28.0 %collective-permute-start = (bf16[152,256]{1,0:T(8,128)(2,1)S(1)}, bf16[152,256]{1,0:T(8,128)(2,1)}, u32[]{:S(2)}, u32[]{:S(2)}) collective-permute-start(bf16[152,256]{1,0:T(8,128)(2,1)S(1)} %fusion.20), channel_id=1, source_target_pairs={{0,1},{1,0},{2,3},{3,2},{4,5},{5,4},{6,7},{7,6},{8,9},{9,8},{10,11... | collective-permute-start | bytes 233480 | tf_op jit(solution)/shard_map/ppermute | solution.py:141
  63.9 0.7 copy-start.6
  64.7 13.1 %copy-start.13 = (bf16[1,2,768,152]{2,3,1,0:T(8,128)(2,1)S(1)}, bf16[1,2,768,152]{2,3,1,0:T(8,128)(2,1)}, u32[]{:S(2)}) copy-start(bf16[1,2,768,152]{2,3,1,0:T(8,128)(2,1)} %param.11) | copy-start | bytes 1400836
  66.5 24.0 %collective-permute-start.1 = (bf16[32,72,128]{2,1,0:T(8,128)(2,1)S(1)}, bf16[32,72,128]{2,1,0:T(8,128)(2,1)S(1)}, u32[]{:S(2)}, u32[]{:S(2)}) collective-permute-start(bf16[32,72,128]{2,1,0:T(8,128)(2,1)S(1)} %get-tuple-element.31), channel_id=1, source_target_pairs={{0,16},{16,0},{1,17},{17,1},{2,18},{18,2},{3,19},{19,3},{4,20},{20... | collective-permute-start | bytes 1769480 | tf_op jit(solution)/shard_map/ppermute | solution.py:257
  74.5 16.0 %copy-start.2 = (bf16[152,1792]{1,0:T(8,128)(2,1)}, bf16[152,1792]{1,0:T(8,128)(2,1)S(1)}, u32[]{:S(2)}) copy-start(bf16[152,1792]{1,0:T(8,128)(2,1)S(1)} %get-tuple-element.34) | copy-start | bytes 1634308
  74.6 16.0 %collective-permute-start.2 = (bf16[152,1792]{1,0:T(8,128)(2,1)S(1)}, bf16[152,1792]{1,0:T(8,128)(2,1)S(1)}, u32[]{:S(2)}, u32[]{:S(2)}) collective-permute-start(bf16[152,1792]{1,0:T(8,128)(2,1)S(1)} %get-tuple-element.38), channel_id=1, source_target_pairs={{0,1},{1,0},{2,3},{3,2},{4,5},{5,4},{6,7},{7,6},{8,9},{9,8},{10,11... | collective-permute-start | bytes 1634312 | tf_op jit(solution)/shard_map/ppermute | solution.py:141
  76.9 0.8 copy-start.8
  77.7 12.8 %copy-start.4 = (bf16[152,1792]{1,0:T(8,128)(2,1)}, bf16[152,1792]{1,0:T(8,128)(2,1)S(1)}, u32[]{:S(2)}) copy-start(bf16[152,1792]{1,0:T(8,128)(2,1)S(1)} %get-tuple-element.36) | copy-start | bytes 1634308
  77.9 26.5 %copy-start.9 = (bf16[152,1792]{1,0:T(8,128)(2,1)S(1)}, bf16[152,1792]{1,0:T(8,128)(2,1)}, u32[]{:S(2)}) copy-start(bf16[152,1792]{1,0:T(8,128)(2,1)} %copy-done.8) | copy-start | bytes 1634308
  90.5 0.8 copy-start.16
  90.6 22.6 %copy-start.3 = (bf16[152,1792]{1,0:T(8,128)(2,1)S(1)}, bf16[152,1792]{1,0:T(8,128)(2,1)}, u32[]{:S(2)}) copy-start(bf16[152,1792]{1,0:T(8,128)(2,1)} %copy-done.2) | copy-start | bytes 1634308
  92.3 45.6 %copy-start.15 = (bf16[2,256,152]{1,2,0:T(8,128)(2,1)S(1)}, bf16[2,256,152]{1,2,0:T(8,128)(2,1)}, u32[]{:S(2)}) copy-start(bf16[2,256,152]{1,2,0:T(8,128)(2,1)} %param.13) | copy-start | bytes 466948
  92.3 45.7 %all-to-all-start.1 = ((bf16[32,72,128]{2,1,0:T(8,128)(2,1)}), bf16[32,72,128]{2,1,0:T(8,128)(2,1)S(1)}, u32[]{:S(2)}, u32[]{:S(2)}) async-start(bf16[32,72,128]{2,1,0:T(8,128)(2,1)} %shard_map.107), calls=%async_computation.1 | async-start | bytes 1179648 | tf_op jit(solution)/shard_map/all_to_all | solution.py:277
  104.4 40.8 %collective-permute-start.5 = (bf16[152,1792]{1,0:T(8,128)(2,1)S(1)}, bf16[152,1792]{1,0:T(8,128)(2,1)S(1)}, u32[]{:S(2)}, u32[]{:S(2)}) collective-permute-start(bf16[152,1792]{1,0:T(8,128)(2,1)S(1)} %copy-done.9), channel_id=1, source_target_pairs={{0,1},{1,0},{2,3},{3,2},{4,5},{5,4},{6,7},{7,6},{8,9},{9,8},{10,11... | collective-permute-start | bytes 1634312 | tf_op jit(solution)/shard_map/ppermute | solution.py:141
  106.5 41.2 %collective-permute-start.6 = (bf16[152,768]{1,0:T(8,128)(2,1)S(1)}, bf16[152,768]{1,0:T(8,128)(2,1)}, u32[]{:S(2)}, u32[]{:S(2)}) collective-permute-start(bf16[152,768]{1,0:T(8,128)(2,1)S(1)} %fusion.2), channel_id=1, source_target_pairs={{0,1},{1,0},{2,3},{3,2},{4,5},{5,4},{6,7},{7,6},{8,9},{9,8},{10,11... | collective-permute-start | bytes 700424 | tf_op jit(solution)/shard_map/ppermute | solution.py:141
  111.1 26.8 %collective-permute-start.3 = (bf16[152,256]{1,0:T(8,128)(2,1)S(1)}, bf16[152,256]{1,0:T(8,128)(2,1)S(1)}, u32[]{:S(2)}, u32[]{:S(2)}) collective-permute-start(bf16[152,256]{1,0:T(8,128)(2,1)S(1)} %convolution_convert_fusion.3), channel_id=1, source_target_pairs={{0,1},{1,0},{2,3},{3,2},{4,5},{5,4},{6,7},{7,6},{8,9},{9,8},{10,11... | collective-permute-start | bytes 233480 | tf_op jit(solution)/shard_map/ppermute | solution.py:141
  138.1 6.4 %collective-permute-start.4 = (bf16[56,152]{1,0:T(8,128)(2,1)S(1)}, bf16[56,152]{1,0:T(8,128)(2,1)S(1)}, u32[]{:S(2)}, u32[]{:S(2)}) collective-permute-start(bf16[56,152]{1,0:T(8,128)(2,1)S(1)} %shard_map.108), channel_id=1, source_target_pairs={{0,65},{1,64},{32,97},{33,96},{64,1},{65,0},{96,33},{97,32},{128,1... | collective-permute-start | bytes 51080 | tf_op jit(solution)/shard_map/ppermute | solution.py:204
  145.2 10.0 %copy-start.5 = (bf16[152,1792]{1,0:T(8,128)(2,1)S(1)}, bf16[152,1792]{1,0:T(8,128)(2,1)}, u32[]{:S(2)}) copy-start(bf16[152,1792]{1,0:T(8,128)(2,1)} %copy-done.4) | copy-start | bytes 1634308
  145.2 2.7 %copy-start.12 = (bf16[1792,768]{1,0:T(8,128)(2,1)S(1)}, bf16[1792,768]{1,0:T(8,128)(2,1)}, u32[]{:S(2)}) copy-start(bf16[1792,768]{1,0:T(8,128)(2,1)} %all-gather.4.cloned.1.call-done) | copy-start | bytes 8257540
  149.9 20.0 %collective-permute-start.8 = (bf16[152,1792]{1,0:T(8,128)(2,1)S(1)}, bf16[152,1792]{1,0:T(8,128)(2,1)S(1)}, u32[]{:S(2)}, u32[]{:S(2)}) collective-permute-start(bf16[152,1792]{1,0:T(8,128)(2,1)S(1)} %convolution_convert_fusion.1), channel_id=1, source_target_pairs={{0,1},{1,0},{2,3},{3,2},{4,5},{5,4},{6,7},{7,6},{8,9},{9,8},{10,11... | collective-permute-start | bytes 1634312 | tf_op jit(solution)/shard_map/ppermute | solution.py:141
  153.0 15.7 %collective-permute-start.7 = (bf16[152,768]{1,0:T(8,128)(2,1)S(1)}, bf16[152,768]{1,0:T(8,128)(2,1)S(1)}, u32[]{:S(2)}, u32[]{:S(2)}) collective-permute-start(bf16[152,768]{1,0:T(8,128)(2,1)S(1)} %convolution_convert_fusion.2), channel_id=1, source_target_pairs={{0,1},{1,0},{2,3},{3,2},{4,5},{5,4},{6,7},{7,6},{8,9},{9,8},{10,11... | collective-permute-start | bytes 700424 | tf_op jit(solution)/shard_map/ppermute | solution.py:141
  155.2 13.6 %copy-start.14 = (bf16[1,2,768,152]{2,3,1,0:T(8,128)(2,1)S(1)}, bf16[1,2,768,152]{2,3,1,0:T(8,128)(2,1)}, u32[]{:S(2)}) copy-start(bf16[1,2,768,152]{2,3,1,0:T(8,128)(2,1)} %param.11) | copy-start | bytes 1400836
Sparse Core Ops, SparseCore 0:
  64.8 50.1 all-gather.3

commit v6 on v5

--- a/solution.py
+++ b/solution.py
@@ -27,7 +27,16 @@
     )
 
 
-def dispatch_kernel(experts, capacity, routes_ref, probs_ref, grad_ref, out_ref):
+def dispatch_kernel(experts, capacity, routes_in, probs_in, grad_in, out_ref, routes_ref, probs_ref, grad_ref, sems):
+    copies = [
+        pltpu.make_async_copy(routes_in, routes_ref, sems.at[0]),
+        pltpu.make_async_copy(probs_in, probs_ref, sems.at[1]),
+        pltpu.make_async_copy(grad_in, grad_ref, sems.at[2]),
+    ]
+    for copy in copies:
+        copy.start()
+    for copy in copies:
+        copy.wait()
     tokens, features = routes_ref.shape[1], grad_ref.shape[0]
     rows = out_ref.shape[0]
     first, second = routes_ref[0:1, :], routes_ref[1:2, :]
@@ -100,25 +109,6 @@
             theirs_ref[...] = columns(1 - half)
 
 
-def join_kernel(runs, half_ref, own_ref, other_ref, out_ref):
-    width = own_ref.shape[1] // runs
-
-    def joined(low_ref, high_ref):
-        pieces = []
-        for run in range(runs):
-            for ref in (low_ref, high_ref):
-                pieces.append(ref[:, run * width : (run + 1) * width])
-        return jnp.concatenate(pieces, axis=1)
-
-    @pl.when(half_ref[0] == 0)
-    def _():
-        out_ref[...] = joined(own_ref, other_ref)
-
-    @pl.when(half_ref[0] == 1)
-    def _():
-        out_ref[...] = joined(other_ref, own_ref)
-
-
 def swiglu_parts(gate_saved, up_saved):
     gate_pre = gate_saved.astype(F32)
     up_pre = up_saved.astype(F32)
@@ -139,6 +129,11 @@
 
 def swap(values):
     return lax.ppermute(values, "zl", [(0, 1), (1, 0)])
+
+
+def in_order(own, other, axis):
+    first = lax.axis_index("zl") == 0
+    return jnp.stack([jnp.where(first, own, other), jnp.where(first, other, own)], axis=axis)
 
 
 def gather_columns(rows):
@@ -219,29 +214,47 @@
     first = half == 0
     grad_rows = grad_out.T
 
-    outgoing = local_kernel(
+    outgoing = pl.pallas_call(
         functools.partial(dispatch_kernel, expert_count, capacity),
-        jax.ShapeDtypeStruct((expert_count * 2 * capacity, LANES), BF),
-        4 * slots * tokens * feature_width,
-        4 * slots * LANES,
-        0,
-        3,
+        out_shape=jax.ShapeDtypeStruct((expert_count * 2 * capacity, LANES), BF),
+        in_specs=[pl.BlockSpec(memory_space=pl.ANY)] * 3,
+        scratch_shapes=[
+            pltpu.VMEM((2, tokens), jnp.int32),
+            pltpu.VMEM((2, tokens), F32),
+            pltpu.VMEM((feature_width, tokens), BF),
+            pltpu.SemaphoreType.DMA((3,)),
+        ],
+        compiler_params=pltpu.CompilerParams(vmem_limit_bytes=VMEM_LIMIT),
+        cost_estimate=pl.CostEstimate(
+            flops=4 * slots * tokens * feature_width, bytes_accessed=4 * slots * LANES, transcendentals=0
+        ),
     )(routes.T, probs.T, grad_rows)
     outgoing = outgoing.reshape(expert_count, 2 * capacity, LANES)
     received = lax.all_to_all(outgoing, EXPERT, split_axis=0, concat_axis=0, tiled=True)
-
-    dense_saved = after(dense_saved, outgoing)
-    gate_dense, up_dense, sigmoid_dense, dense_units = swiglu_parts(dense_saved[0].T, dense_saved[1].T)
-    dense_units_other = swap(dense_units)
-    grad_half = gather_columns(after(grad_rows, (outgoing, dense_units)))
-
-    received = local_kernel(
+    own = local_kernel(
         functools.partial(arrange_kernel, capacity),
         jax.ShapeDtypeStruct((feature_width, slots), BF),
         4 * slots * slots * LANES,
         8 * slots * LANES,
-    )(after(received.reshape(-1, LANES), (grad_half, dense_units_other)))
-    sent_half = gather_columns(received)
+    )(received.reshape(-1, LANES))
+    other = swap(own)
+
+    dense_saved, dense_down = after((dense_saved, dense_down), own)
+    gate_dense, up_dense, sigmoid_dense, dense_units = swiglu_parts(dense_saved[0].T, dense_saved[1].T)
+    dense_mine, dense_theirs = local_kernel(
+        functools.partial(split_kernel, runs),
+        [jax.ShapeDtypeStruct((hidden_count, model_width // 2), BF)] * 2,
+        0,
+        4 * hidden_count * model_width,
+        1,
+        1,
+    )(half_index, dense_down)
+
+    pair = in_order(own, after(other, (dense_units, dense_theirs)), 0).reshape(-1, slots)
+    sent = gather_columns(pair)
+    dense_units_other, dense_theirs = swap(after(dense_units, pair)), swap(after(dense_theirs, pair))
+
+    grad_half = gather_columns(after(grad_rows, (pair, dense_mine, dense_units)))
 
     units = (jnp.where(first, dense_units, dense_units_other), jnp.where(first, dense_units_other, dense_units))
     block = (expert_count // 2, width + STACK, LANES)
@@ -252,62 +265,29 @@
         8 * model_width * LANES,
         1,
         3,
-    )(core_index, grad_half, *after(units, received))
-    expert_saved, dense_down, expert_down = after((expert_saved, dense_down, expert_down), theirs)
-    other = lax.ppermute(theirs, "core", [(0, 1), (1, 0)])
-
+    )(core_index, grad_half, *after(units, (own, dense_theirs)))
+    theirs = lax.ppermute(theirs, "core", [(0, 1), (1, 0)])
+
+    pairs = local_kernel(
+        pair_kernel, jax.ShapeDtypeStruct(block, BF), mine.size, 8 * mine.size, 0, 2
+    )(mine, theirs)
+    came = lax.all_to_all(pairs, ("zh", "x"), split_axis=0, concat_axis=0, tiled=True)
+    expert_saved, expert_down = after((expert_saved, expert_down), pairs)
     gate_expert, up_expert, sigmoid_expert, expert_units = swiglu_parts(
         expert_saved[0, 0].T, expert_saved[0, 1].T
     )
-    split = local_kernel(
-        functools.partial(split_kernel, runs),
-        [jax.ShapeDtypeStruct((hidden_count, model_width // 2), BF)] * 2,
-        0,
-        4 * hidden_count * model_width,
-        1,
-        1,
-    )
-    dense_mine, dense_theirs = split(half_index, dense_down)
-    dense_theirs = swap(dense_theirs)
-    expert_mine, expert_theirs = split(half_index, after(expert_down[0], dense_mine))
-
-    pairs = local_kernel(
-        pair_kernel, jax.ShapeDtypeStruct(block, BF), mine.size, 8 * mine.size, 0, 2
-    )(mine, after(other, (dense_theirs, expert_units, expert_theirs)))
-    came = lax.all_to_all(pairs, ("zh", "x"), split_axis=0, concat_axis=0, tiled=True)
-    expert_theirs, expert_units_other = after((expert_theirs, expert_units), theirs)
-    expert_units_other = swap(expert_units_other)
-    expert_theirs = swap(expert_theirs)
-
     grad_half = after(grad_half, pairs)
     dense_other = jnp.einsum("hf,fr->hr", dense_theirs, grad_half, preferred_element_type=F32)
     dense_cot = jnp.einsum("hf,fr->hr", dense_mine, grad_half, preferred_element_type=F32)
     dense_cot = dense_cot + swap(dense_other.astype(BF)).astype(F32)
     dense_pre_grad = pre_cotangents(dense_cot, gate_dense, up_dense, sigmoid_dense).transpose(0, 2, 1)
     dense_share = scatter_total(came, width, hidden_count)
-    sent_half = after(sent_half, (dense_pre_grad, dense_share))
-
-    cot_other = jnp.einsum("hf,fr->hr", expert_theirs, sent_half, preferred_element_type=F32)
-    cot_other = cot_other.astype(BF)
-    sent_half = after(sent_half, cot_other)
-    cot_other = swap(cot_other)
-    grad_other = jnp.einsum("hr,fr->hf", expert_units_other, sent_half, preferred_element_type=F32)
-    grad_other = grad_other.astype(BF)
-    sent_half = after(sent_half, grad_other)
-    grad_other = swap(grad_other)
-    grad_own = jnp.einsum("hr,fr->hf", expert_units, sent_half, preferred_element_type=F32).astype(BF)
-    cot_own = jnp.einsum("hf,fr->hr", expert_mine, sent_half, preferred_element_type=F32)
-    expert_cot = cot_own + cot_other.astype(F32)
+    sent = after(sent, (dense_pre_grad, dense_share, expert_units))
+    expert_grad = jnp.einsum("hr,fr->hf", expert_units, sent, preferred_element_type=F32)
+    expert_cot = jnp.einsum("hf,fr->hr", expert_down[0], sent, preferred_element_type=F32)
     expert_pre_grad = pre_cotangents(expert_cot, gate_expert, up_expert, sigmoid_expert)
-    expert_down_grad = local_kernel(
-        functools.partial(join_kernel, runs),
-        jax.ShapeDtypeStruct((hidden_count, model_width), BF),
-        0,
-        4 * hidden_count * model_width,
-        1,
-        2,
-    )(half_index, grad_own, grad_other)[None]
     expert_pre_grad = expert_pre_grad.transpose(0, 2, 1)[None]
+    expert_down_grad = expert_grad.astype(BF)[None]
     return (expert_pre_grad, expert_down_grad, dense_pre_grad, dense_share.T)
 
 

time: 180 us -> 158 us (0.88)
  blocking collectives: 23.9 us -> 65.5 us
  waiting for transfers between devices: 50 us -> 18.5 us
  starting transfers between devices: 65.6 us -> 34.1 us
  Pallas kernels: 6.62 us -> 4.28 us
  local copies, waits for them, and re-layouts: 4.71 us -> 2.43 us
  matrix products: 7.96 us -> 10.1 us
    all_to_all x0 -> x1, blocking collectives: none -> 38.8 us  [body(): lax.all_to_all(outgoing, EXPERT, split_axis=0, concat_axis=0, tiled=True)]
    ppermute x7 -> x4, waiting for transfers between devices: 48.9 us -> 13.3 us  [swap(): return lax.ppermute(values, 'zl', [(0, 1), (1, 0)])]
    all_to_all x1 -> x0, starting transfers between devices: 22.7 us -> none  [body(): lax.all_to_all(outgoing, EXPERT, split_axis=0, concat_axis=0, tiled=True)]
    ppermute x7 -> x4, starting transfers between devices: 18.6 us -> 12 us  [swap(): return lax.ppermute(values, 'zl', [(0, 1), (1, 0)])]
    all_to_all x1, starting transfers between devices: 12 us -> 5.94 us  [body(): lax.all_to_all(pairs, ('zh', 'x'), split_axis=0, concat_axis=0, tiled=True)]
    all_to_all x1, waiting for transfers between devices: 0.01 us -> 3.49 us  [body(): lax.all_to_all(pairs, ('zh', 'x'), split_axis=0, concat_axis=0, tiled=True)]
    all_gather x1, blocking collectives: 23.9 us -> 26.7 us  [gather_columns(): whole = lax.all_gather(rows, 'y', axis=0, tiled=False)]
    pallas_call x4 -> x2, Pallas kernels: 4.11 us -> 1.72 us  [the longest x1 1.31 us: body(): pl.pallas_call(functools.partial(dispatch_kernel, expert_count, capacity)...]
  transfers between devices with their start and end apart: 12 -> 8, of which waited for: 4 -> 4; matrix products, arithmetic and copies ran while one was open for 6% -> 4% of each run, Pallas kernels for 1% -> 1%
where the time goes in v6:
time: 158 us; the launch traced here: 155 us
  blocking collectives  65.5 us (41%)
  starting transfers between devices  34.1 us (22%)
  waiting for transfers between devices  18.5 us (12%)
  between operations  14.3 us (9%)
  matrix products  10.1 us (6%)
  other arithmetic  6.28 us (4%)
  Pallas kernels  4.28 us (3%)
  local copies, waits for them, and re-layouts  2.43 us (2%)
    all_to_all x1, blocking collectives, body(): lax.all_to_all(outgoing, EXPERT, split_axis=0, concat_axis=0, tiled=True)  38.8 us
    all_gather x1, blocking collectives, gather_columns(): whole = lax.all_gather(rows, 'y', axis=0, tiled=False)  26.7 us
    ppermute x4, waiting for transfers between devices, swap(): return lax.ppermute(values, 'zl', [(0, 1), (1, 0)])  13.3 us
    ppermute x4, starting transfers between devices, swap(): return lax.ppermute(values, 'zl', [(0, 1), (1, 0)])  12 us
    ppermute x1, starting transfers between devices, body(): theirs = lax.ppermute(theirs, 'core', [(0, 1), (1, 0)])  9.15 us
    ppermute x1, starting transfers between devices, scatter_total(): other = lax.ppermute(mine, ('x', 'zl'), route)  6.94 us
    all_to_all x1, starting transfers between devices, body(): lax.all_to_all(pairs, ('zh', 'x'), split_axis=0, concat_axis=0, tiled=True)  5.94 us
    dot_general x1, matrix products, body(): jnp.einsum('hr,fr->hf', expert_units, sent, preferred_element_type=F32)  5.63 us
  transfers between devices with their start and end apart: 8, of which 4 were waited for; matrix products, arithmetic and copies ran while one was open for 4% of the time, Pallas kernels for 1%

profile of v6, /device:TPU:1, one launch (start us, length us, event | category | flops | bytes accessed | tf_op | source)
XLA Modules:
  0.0 155.4 jit_solution(11207946564774847611)
XLA Ops:
  7.2 1.0 copy-done.2
  8.3 0.7 copy-done.5
  9.0 0.7 copy-done.6
  9.6 1.3 shard_map.102
  11.0 38.8 %all_to_all.10 = bf16[64,24,128]{2,1,0:T(8,128)(2,1)S(1)} all-to-all(bf16[64,24,128]{2,1,0:T(8,128)(2,1)S(1)} %bitcast.186), channel_id=1, replica_groups=mesh['zh'=4,'x'=8,'core'=2,'y'=8,'zl'=2] {'zh','x','core'}, dimensions={0} | all-to-all | bytes 786432 | tf_op jit(solution)/shard_map/all_to_all | solution.py:233
  49.8 0.7 shard_map.103
  50.5 3.4 %collective-permute-start = (bf16[224,768]{1,0:T(8,128)(2,1)S(1)}, bf16[224,768]{1,0:T(8,128)(2,1)}, u32[]{:S(2)}, u32[]{:S(2)}) collective-permute-start(bf16[224,768]{1,0:T(8,128)(2,1)S(1)} %shard_map.103), channel_id=1, source_target_pairs={{0,1},{1,0},{2,3},{3,2},{4,5},{5,4},{6,7},{7,6},{8,9},{9,8},{10,11... | collective-permute-start | bytes 1032200 | tf_op jit(solution)/shard_map/ppermute | solution.py:131
  53.9 0.4 shard_map.104
  54.4 6.7 %collective-permute-done = bf16[224,768]{1,0:T(8,128)(2,1)} collective-permute-done((bf16[224,768]{1,0:T(8,128)(2,1)S(1)}, bf16[224,768]{1,0:T(8,128)(2,1)}, u32[]{:S(2)}, u32[]{:S(2)}) %collective-permute-start) | collective-permute-done | bytes 344096 | tf_op jit(solution)/shard_map/ppermute | solution.py:131
  61.1 1.0 select_bitcast_fusion.1
  62.2 0.9 pad_maximum_fusion
  63.1 3.1 %collective-permute-start.1 = (bf16[152,256]{1,0:T(8,128)(2,1)S(1)}, bf16[152,256]{1,0:T(8,128)(2,1)S(1)}, u32[]{:S(2)}, u32[]{:S(2)}) collective-permute-start(bf16[152,256]{1,0:T(8,128)(2,1)S(1)} %fusion.23), channel_id=1, source_target_pairs={{0,1},{1,0},{2,3},{3,2},{4,5},{5,4},{6,7},{7,6},{8,9},{9,8},{10,11... | collective-permute-start | bytes 233480 | tf_op jit(solution)/shard_map/ppermute | solution.py:131
  66.2 2.2 %collective-permute-start.2 = (bf16[152,1792]{1,0:T(8,128)(2,1)}, bf16[152,1792]{1,0:T(8,128)(2,1)}, u32[]{:S(2)}, u32[]{:S(2)}) collective-permute-start(bf16[152,1792]{1,0:T(8,128)(2,1)} %copy-done.4), channel_id=1, source_target_pairs={{0,1},{1,0},{2,3},{3,2},{4,5},{5,4},{6,7},{7,6},{8,9},{9,8},{10,11... | collective-permute-start | bytes 1634312 | tf_op jit(solution)/shard_map/ppermute | solution.py:131
  68.4 26.7 %all-gather.grad_ref = bf16[1792,256]{1,0:T(8,128)(2,1)S(1)} all-gather(bf16[224,256]{1,0:T(8,128)(2,1)S(1)} %bitcast.188), channel_id=2, replica_groups=mesh['zh'=4,'x'=8,'core'=2,'y'=8,'zl'=2] {'y'}, dimensions={0}, use_global_device_ids=true | all-gather | bytes 1032192 | tf_op jit(solution)/shard_map/all_gather | solution.py:140
  95.2 0.7 shard_map.105
  96.0 9.1 %collective-permute-start.3 = (bf16[32,72,128]{2,1,0:T(8,128)(2,1)S(1)}, bf16[32,72,128]{2,1,0:T(8,128)(2,1)S(1)}, u32[]{:S(2)}, u32[]{:S(2)}) collective-permute-start(bf16[32,72,128]{2,1,0:T(8,128)(2,1)S(1)} %get-tuple-element.31), channel_id=1, source_target_pairs={{0,16},{16,0},{1,17},{17,1},{2,18},{18,2},{3,19},{19,3},{4,20},{20... | collective-permute-start | bytes 1769480 | tf_op jit(solution)/shard_map/ppermute | solution.py:269
  105.1 1.6 %collective-permute-done.3.other_ref = bf16[32,72,128]{2,1,0:T(8,128)(2,1)S(1)} collective-permute-done((bf16[32,72,128]{2,1,0:T(8,128)(2,1)S(1)}, bf16[32,72,128]{2,1,0:T(8,128)(2,1)S(1)}, u32[]{:S(2)}, u32[]{:S(2)}) %collective-permute-start.3) | collective-permute-done | bytes 589856 | tf_op jit(solution)/shard_map/ppermute | solution.py:269
  106.7 1.0 shard_map.106
  107.7 5.9 %all-to-all-start.1 = ((bf16[32,72,128]{2,1,0:T(8,128)(2,1)}), bf16[32,72,128]{2,1,0:T(8,128)(2,1)S(1)}, u32[]{:S(2)}, u32[]{:S(2)}) async-start(bf16[32,72,128]{2,1,0:T(8,128)(2,1)} %shard_map.106), calls=%async_computation.1 | async-start | bytes 1179648 | tf_op jit(solution)/shard_map/all_to_all | solution.py:274
  113.7 1.4 convolution_convert_fusion.1
  115.1 3.3 %collective-permute-start.4 = (bf16[152,256]{1,0:T(8,128)(2,1)S(1)}, bf16[152,256]{1,0:T(8,128)(2,1)S(1)}, u32[]{:S(2)}, u32[]{:S(2)}) collective-permute-start(bf16[152,256]{1,0:T(8,128)(2,1)S(1)} %convolution_convert_fusion.1), channel_id=1, source_target_pairs={{0,1},{1,0},{2,3},{3,2},{4,5},{5,4},{6,7},{7,6},{8,9},{9,8},{10,11... | collective-permute-start | bytes 233480 | tf_op jit(solution)/shard_map/ppermute | solution.py:131
  118.4 1.2 fusion.5
  119.7 6.6 %collective-permute-done.4 = bf16[152,256]{1,0:T(8,128)(2,1)S(1)} collective-permute-done((bf16[152,256]{1,0:T(8,128)(2,1)S(1)}, bf16[152,256]{1,0:T(8,128)(2,1)S(1)}, u32[]{:S(2)}, u32[]{:S(2)}) %collective-permute-start.4) | collective-permute-done | bytes 77856 | tf_op jit(solution)/shard_map/ppermute | solution.py:131
  126.3 1.9 %fusion.38 = (bf16[1,152,256]{2,1,0:T(8,128)(2,1)S(1)}, bf16[1,152,256]{2,1,0:T(8,128)(2,1)}) fusion(bf16[2,256,152]{1,2,0:T(8,128)(2,1)} %param.13, bf16[152,256]{1,0:T(8,128)(2,1)S(1)} %collective-permute-done.4, bf16[152,1792]{1,0:T(8,128)(2,1)S(1)} %get-tuple-element.24, bf16[1792,256]{1,0:T(8,128)(2,1)S(1)} %all-gather.grad_ref), kind=kOutput, calls=%fused_computation.52 | convolution fusion | flops 140122112 | bytes 1851392 | tf_op jit(solution)/shard_map/hf,fr->hr/dot_general | solution.py:281
  128.2 3.5 %all-to-all-done.1.came_ref = bf16[32,72,128]{2,1,0:T(8,128)(2,1)S(1)} async-done(((bf16[32,72,128]{2,1,0:T(8,128)(2,1)}), bf16[32,72,128]{2,1,0:T(8,128)(2,1)S(1)}, u32[]{:S(2)}, u32[]{:S(2)}) %all-to-all-start.1) | async-done | bytes 589856 | tf_op jit(solution)/shard_map/all_to_all | solution.py:274
  131.7 0.1 shard_map.107
  131.8 6.9 %collective-permute-start.5 = (bf16[56,152]{1,0:T(8,128)(2,1)S(1)}, bf16[56,152]{1,0:T(8,128)(2,1)S(1)}, u32[]{:S(2)}, u32[]{:S(2)}) collective-permute-start(bf16[56,152]{1,0:T(8,128)(2,1)S(1)} %shard_map.107), channel_id=1, source_target_pairs={{0,65},{1,64},{32,97},{33,96},{64,1},{65,0},{96,33},{97,32},{128,1... | collective-permute-start | bytes 51080 | tf_op jit(solution)/shard_map/ppermute | solution.py:199
  138.7 1.6 %maximum_bitcast_fusion.1 = bf16[2,256,152]{1,2,0:T(8,128)(2,1)} fusion(bf16[1,152,256]{2,1,0:T(8,128)(2,1)} %get-tuple-element.41, bf16[1,152,256]{2,1,0:T(8,128)(2,1)S(1)} %get-tuple-element.40), kind=kLoop, calls=%fused_computation.30 | loop fusion | flops 77824 | bytes 311296 | tf_op jit(solution)/shard_map/transpose | solution.py:283
  140.3 0.6 broadcast_select_fusion.2
  140.9 5.6 %fusion = bf16[1,152,3584]{2,1,0:T(8,128)(2,1)} fusion(bf16[152,768]{1,0:T(8,128)(2,1)S(1)} %fusion.5, bf16[3584,768]{1,0:T(8,128)(2,1)} %bitcast.191), kind=kOutput, calls=%fused_computation.1 | convolution fusion | flops 837308416 | bytes 6828032 | tf_op jit(solution)/shard_map/hr,fr->hf/dot_general | solution.py:286
  146.6 1.1 fusion.20
  147.7 0.8 maximum_bitcast_fusion
  (25 shorter events, 0.2 us)
Async XLA Ops:
  7.2 139.4 %copy-start = (bf16[1,152,3584]{2,1,0:T(8,128)(2,1)S(1)}, bf16[1,152,3584]{2,1,0:T(8,128)(2,1)}, u32[]{:S(2)}) copy-start(bf16[1,152,3584]{2,1,0:T(8,128)(2,1)} %param.10) | copy-start | bytes 3268612
  7.2 46.7 %copy-start.1 = (bf16[152,3584]{1,0:T(8,128)(2,1)S(1)}, bf16[152,3584]{1,0:T(8,128)(2,1)}, u32[]{:S(2)}) copy-start(bf16[152,3584]{1,0:T(8,128)(2,1)} %weights_ref) | copy-start | bytes 3268612
  7.2 133.7 %all-gather.3.cloned.1.call-start = ((), (), s32[]{:S(2)}) async-start(), calls=%async_computation.2 | async-start | bytes 6193152 | tf_op jit(solution)/shard_map/all_gather | solution.py:140
  7.2 1.0 copy-start.2
  8.3 0.7 copy-start.5
  9.0 0.7 copy-start.6
  9.6 44.7 %copy-start.8 = (bf16[2,256,152]{1,2,0:T(8,128)(2,1)S(1)}, bf16[2,256,152]{1,2,0:T(8,128)(2,1)}, u32[]{:S(2)}) copy-start(bf16[2,256,152]{1,2,0:T(8,128)(2,1)} %param.13) | copy-start | bytes 466948
  50.5 10.6 %collective-permute-start = (bf16[224,768]{1,0:T(8,128)(2,1)S(1)}, bf16[224,768]{1,0:T(8,128)(2,1)}, u32[]{:S(2)}, u32[]{:S(2)}) collective-permute-start(bf16[224,768]{1,0:T(8,128)(2,1)S(1)} %shard_map.103), channel_id=1, source_target_pairs={{0,1},{1,0},{2,3},{3,2},{4,5},{5,4},{6,7},{7,6},{8,9},{9,8},{10,11... | collective-permute-start | bytes 1032200 | tf_op jit(solution)/shard_map/ppermute | solution.py:131
  53.9 14.5 %copy-start.3 = (bf16[256,224]{0,1:T(8,128)(2,1)S(1)}, bf16[256,224]{0,1:T(8,128)(2,1)}, u32[]{:S(2)}) copy-start(bf16[256,224]{0,1:T(8,128)(2,1)} %param.7) | copy-start | bytes 344068
  54.3 7.8 %copy-start.4 = (bf16[152,1792]{1,0:T(8,128)(2,1)}, bf16[152,1792]{1,0:T(8,128)(2,1)S(1)}, u32[]{:S(2)}) copy-start(bf16[152,1792]{1,0:T(8,128)(2,1)S(1)} %get-tuple-element.27) | copy-start | bytes 1634308
  63.1 32.0 %collective-permute-start.1 = (bf16[152,256]{1,0:T(8,128)(2,1)S(1)}, bf16[152,256]{1,0:T(8,128)(2,1)S(1)}, u32[]{:S(2)}, u32[]{:S(2)}) collective-permute-start(bf16[152,256]{1,0:T(8,128)(2,1)S(1)} %fusion.23), channel_id=1, source_target_pairs={{0,1},{1,0},{2,3},{3,2},{4,5},{5,4},{6,7},{7,6},{8,9},{9,8},{10,11... | collective-permute-start | bytes 233480 | tf_op jit(solution)/shard_map/ppermute | solution.py:131
  66.2 29.0 %collective-permute-start.2 = (bf16[152,1792]{1,0:T(8,128)(2,1)}, bf16[152,1792]{1,0:T(8,128)(2,1)}, u32[]{:S(2)}, u32[]{:S(2)}) collective-permute-start(bf16[152,1792]{1,0:T(8,128)(2,1)} %copy-done.4), channel_id=1, source_target_pairs={{0,1},{1,0},{2,3},{3,2},{4,5},{5,4},{6,7},{7,6},{8,9},{9,8},{10,11... | collective-permute-start | bytes 1634312 | tf_op jit(solution)/shard_map/ppermute | solution.py:131
  96.0 10.8 %collective-permute-start.3 = (bf16[32,72,128]{2,1,0:T(8,128)(2,1)S(1)}, bf16[32,72,128]{2,1,0:T(8,128)(2,1)S(1)}, u32[]{:S(2)}, u32[]{:S(2)}) collective-permute-start(bf16[32,72,128]{2,1,0:T(8,128)(2,1)S(1)} %get-tuple-element.31), channel_id=1, source_target_pairs={{0,16},{16,0},{1,17},{17,1},{2,18},{18,2},{3,19},{19,3},{4,20},{20... | collective-permute-start | bytes 1769480 | tf_op jit(solution)/shard_map/ppermute | solution.py:269
  107.7 24.0 %all-to-all-start.1 = ((bf16[32,72,128]{2,1,0:T(8,128)(2,1)}), bf16[32,72,128]{2,1,0:T(8,128)(2,1)S(1)}, u32[]{:S(2)}, u32[]{:S(2)}) async-start(bf16[32,72,128]{2,1,0:T(8,128)(2,1)} %shard_map.106), calls=%async_computation.1 | async-start | bytes 1179648 | tf_op jit(solution)/shard_map/all_to_all | solution.py:274
  115.1 11.2 %collective-permute-start.4 = (bf16[152,256]{1,0:T(8,128)(2,1)S(1)}, bf16[152,256]{1,0:T(8,128)(2,1)S(1)}, u32[]{:S(2)}, u32[]{:S(2)}) collective-permute-start(bf16[152,256]{1,0:T(8,128)(2,1)S(1)} %convolution_convert_fusion.1), channel_id=1, source_target_pairs={{0,1},{1,0},{2,3},{3,2},{4,5},{5,4},{6,7},{7,6},{8,9},{9,8},{10,11... | collective-permute-start | bytes 233480 | tf_op jit(solution)/shard_map/ppermute | solution.py:131
  131.8 8.5 %collective-permute-start.5 = (bf16[56,152]{1,0:T(8,128)(2,1)S(1)}, bf16[56,152]{1,0:T(8,128)(2,1)S(1)}, u32[]{:S(2)}, u32[]{:S(2)}) collective-permute-start(bf16[56,152]{1,0:T(8,128)(2,1)S(1)} %shard_map.107), channel_id=1, source_target_pairs={{0,65},{1,64},{32,97},{33,96},{64,1},{65,0},{96,33},{97,32},{128,1... | collective-permute-start | bytes 51080 | tf_op jit(solution)/shard_map/ppermute | solution.py:199
  140.9 5.6 %copy-start.7 = (bf16[8,448,768]{2,1,0:T(8,128)(2,1)S(1)}, bf16[8,448,768]{2,1,0:T(8,128)(2,1)}, u32[]{:S(2)}) copy-start(bf16[8,448,768]{2,1,0:T(8,128)(2,1)} %all-gather.3.cloned.1.call-done) | copy-start | bytes 16515076
  140.9 5.6 %copy-start.9 = (bf16[1,2,768,152]{2,3,1,0:T(8,128)(2,1)S(1)}, bf16[1,2,768,152]{2,3,1,0:T(8,128)(2,1)}, u32[]{:S(2)}) copy-start(bf16[1,2,768,152]{2,3,1,0:T(8,128)(2,1)} %param.11) | copy-start | bytes 1400836
Sparse Core Ops, SparseCore 0:
  63.2 76.1 all-gather.2

commit v7 on v6

--- a/solution.py
+++ b/solution.py
@@ -92,21 +92,40 @@
             ]
 
 
-def split_kernel(runs, half_ref, weights_ref, mine_ref, theirs_ref):
-    width = weights_ref.shape[1] // (2 * runs)
-
-    def columns(half):
+def split_kernel(runs, half_ref, dense_ref, expert_ref, mine_ref, theirs_ref):
+    width = dense_ref.shape[1] // (2 * runs)
+
+    def columns(ref, half):
         return jnp.concatenate(
-            [weights_ref[:, (2 * run + half) * width : (2 * run + half + 1) * width] for run in range(runs)],
-            axis=1,
+            [ref[:, (2 * run + half) * width : (2 * run + half + 1) * width] for run in range(runs)], axis=1
         )
 
     for half in range(2):
 
         @pl.when(half_ref[0] == half)
         def _():
-            mine_ref[...] = columns(half)
-            theirs_ref[...] = columns(1 - half)
+            for index, ref in enumerate((dense_ref, expert_ref)):
+                mine_ref[index] = columns(ref, half)
+                theirs_ref[index] = columns(ref, 1 - half)
+
+
+def join_kernel(runs, half_ref, own_ref, other_ref, out_ref):
+    width = own_ref.shape[1] // runs
+
+    def joined(low_ref, high_ref):
+        pieces = []
+        for run in range(runs):
+            for ref in (low_ref, high_ref):
+                pieces.append(ref[:, run * width : (run + 1) * width])
+        return jnp.concatenate(pieces, axis=1)
+
+    @pl.when(half_ref[0] == 0)
+    def _():
+        out_ref[...] = joined(own_ref, other_ref)
+
+    @pl.when(half_ref[0] == 1)
+    def _():
+        out_ref[...] = joined(other_ref, own_ref)
 
 
 def swiglu_parts(gate_saved, up_saved):
@@ -129,11 +148,6 @@
 
 def swap(values):
     return lax.ppermute(values, "zl", [(0, 1), (1, 0)])
-
-
-def in_order(own, other, axis):
-    first = lax.axis_index("zl") == 0
-    return jnp.stack([jnp.where(first, own, other), jnp.where(first, other, own)], axis=axis)
 
 
 def gather_columns(rows):
@@ -237,24 +251,25 @@
         4 * slots * slots * LANES,
         8 * slots * LANES,
     )(received.reshape(-1, LANES))
-    other = swap(own)
-
-    dense_saved, dense_down = after((dense_saved, dense_down), own)
+    sent_half = gather_columns(own)
+
+    dense_saved, expert_saved, dense_down, expert_down = after(
+        (dense_saved, expert_saved, dense_down, expert_down), own
+    )
     gate_dense, up_dense, sigmoid_dense, dense_units = swiglu_parts(dense_saved[0].T, dense_saved[1].T)
-    dense_mine, dense_theirs = local_kernel(
-        functools.partial(split_kernel, runs),
-        [jax.ShapeDtypeStruct((hidden_count, model_width // 2), BF)] * 2,
-        0,
-        4 * hidden_count * model_width,
-        1,
-        1,
-    )(half_index, dense_down)
-
-    pair = in_order(own, after(other, (dense_units, dense_theirs)), 0).reshape(-1, slots)
-    sent = gather_columns(pair)
-    dense_units_other, dense_theirs = swap(after(dense_units, pair)), swap(after(dense_theirs, pair))
-
-    grad_half = gather_columns(after(grad_rows, (pair, dense_mine, dense_units)))
+    gate_expert, up_expert, sigmoid_expert, expert_units = swiglu_parts(
+        expert_saved[0, 0].T, expert_saved[0, 1].T
+    )
+    weights = jax.ShapeDtypeStruct((2, hidden_count, model_width // 2), BF)
+    weights_mine, weights_theirs = local_kernel(
+        functools.partial(split_kernel, runs), [weights, weights], 0, 8 * hidden_count * model_width, 1, 2
+    )(half_index, dense_down, expert_down[0])
+    both_units = jnp.concatenate([dense_units, expert_units], axis=1)
+    units_other = swap(both_units)
+    dense_units_other, expert_units_other = units_other[:, :tokens], units_other[:, tokens:]
+    weights_swapped = swap(weights_theirs)
+
+    grad_half = gather_columns(after(grad_rows, (own, both_units, weights_theirs)))
 
     units = (jnp.where(first, dense_units, dense_units_other), jnp.where(first, dense_units_other, dense_units))
     block = (expert_count // 2, width + STACK, LANES)
@@ -265,29 +280,45 @@
         8 * model_width * LANES,
         1,
         3,
-    )(core_index, grad_half, *after(units, (own, dense_theirs)))
+    )(core_index, grad_half, *units)
     theirs = lax.ppermute(theirs, "core", [(0, 1), (1, 0)])
 
     pairs = local_kernel(
         pair_kernel, jax.ShapeDtypeStruct(block, BF), mine.size, 8 * mine.size, 0, 2
-    )(mine, theirs)
+    )(mine, after(theirs, weights_swapped))
     came = lax.all_to_all(pairs, ("zh", "x"), split_axis=0, concat_axis=0, tiled=True)
-    expert_saved, expert_down = after((expert_saved, expert_down), pairs)
-    gate_expert, up_expert, sigmoid_expert, expert_units = swiglu_parts(
-        expert_saved[0, 0].T, expert_saved[0, 1].T
-    )
     grad_half = after(grad_half, pairs)
-    dense_other = jnp.einsum("hf,fr->hr", dense_theirs, grad_half, preferred_element_type=F32)
-    dense_cot = jnp.einsum("hf,fr->hr", dense_mine, grad_half, preferred_element_type=F32)
-    dense_cot = dense_cot + swap(dense_other.astype(BF)).astype(F32)
+    dense_other = jnp.einsum("hf,fr->hr", weights_swapped[0], grad_half, preferred_element_type=F32)
+    dense_other = dense_other.astype(BF)
+    dense_cot = jnp.einsum("hf,fr->hr", weights_mine[0], grad_half, preferred_element_type=F32)
+    sent_half = after(sent_half, (dense_other, dense_cot))
+    dense_other = swap(dense_other)
+
+    grad_other = jnp.einsum("hr,fr->hf", expert_units_other, sent_half, preferred_element_type=F32)
+    grad_other = grad_other.astype(BF)
+    sent_half = after(sent_half, grad_other)
+    grad_other = swap(grad_other)
+    cot_other = jnp.einsum("hf,fr->hr", weights_swapped[1], sent_half, preferred_element_type=F32)
+    cot_other = cot_other.astype(BF)
+    sent_half, came, dense_other = after((sent_half, came, dense_other), cot_other)
+    cot_other = swap(cot_other)
+    grad_own = jnp.einsum("hr,fr->hf", expert_units, sent_half, preferred_element_type=F32).astype(BF)
+    cot_own = jnp.einsum("hf,fr->hr", weights_mine[1], sent_half, preferred_element_type=F32)
+
+    dense_share = scatter_total(came, width, hidden_count)
+    dense_cot = dense_cot + dense_other.astype(F32)
     dense_pre_grad = pre_cotangents(dense_cot, gate_dense, up_dense, sigmoid_dense).transpose(0, 2, 1)
-    dense_share = scatter_total(came, width, hidden_count)
-    sent = after(sent, (dense_pre_grad, dense_share, expert_units))
-    expert_grad = jnp.einsum("hr,fr->hf", expert_units, sent, preferred_element_type=F32)
-    expert_cot = jnp.einsum("hf,fr->hr", expert_down[0], sent, preferred_element_type=F32)
+    expert_cot = cot_own + cot_other.astype(F32)
     expert_pre_grad = pre_cotangents(expert_cot, gate_expert, up_expert, sigmoid_expert)
+    expert_down_grad = local_kernel(
+        functools.partial(join_kernel, runs),
+        jax.ShapeDtypeStruct((hidden_count, model_width), BF),
+        0,
+        4 * hidden_count * model_width,
+        1,
+        2,
+    )(half_index, grad_own, grad_other)[None]
     expert_pre_grad = expert_pre_grad.transpose(0, 2, 1)[None]
-    expert_down_grad = expert_grad.astype(BF)[None]
     return (expert_pre_grad, expert_down_grad, dense_pre_grad, dense_share.T)
 
 

time: 158 us -> 151 us (0.956); the launches traced: 155 us -> 150 us
  waiting for transfers between devices: 18.5 us -> 9.45 us
  other arithmetic: 6.28 us -> 2.54 us
  Pallas kernels: 4.28 us -> 7.63 us
  matrix products: 10.1 us -> 11.8 us
    ppermute x4 -> x5, waiting for transfers between devices: 13.3 us -> 6.16 us  [swap(): return lax.ppermute(values, 'zl', [(0, 1), (1, 0)])]
    pallas_call x1 -> x2, Pallas kernels: 0.42 us -> 3.14 us  [the longest x1 1.74 us: body(): local_kernel(functools.partial(split_kernel, runs), [weights, weights], 0...]
    ppermute x4 -> x5, starting transfers between devices: 12 us -> 14.4 us  [swap(): return lax.ppermute(values, 'zl', [(0, 1), (1, 0)])]
    another operation x2 -> x1, other arithmetic: 1.94 us -> 0.11 us  [pre_cotangents(): return jnp.stack([gate_cot, up_cot]).astype(BF)]
    all_to_all x1, waiting for transfers between devices: 3.49 us -> 1.67 us  [body(): lax.all_to_all(pairs, ('zh', 'x'), split_axis=0, concat_axis=0, tiled=True)]
    dot_general x4 -> x6, matrix products: 10.1 us -> 11.8 us  [the longest x1 3.79 us: body(): jnp.einsum('hr,fr->hf', expert_units_other, sent_half, preferred_element_...]
    unnamed x20 -> x32, local copies, waits for them, and re-layouts: 2.43 us -> 3.94 us
  transfers between devices with their start and end apart: 8 -> 9, of which waited for: 4 -> 3; matrix products, arithmetic and copies ran while one was open for 4% -> 10% of each run, Pallas kernels for 1% -> 2%
where the time goes in v7:
time: 151 us; the launch traced here: 150 us
  blocking collectives  65.8 us (44%)
  starting transfers between devices  34.9 us (23%)
  between operations  14.4 us (10%)
  matrix products  11.8 us (8%)
  waiting for transfers between devices  9.45 us (6%)
  Pallas kernels  7.63 us (5%)
  local copies, waits for them, and re-layouts  3.94 us (3%)
  other arithmetic  2.54 us (2%)
    all_to_all x1, blocking collectives, body(): lax.all_to_all(outgoing, EXPERT, split_axis=0, concat_axis=0, tiled=True)  38.9 us
    all_gather x1, blocking collectives, gather_columns(): whole = lax.all_gather(rows, 'y', axis=0, tiled=False)  26.9 us
    ppermute x5, starting transfers between devices, swap(): return lax.ppermute(values, 'zl', [(0, 1), (1, 0)])  14.4 us
    ppermute x1, starting transfers between devices, body(): theirs = lax.ppermute(theirs, 'core', [(0, 1), (1, 0)])  7.61 us
    ppermute x1, starting transfers between devices, scatter_total(): other = lax.ppermute(mine, ('x', 'zl'), route)  7.12 us
    ppermute x5, waiting for transfers between devices, swap(): return lax.ppermute(values, 'zl', [(0, 1), (1, 0)])  6.16 us
    all_to_all x1, starting transfers between devices, body(): lax.all_to_all(pairs, ('zh', 'x'), split_axis=0, concat_axis=0, tiled=True)  5.74 us
    unnamed x32, local copies, waits for them, and re-layouts  3.94 us
  transfers between devices with their start and end apart: 9, of which 3 were waited for; matrix products, arithmetic and copies ran while one was open for 10% of the time, Pallas kernels for 2%

profile of v7, /device:TPU:1, one launch (start us, length us, event | category | flops | bytes accessed | tf_op | source)
XLA Modules:
  0.0 150.5 jit_solution(11351591041938692505)
XLA Ops:
  7.2 0.9 copy-done.4
  8.1 0.7 copy-done.6
  8.8 0.7 copy-done.7
  9.5 1.3 shard_map.102
  10.8 38.9 %all_to_all.10 = bf16[64,24,128]{2,1,0:T(8,128)(2,1)S(1)} all-to-all(bf16[64,24,128]{2,1,0:T(8,128)(2,1)S(1)} %bitcast.190), channel_id=1, replica_groups=mesh['zh'=4,'x'=8,'core'=2,'y'=8,'zl'=2] {'zh','x','core'}, dimensions={0} | all-to-all | bytes 786432 | tf_op jit(solution)/shard_map/all_to_all | solution.py:247
  49.7 1.4 shard_map.103
  51.5 3.4 %collective-permute-start.1 = (bf16[152,1024]{1,0:T(8,128)(2,1)S(1)}, bf16[152,1024]{1,0:T(8,128)(2,1)S(1)}, u32[]{:S(2)}, u32[]{:S(2)}) collective-permute-start(bf16[152,1024]{1,0:T(8,128)(2,1)S(1)} %pad_maximum_fusion), channel_id=1, source_target_pairs={{0,1},{1,0},{2,3},{3,2},{4,5},{5,4},{6,7},{7,6},{8,9},{9,8},{10,11... | collective-permute-start | bytes 933896 | tf_op jit(solution)/shard_map/ppermute | solution.py:150
  54.9 1.7 %shard_map.104 = (bf16[2,152,1792]{2,1,0:T(8,128)(2,1)S(1)}, bf16[2,152,1792]{2,1,0:T(8,128)(2,1)}) custom-call(s32[1]{0:T(128)} %bitcast.half_ref, bf16[152,3584]{1,0:T(8,128)(2,1)S(1)} %copy-done, bf16[152,3584]{1,0:T(8,128)(2,1)S(1)} %bitcast.188), custom_call_target="tpu_custom_call" | custom-call | bytes 4358144 | tf_op jit(solution)/shard_map/pallas_call | solution.py:264
  56.7 1.0 copy-done.2
  57.7 1.9 %collective-permute-start = (bf16[2,152,1792]{2,1,0:T(8,128)(2,1)}, bf16[2,152,1792]{2,1,0:T(8,128)(2,1)}, u32[]{:S(2)}, u32[]{:S(2)}) collective-permute-start(bf16[2,152,1792]{2,1,0:T(8,128)(2,1)} %get-tuple-element.23), channel_id=1, source_target_pairs={{0,1},{1,0},{2,3},{3,2},{4,5},{5,4},{6,7},{7,6},{8,9},{9,8},{10,11... | collective-permute-start | bytes 3268616 | tf_op jit(solution)/shard_map/ppermute | solution.py:150
  59.6 26.9 %all-gather.1.grad_ref = bf16[1792,256]{1,0:T(8,128)(2,1)S(1)} all-gather(bf16[224,256]{1,0:T(8,128)(2,1)S(1)} %bitcast.192), channel_id=3, replica_groups=mesh['zh'=4,'x'=8,'core'=2,'y'=8,'zl'=2] {'y'}, dimensions={0}, use_global_device_ids=true | all-gather | bytes 1032192 | tf_op jit(solution)/shard_map/all_gather | solution.py:154
  86.6 0.6 copy-done.14
  87.2 0.7 shard_map.105
  87.9 7.6 %collective-permute-start.2 = (bf16[32,72,128]{2,1,0:T(8,128)(2,1)S(1)}, bf16[32,72,128]{2,1,0:T(8,128)(2,1)S(1)}, u32[]{:S(2)}, u32[]{:S(2)}) collective-permute-start(bf16[32,72,128]{2,1,0:T(8,128)(2,1)S(1)} %get-tuple-element.28), channel_id=1, source_target_pairs={{0,16},{16,0},{1,17},{17,1},{2,18},{18,2},{3,19},{19,3},{4,20},{20... | collective-permute-start | bytes 1769480 | tf_op jit(solution)/shard_map/ppermute | solution.py:284
  95.6 1.6 %collective-permute-done.2.other_ref = bf16[32,72,128]{2,1,0:T(8,128)(2,1)S(1)} collective-permute-done((bf16[32,72,128]{2,1,0:T(8,128)(2,1)S(1)}, bf16[32,72,128]{2,1,0:T(8,128)(2,1)S(1)}, u32[]{:S(2)}, u32[]{:S(2)}) %collective-permute-start.2) | collective-permute-done | bytes 589856 | tf_op jit(solution)/shard_map/ppermute | solution.py:284
  97.2 0.9 shard_map.106
  98.1 5.7 %all-to-all-start.1 = ((bf16[32,72,128]{2,1,0:T(8,128)(2,1)}), bf16[32,72,128]{2,1,0:T(8,128)(2,1)S(1)}, u32[]{:S(2)}, u32[]{:S(2)}) async-start(bf16[32,72,128]{2,1,0:T(8,128)(2,1)} %shard_map.106), calls=%async_computation.1 | async-start | bytes 1179648 | tf_op jit(solution)/shard_map/all_to_all | solution.py:289
  103.8 1.4 convolution_convert_fusion.3
  105.2 3.7 %collective-permute-start.3 = (bf16[152,256]{1,0:T(8,128)(2,1)S(1)}, bf16[152,256]{1,0:T(8,128)(2,1)S(1)}, u32[]{:S(2)}, u32[]{:S(2)}) collective-permute-start(bf16[152,256]{1,0:T(8,128)(2,1)S(1)} %convolution_convert_fusion.3), channel_id=1, source_target_pairs={{0,1},{1,0},{2,3},{3,2},{4,5},{5,4},{6,7},{7,6},{8,9},{9,8},{10,11... | collective-permute-start | bytes 233480 | tf_op jit(solution)/shard_map/ppermute | solution.py:150
  109.3 3.8 %convolution_convert_fusion.1 = bf16[152,1792]{1,0:T(8,128)(2,1)} fusion(bf16[1792,768]{1,0:T(8,128)(2,1)} %all-gather.4.cloned.1.call-done, bf16[152,1024]{1,0:T(8,128)(2,1)S(1)} %copy-done.15), kind=kOutput, calls=%fused_computation.1 | convolution fusion | flops 418654208 | bytes 3530752 | tf_op jit(solution)/shard_map/hr,fr->hf/dot_general | solution.py:297
  113.1 2.0 %collective-permute-start.5 = (bf16[152,1792]{1,0:T(8,128)(2,1)}, bf16[152,1792]{1,0:T(8,128)(2,1)S(1)}, u32[]{:S(2)}, u32[]{:S(2)}) collective-permute-start(bf16[152,1792]{1,0:T(8,128)(2,1)} %convolution_convert_fusion.1), channel_id=1, source_target_pairs={{0,1},{1,0},{2,3},{3,2},{4,5},{5,4},{6,7},{7,6},{8,9},{9,8},{10,11... | collective-permute-start | bytes 1634312 | tf_op jit(solution)/shard_map/ppermute | solution.py:150
  115.2 1.7 %convolution_convert_fusion.2 = bf16[152,768]{1,0:T(8,128)(2,1)S(1)} fusion(bf16[1792,768]{1,0:T(8,128)(2,1)S(1)} %copy-done.8, bf16[2,152,1792]{2,1,0:T(8,128)(2,1)} %collective-permute-done), kind=kOutput, calls=%fused_computation.3 | convolution fusion | flops 418498560 | bytes 3530752 | tf_op jit(solution)/shard_map/hf,fr->hr/dot_general | solution.py:301
  116.9 3.4 %collective-permute-start.4 = (bf16[152,768]{1,0:T(8,128)(2,1)S(1)}, bf16[152,768]{1,0:T(8,128)(2,1)}, u32[]{:S(2)}, u32[]{:S(2)}) collective-permute-start(bf16[152,768]{1,0:T(8,128)(2,1)S(1)} %convolution_convert_fusion.2), channel_id=1, source_target_pairs={{0,1},{1,0},{2,3},{3,2},{4,5},{5,4},{6,7},{7,6},{8,9},{9,8},{10,11... | collective-permute-start | bytes 700424 | tf_op jit(solution)/shard_map/ppermute | solution.py:150
  120.2 1.7 %all-to-all-done.1.came_ref = bf16[32,72,128]{2,1,0:T(8,128)(2,1)S(1)} async-done(((bf16[32,72,128]{2,1,0:T(8,128)(2,1)}), bf16[32,72,128]{2,1,0:T(8,128)(2,1)S(1)}, u32[]{:S(2)}, u32[]{:S(2)}) %all-to-all-start.1) | async-done | bytes 589856 | tf_op jit(solution)/shard_map/all_to_all | solution.py:289
  122.0 7.1 %collective-permute-start.6 = (bf16[56,152]{1,0:T(8,128)(2,1)S(1)}, bf16[56,152]{1,0:T(8,128)(2,1)S(1)}, u32[]{:S(2)}, u32[]{:S(2)}) collective-permute-start(bf16[56,152]{1,0:T(8,128)(2,1)S(1)} %shard_map.108), channel_id=1, source_target_pairs={{0,65},{1,64},{32,97},{33,96},{64,1},{65,0},{96,33},{97,32},{128,1... | collective-permute-start | bytes 51080 | tf_op jit(solution)/shard_map/ppermute | solution.py:213
  129.3 3.0 %convolution_convert_fusion.own_ref = bf16[152,1792]{1,0:T(8,128)(2,1)S(1)} fusion(bf16[152,768]{1,0:T(8,128)(2,1)S(1)} %fusion.7, bf16[1792,768]{1,0:T(8,128)(2,1)} %all-gather.4.cloned.1.call-done), kind=kOutput, calls=%fused_computation | convolution fusion | flops 418654208 | bytes 3530752 | tf_op jit(solution)/shard_map/hr,fr->hf/dot_general | solution.py:305
  132.3 0.7 maximum_bitcast_fusion.1
  133.0 0.6 select_bitcast_fusion
  133.6 6.1 %collective-permute-done.4 = bf16[152,768]{1,0:T(8,128)(2,1)} collective-permute-done((bf16[152,768]{1,0:T(8,128)(2,1)S(1)}, bf16[152,768]{1,0:T(8,128)(2,1)}, u32[]{:S(2)}, u32[]{:S(2)}) %collective-permute-start.4) | collective-permute-done | bytes 233504 | tf_op jit(solution)/shard_map/ppermute | solution.py:150
  139.7 1.7 %fusion.23 = (bf16[1,152,768]{2,1,0:T(8,128)(2,1)S(1)}, bf16[1,152,768]{2,1,0:T(8,128)(2,1)S(1)}) fusion(bf16[1,2,768,152]{2,3,1,0:T(8,128)(2,1)S(1)} %copy-done.13, bf16[152,768]{1,0:T(8,128)(2,1)} %collective-permute-done.4, bf16[1792,768]{1,0:T(8,128)(2,1)S(1)} %copy-done.9, bf16[2,152,1792]{2,1,0:T(8,128)(2,1)S(1)} %copy-done.3), kind=kOutput, calls=%fused_computation.34 | convolution fusion | flops 420366336 | bytes 4464640 | tf_op jit(solution)/shard_map/hf,fr->hr/dot_general | solution.py:306
  141.4 0.8 maximum_bitcast_fusion
  142.2 1.4 shard_map.107
  (42 shorter events, 1.0 us)
Async XLA Ops:
  7.2 102.1 %all-gather.4.cloned.1.call-start = ((), (), s32[]{:S(2)}) async-start(), calls=%async_computation.2 | async-start | bytes 3096576 | tf_op jit(solution)/shard_map/all_gather | solution.py:154
  7.2 0.9 copy-start.4
  8.1 0.7 copy-start.6
  8.8 0.7 copy-start.7
  10.8 40.4 %copy-start.10 = (bf16[2,256,152]{1,2,0:T(8,128)(2,1)S(1)}, bf16[2,256,152]{1,2,0:T(8,128)(2,1)}, u32[]{:S(2)}) copy-start(bf16[2,256,152]{1,2,0:T(8,128)(2,1)} %param.13) | copy-start | bytes 466948
  10.8 40.5 %copy-start.12 = (bf16[1,2,768,152]{2,3,1,0:T(8,128)(2,1)S(1)}, bf16[1,2,768,152]{2,3,1,0:T(8,128)(2,1)}, u32[]{:S(2)}) copy-start(bf16[1,2,768,152]{2,3,1,0:T(8,128)(2,1)} %param.11) | copy-start | bytes 1400836
  49.7 5.2 %copy-start.1 = (bf16[1,152,3584]{2,1,0:T(8,128)(2,1)S(1)}, bf16[1,152,3584]{2,1,0:T(8,128)(2,1)}, u32[]{:S(2)}) copy-start(bf16[1,152,3584]{2,1,0:T(8,128)(2,1)} %param.10) | copy-start | bytes 3268612
  51.2 3.7 %copy-start = (bf16[152,3584]{1,0:T(8,128)(2,1)S(1)}, bf16[152,3584]{1,0:T(8,128)(2,1)}, u32[]{:S(2)}) copy-start(bf16[152,3584]{1,0:T(8,128)(2,1)} %dense_ref) | copy-start | bytes 3268612
  51.5 35.0 %collective-permute-start.1 = (bf16[152,1024]{1,0:T(8,128)(2,1)S(1)}, bf16[152,1024]{1,0:T(8,128)(2,1)S(1)}, u32[]{:S(2)}, u32[]{:S(2)}) collective-permute-start(bf16[152,1024]{1,0:T(8,128)(2,1)S(1)} %pad_maximum_fusion), channel_id=1, source_target_pairs={{0,1},{1,0},{2,3},{3,2},{4,5},{5,4},{6,7},{7,6},{8,9},{9,8},{10,11... | collective-permute-start | bytes 933896 | tf_op jit(solution)/shard_map/ppermute | solution.py:150
  54.9 4.7 %copy-start.5 = (bf16[256,224]{0,1:T(8,128)(2,1)S(1)}, bf16[256,224]{0,1:T(8,128)(2,1)}, u32[]{:S(2)}) copy-start(bf16[256,224]{0,1:T(8,128)(2,1)} %param.7) | copy-start | bytes 344068
  56.7 1.0 copy-start.2
  57.7 39.5 %collective-permute-start = (bf16[2,152,1792]{2,1,0:T(8,128)(2,1)}, bf16[2,152,1792]{2,1,0:T(8,128)(2,1)}, u32[]{:S(2)}, u32[]{:S(2)}) collective-permute-start(bf16[2,152,1792]{2,1,0:T(8,128)(2,1)} %get-tuple-element.23), channel_id=1, source_target_pairs={{0,1},{1,0},{2,3},{3,2},{4,5},{5,4},{6,7},{7,6},{8,9},{9,8},{10,11... | collective-permute-start | bytes 3268616 | tf_op jit(solution)/shard_map/ppermute | solution.py:150
  86.5 0.7 copy-start.14
  87.9 9.2 %collective-permute-start.2 = (bf16[32,72,128]{2,1,0:T(8,128)(2,1)S(1)}, bf16[32,72,128]{2,1,0:T(8,128)(2,1)S(1)}, u32[]{:S(2)}, u32[]{:S(2)}) collective-permute-start(bf16[32,72,128]{2,1,0:T(8,128)(2,1)S(1)} %get-tuple-element.28), channel_id=1, source_target_pairs={{0,16},{16,0},{1,17},{17,1},{2,18},{18,2},{3,19},{19,3},{4,20},{20... | collective-permute-start | bytes 1769480 | tf_op jit(solution)/shard_map/ppermute | solution.py:284
  98.1 10.9 %copy-start.3 = (bf16[2,152,1792]{2,1,0:T(8,128)(2,1)S(1)}, bf16[2,152,1792]{2,1,0:T(8,128)(2,1)}, u32[]{:S(2)}) copy-start(bf16[2,152,1792]{2,1,0:T(8,128)(2,1)} %copy-done.2) | copy-start | bytes 3268612
  98.1 23.8 %all-to-all-start.1 = ((bf16[32,72,128]{2,1,0:T(8,128)(2,1)}), bf16[32,72,128]{2,1,0:T(8,128)(2,1)S(1)}, u32[]{:S(2)}, u32[]{:S(2)}) async-start(bf16[32,72,128]{2,1,0:T(8,128)(2,1)} %shard_map.106), calls=%async_computation.1 | async-start | bytes 1179648 | tf_op jit(solution)/shard_map/all_to_all | solution.py:289
  105.2 4.1 %copy-start.15 = (bf16[152,1024]{1,0:T(8,128)(2,1)S(1)}, bf16[152,1024]{1,0:T(8,128)(2,1)}, u32[]{:S(2)}) copy-start(bf16[152,1024]{1,0:T(8,128)(2,1)} %copy-done.14) | copy-start | bytes 933892
  105.2 15.0 %collective-permute-start.3 = (bf16[152,256]{1,0:T(8,128)(2,1)S(1)}, bf16[152,256]{1,0:T(8,128)(2,1)S(1)}, u32[]{:S(2)}, u32[]{:S(2)}) collective-permute-start(bf16[152,256]{1,0:T(8,128)(2,1)S(1)} %convolution_convert_fusion.3), channel_id=1, source_target_pairs={{0,1},{1,0},{2,3},{3,2},{4,5},{5,4},{6,7},{7,6},{8,9},{9,8},{10,11... | collective-permute-start | bytes 233480 | tf_op jit(solution)/shard_map/ppermute | solution.py:150
  109.3 5.9 %copy-start.8 = (bf16[1792,768]{1,0:T(8,128)(2,1)S(1)}, bf16[1792,768]{1,0:T(8,128)(2,1)}, u32[]{:S(2)}) copy-start(bf16[1792,768]{1,0:T(8,128)(2,1)} %all-gather.4.cloned.1.call-done) | copy-start | bytes 8257540
  113.1 16.0 %copy-start.11 = (bf16[2,256,152]{1,2,0:T(8,128)(2,1)S(1)}, bf16[2,256,152]{1,2,0:T(8,128)(2,1)}, u32[]{:S(2)}) copy-start(bf16[2,256,152]{1,2,0:T(8,128)(2,1)} %param.13) | copy-start | bytes 466948
  113.1 29.1 %collective-permute-start.5 = (bf16[152,1792]{1,0:T(8,128)(2,1)}, bf16[152,1792]{1,0:T(8,128)(2,1)S(1)}, u32[]{:S(2)}, u32[]{:S(2)}) collective-permute-start(bf16[152,1792]{1,0:T(8,128)(2,1)} %convolution_convert_fusion.1), channel_id=1, source_target_pairs={{0,1},{1,0},{2,3},{3,2},{4,5},{5,4},{6,7},{7,6},{8,9},{9,8},{10,11... | collective-permute-start | bytes 1634312 | tf_op jit(solution)/shard_map/ppermute | solution.py:150
  116.9 22.9 %collective-permute-start.4 = (bf16[152,768]{1,0:T(8,128)(2,1)S(1)}, bf16[152,768]{1,0:T(8,128)(2,1)}, u32[]{:S(2)}, u32[]{:S(2)}) collective-permute-start(bf16[152,768]{1,0:T(8,128)(2,1)S(1)} %convolution_convert_fusion.2), channel_id=1, source_target_pairs={{0,1},{1,0},{2,3},{3,2},{4,5},{5,4},{6,7},{7,6},{8,9},{9,8},{10,11... | collective-permute-start | bytes 700424 | tf_op jit(solution)/shard_map/ppermute | solution.py:150
  122.0 10.9 %collective-permute-start.6 = (bf16[56,152]{1,0:T(8,128)(2,1)S(1)}, bf16[56,152]{1,0:T(8,128)(2,1)S(1)}, u32[]{:S(2)}, u32[]{:S(2)}) collective-permute-start(bf16[56,152]{1,0:T(8,128)(2,1)S(1)} %shard_map.108), channel_id=1, source_target_pairs={{0,65},{1,64},{32,97},{33,96},{64,1},{65,0},{96,33},{97,32},{128,1... | collective-permute-start | bytes 51080 | tf_op jit(solution)/shard_map/ppermute | solution.py:213
  129.3 10.5 %copy-start.9 = (bf16[1792,768]{1,0:T(8,128)(2,1)S(1)}, bf16[1792,768]{1,0:T(8,128)(2,1)}, u32[]{:S(2)}) copy-start(bf16[1792,768]{1,0:T(8,128)(2,1)} %all-gather.4.cloned.1.call-done) | copy-start | bytes 8257540
  129.3 10.5 %copy-start.13 = (bf16[1,2,768,152]{2,3,1,0:T(8,128)(2,1)S(1)}, bf16[1,2,768,152]{2,3,1,0:T(8,128)(2,1)}, u32[]{:S(2)}) copy-start(bf16[1,2,768,152]{2,3,1,0:T(8,128)(2,1)} %param.11) | copy-start | bytes 1400836
Sparse Core Ops, SparseCore 0:
  51.3 50.5 all-gather.3

commit v8 on v7

--- a/solution.py
+++ b/solution.py
@@ -294,14 +294,14 @@
     sent_half = after(sent_half, (dense_other, dense_cot))
     dense_other = swap(dense_other)
 
+    cot_other = jnp.einsum("hf,fr->hr", weights_swapped[1], sent_half, preferred_element_type=F32)
+    cot_other = cot_other.astype(BF)
+    sent_half = after(sent_half, cot_other)
+    cot_other = swap(cot_other)
     grad_other = jnp.einsum("hr,fr->hf", expert_units_other, sent_half, preferred_element_type=F32)
     grad_other = grad_other.astype(BF)
-    sent_half = after(sent_half, grad_other)
+    sent_half, came, dense_other = after((sent_half, came, dense_other), grad_other)
     grad_other = swap(grad_other)
-    cot_other = jnp.einsum("hf,fr->hr", weights_swapped[1], sent_half, preferred_element_type=F32)
-    cot_other = cot_other.astype(BF)
-    sent_half, came, dense_other = after((sent_half, came, dense_other), cot_other)
-    cot_other = swap(cot_other)
     grad_own = jnp.einsum("hr,fr->hf", expert_units, sent_half, preferred_element_type=F32).astype(BF)
     cot_own = jnp.einsum("hf,fr->hr", weights_mine[1], sent_half, preferred_element_type=F32)
 

time: 151 us -> 148 us (0.980)
  waiting for transfers between devices: 9.45 us -> 7.17 us
    ppermute x5, waiting for transfers between devices: 6.16 us -> 3.55 us  [swap(): return lax.ppermute(values, 'zl', [(0, 1), (1, 0)])]
    dot_general x1, matrix products: 3.79 us -> 1.89 us  [body(): jnp.einsum('hr,fr->hf', expert_units_other, sent_half, preferred_element_...]
    dot_general x1, matrix products: 1.69 us -> 3.39 us  [body(): jnp.einsum('hf,fr->hr', weights_swapped[1], sent_half, preferred_element_...]
where the time goes in v8:
time: 148 us
  blocking collectives  65.8 us (44%)
  starting transfers between devices  34.8 us (24%)
  between operations  14.4 us (10%)
  matrix products  11.6 us (8%)
  Pallas kernels  7.63 us (5%)
  waiting for transfers between devices  7.17 us (5%)
  local copies, waits for them, and re-layouts  3.94 us (3%)
  other arithmetic  2.54 us (2%)
    all_to_all x1, blocking collectives, body(): lax.all_to_all(outgoing, EXPERT, split_axis=0, concat_axis=0, tiled=True)  38.9 us
    all_gather x1, blocking collectives, gather_columns(): whole = lax.all_gather(rows, 'y', axis=0, tiled=False)  26.9 us
    ppermute x5, starting transfers between devices, swap(): return lax.ppermute(values, 'zl', [(0, 1), (1, 0)])  14.3 us
    ppermute x1, starting transfers between devices, body(): theirs = lax.ppermute(theirs, 'core', [(0, 1), (1, 0)])  7.61 us
    ppermute x1, starting transfers between devices, scatter_total(): other = lax.ppermute(mine, ('x', 'zl'), route)  7.12 us
    all_to_all x1, starting transfers between devices, body(): lax.all_to_all(pairs, ('zh', 'x'), split_axis=0, concat_axis=0, tiled=True)  5.74 us
    unnamed x32, local copies, waits for them, and re-layouts  3.94 us
    ppermute x5, waiting for transfers between devices, swap(): return lax.ppermute(values, 'zl', [(0, 1), (1, 0)])  3.55 us
  transfers between devices with their start and end apart: 9, of which 3 were waited for; matrix products, arithmetic and copies ran while one was open for 10% of the time, Pallas kernels for 2%

profile of v8, /device:TPU:1, one launch (start us, length us, event | category | flops | bytes accessed | tf_op | source)
XLA Modules:
  0.0 147.9 jit_solution(4336001086233913841)
XLA Ops:
  7.2 0.9 copy-done.4
  8.1 0.7 copy-done.6
  8.8 0.7 copy-done.7
  9.5 1.3 shard_map.102
  10.8 38.9 %all_to_all.10 = bf16[64,24,128]{2,1,0:T(8,128)(2,1)S(1)} all-to-all(bf16[64,24,128]{2,1,0:T(8,128)(2,1)S(1)} %bitcast.190), channel_id=1, replica_groups=mesh['zh'=4,'x'=8,'core'=2,'y'=8,'zl'=2] {'zh','x','core'}, dimensions={0} | all-to-all | bytes 786432 | tf_op jit(solution)/shard_map/all_to_all | solution.py:247
  49.7 1.4 shard_map.103
  51.5 3.4 %collective-permute-start.1 = (bf16[152,1024]{1,0:T(8,128)(2,1)S(1)}, bf16[152,1024]{1,0:T(8,128)(2,1)S(1)}, u32[]{:S(2)}, u32[]{:S(2)}) collective-permute-start(bf16[152,1024]{1,0:T(8,128)(2,1)S(1)} %pad_maximum_fusion), channel_id=1, source_target_pairs={{0,1},{1,0},{2,3},{3,2},{4,5},{5,4},{6,7},{7,6},{8,9},{9,8},{10,11... | collective-permute-start | bytes 933896 | tf_op jit(solution)/shard_map/ppermute | solution.py:150
  54.9 1.7 %shard_map.104 = (bf16[2,152,1792]{2,1,0:T(8,128)(2,1)S(1)}, bf16[2,152,1792]{2,1,0:T(8,128)(2,1)}) custom-call(s32[1]{0:T(128)} %bitcast.half_ref, bf16[152,3584]{1,0:T(8,128)(2,1)S(1)} %copy-done, bf16[152,3584]{1,0:T(8,128)(2,1)S(1)} %bitcast.188), custom_call_target="tpu_custom_call" | custom-call | bytes 4358144 | tf_op jit(solution)/shard_map/pallas_call | solution.py:264
  56.7 1.0 copy-done.2
  57.7 1.9 %collective-permute-start = (bf16[2,152,1792]{2,1,0:T(8,128)(2,1)}, bf16[2,152,1792]{2,1,0:T(8,128)(2,1)}, u32[]{:S(2)}, u32[]{:S(2)}) collective-permute-start(bf16[2,152,1792]{2,1,0:T(8,128)(2,1)} %get-tuple-element.23), channel_id=1, source_target_pairs={{0,1},{1,0},{2,3},{3,2},{4,5},{5,4},{6,7},{7,6},{8,9},{9,8},{10,11... | collective-permute-start | bytes 3268616 | tf_op jit(solution)/shard_map/ppermute | solution.py:150
  59.6 26.9 %all-gather.1.grad_ref = bf16[1792,256]{1,0:T(8,128)(2,1)S(1)} all-gather(bf16[224,256]{1,0:T(8,128)(2,1)S(1)} %bitcast.192), channel_id=3, replica_groups=mesh['zh'=4,'x'=8,'core'=2,'y'=8,'zl'=2] {'y'}, dimensions={0}, use_global_device_ids=true | all-gather | bytes 1032192 | tf_op jit(solution)/shard_map/all_gather | solution.py:154
  86.6 0.6 copy-done.14
  87.2 0.7 shard_map.105
  87.9 7.6 %collective-permute-start.2 = (bf16[32,72,128]{2,1,0:T(8,128)(2,1)S(1)}, bf16[32,72,128]{2,1,0:T(8,128)(2,1)S(1)}, u32[]{:S(2)}, u32[]{:S(2)}) collective-permute-start(bf16[32,72,128]{2,1,0:T(8,128)(2,1)S(1)} %get-tuple-element.28), channel_id=1, source_target_pairs={{0,16},{16,0},{1,17},{17,1},{2,18},{18,2},{3,19},{19,3},{4,20},{20... | collective-permute-start | bytes 1769480 | tf_op jit(solution)/shard_map/ppermute | solution.py:284
  95.6 1.6 %collective-permute-done.2.other_ref = bf16[32,72,128]{2,1,0:T(8,128)(2,1)S(1)} collective-permute-done((bf16[32,72,128]{2,1,0:T(8,128)(2,1)S(1)}, bf16[32,72,128]{2,1,0:T(8,128)(2,1)S(1)}, u32[]{:S(2)}, u32[]{:S(2)}) %collective-permute-start.2) | collective-permute-done | bytes 589856 | tf_op jit(solution)/shard_map/ppermute | solution.py:284
  97.2 0.9 shard_map.106
  98.1 5.7 %all-to-all-start.1 = ((bf16[32,72,128]{2,1,0:T(8,128)(2,1)}), bf16[32,72,128]{2,1,0:T(8,128)(2,1)S(1)}, u32[]{:S(2)}, u32[]{:S(2)}) async-start(bf16[32,72,128]{2,1,0:T(8,128)(2,1)} %shard_map.106), calls=%async_computation.1 | async-start | bytes 1179648 | tf_op jit(solution)/shard_map/all_to_all | solution.py:289
  103.8 1.4 convolution_convert_fusion.3
  105.2 3.6 %collective-permute-start.3 = (bf16[152,256]{1,0:T(8,128)(2,1)S(1)}, bf16[152,256]{1,0:T(8,128)(2,1)S(1)}, u32[]{:S(2)}, u32[]{:S(2)}) collective-permute-start(bf16[152,256]{1,0:T(8,128)(2,1)S(1)} %convolution_convert_fusion.3), channel_id=1, source_target_pairs={{0,1},{1,0},{2,3},{3,2},{4,5},{5,4},{6,7},{7,6},{8,9},{9,8},{10,11... | collective-permute-start | bytes 233480 | tf_op jit(solution)/shard_map/ppermute | solution.py:150
  109.2 3.4 %convolution_convert_fusion.2 = bf16[152,768]{1,0:T(8,128)(2,1)} fusion(bf16[1792,768]{1,0:T(8,128)(2,1)} %all-gather.4.cloned.1.call-done, bf16[2,152,1792]{2,1,0:T(8,128)(2,1)} %collective-permute-done), kind=kOutput, calls=%fused_computation.3 | convolution fusion | flops 418498560 | bytes 3530752 | tf_op jit(solution)/shard_map/hf,fr->hr/dot_general | solution.py:297
  112.6 2.0 %collective-permute-start.4 = (bf16[152,768]{1,0:T(8,128)(2,1)}, bf16[152,768]{1,0:T(8,128)(2,1)}, u32[]{:S(2)}, u32[]{:S(2)}) collective-permute-start(bf16[152,768]{1,0:T(8,128)(2,1)} %convolution_convert_fusion.2), channel_id=1, source_target_pairs={{0,1},{1,0},{2,3},{3,2},{4,5},{5,4},{6,7},{7,6},{8,9},{9,8},{10,11... | collective-permute-start | bytes 700424 | tf_op jit(solution)/shard_map/ppermute | solution.py:150
  114.6 1.9 %convolution_convert_fusion.1 = bf16[152,1792]{1,0:T(8,128)(2,1)} fusion(bf16[1792,768]{1,0:T(8,128)(2,1)S(1)} %copy-done.8, bf16[152,1024]{1,0:T(8,128)(2,1)S(1)} %copy-done.15), kind=kOutput, calls=%fused_computation.1 | convolution fusion | flops 418654208 | bytes 3530752 | tf_op jit(solution)/shard_map/hr,fr->hf/dot_general | solution.py:301
  116.5 3.3 %collective-permute-start.5 = (bf16[152,1792]{1,0:T(8,128)(2,1)}, bf16[152,1792]{1,0:T(8,128)(2,1)S(1)}, u32[]{:S(2)}, u32[]{:S(2)}) collective-permute-start(bf16[152,1792]{1,0:T(8,128)(2,1)} %convolution_convert_fusion.1), channel_id=1, source_target_pairs={{0,1},{1,0},{2,3},{3,2},{4,5},{5,4},{6,7},{7,6},{8,9},{9,8},{10,11... | collective-permute-start | bytes 1634312 | tf_op jit(solution)/shard_map/ppermute | solution.py:150
  119.9 2.0 %all-to-all-done.1.came_ref = bf16[32,72,128]{2,1,0:T(8,128)(2,1)S(1)} async-done(((bf16[32,72,128]{2,1,0:T(8,128)(2,1)}), bf16[32,72,128]{2,1,0:T(8,128)(2,1)S(1)}, u32[]{:S(2)}, u32[]{:S(2)}) %all-to-all-start.1) | async-done | bytes 589856 | tf_op jit(solution)/shard_map/all_to_all | solution.py:289
  122.0 7.1 %collective-permute-start.6 = (bf16[56,152]{1,0:T(8,128)(2,1)S(1)}, bf16[56,152]{1,0:T(8,128)(2,1)S(1)}, u32[]{:S(2)}, u32[]{:S(2)}) collective-permute-start(bf16[56,152]{1,0:T(8,128)(2,1)S(1)} %shard_map.108), channel_id=1, source_target_pairs={{0,65},{1,64},{32,97},{33,96},{64,1},{65,0},{96,33},{97,32},{128,1... | collective-permute-start | bytes 51080 | tf_op jit(solution)/shard_map/ppermute | solution.py:213
  129.3 3.0 %convolution_convert_fusion.own_ref = bf16[152,1792]{1,0:T(8,128)(2,1)S(1)} fusion(bf16[152,768]{1,0:T(8,128)(2,1)S(1)} %fusion.7, bf16[1792,768]{1,0:T(8,128)(2,1)} %all-gather.4.cloned.1.call-done), kind=kOutput, calls=%fused_computation | convolution fusion | flops 418654208 | bytes 3530752 | tf_op jit(solution)/shard_map/hr,fr->hf/dot_general | solution.py:305
  132.3 0.7 maximum_bitcast_fusion.1
  133.0 0.6 select_bitcast_fusion
  133.6 1.7 %fusion.23 = (bf16[1,152,768]{2,1,0:T(8,128)(2,1)S(1)}, bf16[1,152,768]{2,1,0:T(8,128)(2,1)S(1)}) fusion(bf16[1,2,768,152]{2,3,1,0:T(8,128)(2,1)S(1)} %copy-done.13, bf16[152,768]{1,0:T(8,128)(2,1)} %collective-permute-done.4, bf16[1792,768]{1,0:T(8,128)(2,1)S(1)} %copy-done.9, bf16[2,152,1792]{2,1,0:T(8,128)(2,1)S(1)} %copy-done.3), kind=kOutput, calls=%fused_computation.34 | convolution fusion | flops 420366336 | bytes 4464640 | tf_op jit(solution)/shard_map/hf,fr->hr/dot_general | solution.py:306
  135.3 0.8 maximum_bitcast_fusion
  136.1 3.5 %collective-permute-done.5.other_ref = bf16[152,1792]{1,0:T(8,128)(2,1)S(1)} collective-permute-done((bf16[152,1792]{1,0:T(8,128)(2,1)}, bf16[152,1792]{1,0:T(8,128)(2,1)S(1)}, u32[]{:S(2)}, u32[]{:S(2)}) %collective-permute-start.5) | collective-permute-done | bytes 544800 | tf_op jit(solution)/shard_map/ppermute | solution.py:150
  139.6 1.4 shard_map.107
  (42 shorter events, 1.0 us)
Async XLA Ops:
  7.2 102.0 %all-gather.4.cloned.1.call-start = ((), (), s32[]{:S(2)}) async-start(), calls=%async_computation.2 | async-start | bytes 3096576 | tf_op jit(solution)/shard_map/all_gather | solution.py:154
  7.2 0.9 copy-start.4
  8.1 0.7 copy-start.6
  8.8 0.7 copy-start.7
  10.8 40.4 %copy-start.10 = (bf16[2,256,152]{1,2,0:T(8,128)(2,1)S(1)}, bf16[2,256,152]{1,2,0:T(8,128)(2,1)}, u32[]{:S(2)}) copy-start(bf16[2,256,152]{1,2,0:T(8,128)(2,1)} %param.13) | copy-start | bytes 466948
  10.8 40.5 %copy-start.12 = (bf16[1,2,768,152]{2,3,1,0:T(8,128)(2,1)S(1)}, bf16[1,2,768,152]{2,3,1,0:T(8,128)(2,1)}, u32[]{:S(2)}) copy-start(bf16[1,2,768,152]{2,3,1,0:T(8,128)(2,1)} %param.11) | copy-start | bytes 1400836
  49.7 5.2 %copy-start.1 = (bf16[1,152,3584]{2,1,0:T(8,128)(2,1)S(1)}, bf16[1,152,3584]{2,1,0:T(8,128)(2,1)}, u32[]{:S(2)}) copy-start(bf16[1,152,3584]{2,1,0:T(8,128)(2,1)} %param.10) | copy-start | bytes 3268612
  51.2 3.7 %copy-start = (bf16[152,3584]{1,0:T(8,128)(2,1)S(1)}, bf16[152,3584]{1,0:T(8,128)(2,1)}, u32[]{:S(2)}) copy-start(bf16[152,3584]{1,0:T(8,128)(2,1)} %dense_ref) | copy-start | bytes 3268612
  51.5 35.0 %collective-permute-start.1 = (bf16[152,1024]{1,0:T(8,128)(2,1)S(1)}, bf16[152,1024]{1,0:T(8,128)(2,1)S(1)}, u32[]{:S(2)}, u32[]{:S(2)}) collective-permute-start(bf16[152,1024]{1,0:T(8,128)(2,1)S(1)} %pad_maximum_fusion), channel_id=1, source_target_pairs={{0,1},{1,0},{2,3},{3,2},{4,5},{5,4},{6,7},{7,6},{8,9},{9,8},{10,11... | collective-permute-start | bytes 933896 | tf_op jit(solution)/shard_map/ppermute | solution.py:150
  54.9 4.7 %copy-start.5 = (bf16[256,224]{0,1:T(8,128)(2,1)S(1)}, bf16[256,224]{0,1:T(8,128)(2,1)}, u32[]{:S(2)}) copy-start(bf16[256,224]{0,1:T(8,128)(2,1)} %param.7) | copy-start | bytes 344068
  56.7 1.0 copy-start.2
  57.7 39.5 %collective-permute-start = (bf16[2,152,1792]{2,1,0:T(8,128)(2,1)}, bf16[2,152,1792]{2,1,0:T(8,128)(2,1)}, u32[]{:S(2)}, u32[]{:S(2)}) collective-permute-start(bf16[2,152,1792]{2,1,0:T(8,128)(2,1)} %get-tuple-element.23), channel_id=1, source_target_pairs={{0,1},{1,0},{2,3},{3,2},{4,5},{5,4},{6,7},{7,6},{8,9},{9,8},{10,11... | collective-permute-start | bytes 3268616 | tf_op jit(solution)/shard_map/ppermute | solution.py:150
  86.5 0.7 copy-start.14
  87.9 9.2 %collective-permute-start.2 = (bf16[32,72,128]{2,1,0:T(8,128)(2,1)S(1)}, bf16[32,72,128]{2,1,0:T(8,128)(2,1)S(1)}, u32[]{:S(2)}, u32[]{:S(2)}) collective-permute-start(bf16[32,72,128]{2,1,0:T(8,128)(2,1)S(1)} %get-tuple-element.28), channel_id=1, source_target_pairs={{0,16},{16,0},{1,17},{17,1},{2,18},{18,2},{3,19},{19,3},{4,20},{20... | collective-permute-start | bytes 1769480 | tf_op jit(solution)/shard_map/ppermute | solution.py:284
  98.1 10.7 %copy-start.3 = (bf16[2,152,1792]{2,1,0:T(8,128)(2,1)S(1)}, bf16[2,152,1792]{2,1,0:T(8,128)(2,1)}, u32[]{:S(2)}) copy-start(bf16[2,152,1792]{2,1,0:T(8,128)(2,1)} %copy-done.2) | copy-start | bytes 3268612
  98.1 23.8 %all-to-all-start.1 = ((bf16[32,72,128]{2,1,0:T(8,128)(2,1)}), bf16[32,72,128]{2,1,0:T(8,128)(2,1)S(1)}, u32[]{:S(2)}, u32[]{:S(2)}) async-start(bf16[32,72,128]{2,1,0:T(8,128)(2,1)} %shard_map.106), calls=%async_computation.1 | async-start | bytes 1179648 | tf_op jit(solution)/shard_map/all_to_all | solution.py:289
  105.2 14.7 %collective-permute-start.3 = (bf16[152,256]{1,0:T(8,128)(2,1)S(1)}, bf16[152,256]{1,0:T(8,128)(2,1)S(1)}, u32[]{:S(2)}, u32[]{:S(2)}) collective-permute-start(bf16[152,256]{1,0:T(8,128)(2,1)S(1)} %convolution_convert_fusion.3), channel_id=1, source_target_pairs={{0,1},{1,0},{2,3},{3,2},{4,5},{5,4},{6,7},{7,6},{8,9},{9,8},{10,11... | collective-permute-start | bytes 233480 | tf_op jit(solution)/shard_map/ppermute | solution.py:150
  109.1 5.5 %copy-start.15 = (bf16[152,1024]{1,0:T(8,128)(2,1)S(1)}, bf16[152,1024]{1,0:T(8,128)(2,1)}, u32[]{:S(2)}) copy-start(bf16[152,1024]{1,0:T(8,128)(2,1)} %copy-done.14) | copy-start | bytes 933892
  109.2 5.5 %copy-start.8 = (bf16[1792,768]{1,0:T(8,128)(2,1)S(1)}, bf16[1792,768]{1,0:T(8,128)(2,1)}, u32[]{:S(2)}) copy-start(bf16[1792,768]{1,0:T(8,128)(2,1)} %all-gather.4.cloned.1.call-done) | copy-start | bytes 8257540
  112.6 16.6 %copy-start.11 = (bf16[2,256,152]{1,2,0:T(8,128)(2,1)S(1)}, bf16[2,256,152]{1,2,0:T(8,128)(2,1)}, u32[]{:S(2)}) copy-start(bf16[2,256,152]{1,2,0:T(8,128)(2,1)} %param.13) | copy-start | bytes 466948
  112.6 21.0 %collective-permute-start.4 = (bf16[152,768]{1,0:T(8,128)(2,1)}, bf16[152,768]{1,0:T(8,128)(2,1)}, u32[]{:S(2)}, u32[]{:S(2)}) collective-permute-start(bf16[152,768]{1,0:T(8,128)(2,1)} %convolution_convert_fusion.2), channel_id=1, source_target_pairs={{0,1},{1,0},{2,3},{3,2},{4,5},{5,4},{6,7},{7,6},{8,9},{9,8},{10,11... | collective-permute-start | bytes 700424 | tf_op jit(solution)/shard_map/ppermute | solution.py:150
  116.5 23.1 %collective-permute-start.5 = (bf16[152,1792]{1,0:T(8,128)(2,1)}, bf16[152,1792]{1,0:T(8,128)(2,1)S(1)}, u32[]{:S(2)}, u32[]{:S(2)}) collective-permute-start(bf16[152,1792]{1,0:T(8,128)(2,1)} %convolution_convert_fusion.1), channel_id=1, source_target_pairs={{0,1},{1,0},{2,3},{3,2},{4,5},{5,4},{6,7},{7,6},{8,9},{9,8},{10,11... | collective-permute-start | bytes 1634312 | tf_op jit(solution)/shard_map/ppermute | solution.py:150
  122.0 11.0 %collective-permute-start.6 = (bf16[56,152]{1,0:T(8,128)(2,1)S(1)}, bf16[56,152]{1,0:T(8,128)(2,1)S(1)}, u32[]{:S(2)}, u32[]{:S(2)}) collective-permute-start(bf16[56,152]{1,0:T(8,128)(2,1)S(1)} %shard_map.108), channel_id=1, source_target_pairs={{0,65},{1,64},{32,97},{33,96},{64,1},{65,0},{96,33},{97,32},{128,1... | collective-permute-start | bytes 51080 | tf_op jit(solution)/shard_map/ppermute | solution.py:213
  129.3 4.3 %copy-start.9 = (bf16[1792,768]{1,0:T(8,128)(2,1)S(1)}, bf16[1792,768]{1,0:T(8,128)(2,1)}, u32[]{:S(2)}) copy-start(bf16[1792,768]{1,0:T(8,128)(2,1)} %all-gather.4.cloned.1.call-done) | copy-start | bytes 8257540
  129.3 4.3 %copy-start.13 = (bf16[1,2,768,152]{2,3,1,0:T(8,128)(2,1)S(1)}, bf16[1,2,768,152]{2,3,1,0:T(8,128)(2,1)}, u32[]{:S(2)}) copy-start(bf16[1,2,768,152]{2,3,1,0:T(8,128)(2,1)} %param.11) | copy-start | bytes 1400836
Sparse Core Ops, SparseCore 0:
  51.3 50.5 all-gather.3
